TPU v7x, 128 devices: a whole 4x4x4 slice. The times are simulated.
128 devices in a mesh: grp: 8 (over x, core), row: 16 (over z, y).
Axes of the slice: x: 4, y: 4, z: 4, core: 2. Of those that a mesh axis runs over, the one named last changes fastest.
Arguments:
- lhs_emb: float32 [8, 4096, 400], P('grp', 'row'), may hold values from -3 to 3
- lhs_accum: float32 [8, 4096], P('grp', 'row'), may hold values from 0.5 to 20
- rhs_emb: float32 [8, 4096, 400], P('grp', 'row'), may hold values from -40 to 40
- rhs_accum: float32 [8, 4096], P('grp', 'row'), may hold values from 0.5 to 20
- rel_emb: float32 [1000, 400], replicated, may hold values from -3 to 3
- rel_accum: float32 [1000], replicated, may hold values from 5 to 500
- partner: int32 [8], P('grp'), may hold values from 0 to 7, as said below
- edge_lhs: int32 [8, 16, 2048], P('grp', 'row'), may hold values from 0 to 255
- edge_rhs: int32 [8, 16, 2048], P('grp', 'row'), may hold values from 0 to 4095, as said below
- edge_rel: int32 [8, 16, 2048], P('grp', 'row'), may hold values from 0 to 999
- edge_count: int32 [8, 16], P('grp', 'row'), may hold values from 1 to 2048, as said below
- neg_rhs: int32 [8, 16, 1024], P('grp', 'row'), may hold values from 0 to 4095, as said below
Outputs:
- new_lhs: float32 [8, 4096, 400], P('grp', 'row')
- new_lhs_accum: float32 [8, 4096], P('grp', 'row')
- new_rhs: float32 [8, 4096, 400], P('grp', 'row')
- new_rhs_accum: float32 [8, 4096], P('grp', 'row')
- new_rel: float32 [1000, 400], replicated
- new_rel_accum: float32 [1000], replicated
Inputs may be any that keep to these rules, and one draw needn't show every extreme that they name: partner is a permutation of the groups; in it some group g trains the partition of group (g + 4) mod 8. `edge_count`: one device of every group has all 2048 slots live. `edge_rhs`: among the 2048 slots of each device, exactly 128 name a row of each block of 256 rows (rows k * 256 to (k + 1) * 256 - 1). `neg_rhs`: among the 1024 negatives of each device, exactly 64 name a row of each block of 256 rows.
All inputs are finite; a program needn't handle non-finite values.
Results may differ from a plain program's by a relative error of at most 0.003.
Values may be sent and summed in bfloat16 or wider, within the bound.
No kernel may reach another device: no remote copies, remote signals or barrier semaphores. Data moves between devices by JAX's collectives and lax.ppermute only.
A program may use at most 64 MiB of HBM per device.

v0:
```python
import jax
import jax.numpy as jnp
from jax import lax
from jax.sharding import PartitionSpec as P

LEARN = 0.25
TINY = 1e-10


def complex_mul(left, right):
    half = left.shape[-1] // 2
    left_a, left_b = (left[..., :half], left[..., half:])
    right_a, right_b = (right[..., :half], right[..., half:])
    return jnp.concatenate(
        [left_a * right_a - left_b * right_b, left_a * right_b + left_b * right_a], -1
    )


def edge_terms(lhs_rows, rel_rows, pos_rows, neg_rows, live):
    query, pull = jax.vjp(complex_mul, lhs_rows, rel_rows)
    query_low = query.astype(jnp.bfloat16)
    pos_score = jnp.sum(query_low.astype(jnp.float32) * pos_rows.astype(jnp.float32), -1)
    neg_score = lax.dot_general(
        query_low, neg_rows, (((1,), (1,)), ((), ())), preferred_element_type=jnp.float32
    )
    highest = jnp.maximum(pos_score, jnp.max(neg_score, -1))
    pos_exp = jnp.exp(pos_score - highest)
    neg_exp = jnp.exp(neg_score - highest[:, None])
    total = pos_exp + jnp.sum(neg_exp, -1)
    pos_weight = live * (pos_exp / total - 1.0)
    neg_weight = (neg_exp * (live / total)[:, None]).astype(jnp.bfloat16)
    query_grad = pos_weight[:, None] * pos_rows.astype(jnp.float32) + jnp.dot(
        neg_weight, neg_rows, preferred_element_type=jnp.float32
    )
    lhs_grad, rel_grad = pull(query_grad)
    pos_grad = (pos_weight[:, None] * query_low.astype(jnp.float32)).astype(jnp.bfloat16)
    neg_grad = lax.dot_general(
        neg_weight, query_low, (((0,), (0,)), ((), ())), preferred_element_type=jnp.float32
    )
    return (lhs_grad, rel_grad, pos_grad, neg_grad)


def adagrad(table, accum, grad):
    new_accum = accum + jnp.mean(grad * grad, -1)
    return (table - LEARN * grad / (jnp.sqrt(new_accum)[..., None] + TINY), new_accum)


def onehot_sum(index, values, count):
    marks = (jnp.arange(count, dtype=jnp.int32)[:, None] == index[None, :]).astype(jnp.float32)
    return jnp.dot(
        marks, values, precision=lax.Precision.HIGHEST, preferred_element_type=jnp.float32
    )


def body(
    lhs_emb,
    lhs_accum,
    rhs_emb,
    rhs_accum,
    rel_emb,
    rel_accum,
    partner,
    edge_lhs,
    edge_rhs,
    edge_rel,
    edge_count,
    neg_rhs,
):
    target = partner[0]
    carried = (jnp.zeros_like(rhs_emb), jnp.zeros_like(rhs_accum))
    pieces = (
        lax.all_gather(rhs_emb, "grp", axis=0, tiled=True),
        lax.all_gather(rhs_accum, "grp", axis=0, tiled=True),
    )
    length = pieces[0].shape[0]
    offset = target
    inside = (offset >= 0) & (offset < length)
    place = jnp.clip(offset, 0, length - 1)
    emb_piece = lax.dynamic_index_in_dim(pieces[0], place, 0, True)
    accum_piece = lax.dynamic_index_in_dim(pieces[1], place, 0, True)
    held_emb = jnp.where(inside, emb_piece, carried[0])
    held_accum = jnp.where(inside, accum_piece, carried[1])
    rows_here = held_emb.shape[1]
    width_all = held_emb.shape[2]
    pos_index = edge_rhs[0, 0]
    neg_index = neg_rhs[0, 0]
    right_low = held_emb.astype(jnp.bfloat16)
    whole_table = lax.all_gather(right_low, "row", axis=1, tiled=True)[0]
    pos_rows = jnp.take(whole_table, pos_index, axis=0)
    neg_rows = jnp.take(whole_table, neg_index, axis=0)
    slots = edge_lhs.shape[2]
    negatives = neg_index.shape[0]
    block_rows = min(512, slots)
    live_count = edge_count[0, 0]
    blocks = (live_count + block_rows - 1) // block_rows
    lhs_table = lhs_emb[0]
    lhs_slots = edge_lhs[0, 0]
    rel_slots = edge_rel[0, 0]
    relations = rel_emb.shape[0]

    def advance(block, carried):
        lhs_sum, rel_sum, pos_grads, neg_sum = carried
        start = block * block_rows
        lhs_index = lax.dynamic_slice_in_dim(lhs_slots, start, block_rows)
        rel_index = lax.dynamic_slice_in_dim(rel_slots, start, block_rows)
        pos_block = lax.dynamic_slice_in_dim(pos_rows, start, block_rows, 0)
        live = (start + jnp.arange(block_rows, dtype=jnp.int32) < live_count).astype(jnp.float32)
        lhs_grad, rel_grad, pos_grad, neg_grad = edge_terms(
            jnp.take(lhs_table, lhs_index, axis=0),
            jnp.take(rel_emb, rel_index, axis=0),
            pos_block,
            neg_rows,
            live,
        )
        lhs_sum = lhs_sum + onehot_sum(lhs_index, lhs_grad, rows_here)
        rel_sum = rel_sum + onehot_sum(rel_index, rel_grad, relations)
        pos_grads = lax.dynamic_update_slice_in_dim(pos_grads, pos_grad, start, 0)
        return (lhs_sum, rel_sum, pos_grads, neg_sum + neg_grad)

    initial = (
        jnp.zeros((rows_here, width_all), jnp.float32),
        jnp.zeros(rel_emb.shape, jnp.float32),
        jnp.zeros((slots, width_all), jnp.bfloat16),
        jnp.zeros((negatives, width_all), jnp.float32),
    )
    lhs_sum, rel_sum, pos_grads, neg_sum = lax.fori_loop(0, blocks, advance, initial)
    neg_low = neg_sum.astype(jnp.bfloat16)
    every_index = jnp.concatenate([pos_index, neg_index])
    every_grad = jnp.concatenate([pos_grads, neg_low], 0)
    offset = every_index
    marks = (
        jnp.arange(rows_here * lax.axis_size("row"), dtype=jnp.int32)[:, None] == offset[None, :]
    ).astype(jnp.bfloat16)
    rhs_grad = lax.psum_scatter(
        jnp.dot(marks, every_grad, preferred_element_type=jnp.float32).astype(jnp.bfloat16),
        "row",
        scatter_dimension=0,
        tiled=True,
    ).astype(jnp.float32)
    rel_grad = lax.psum(rel_sum, ("grp", "row"))
    new_lhs, new_lhs_accum = adagrad(lhs_table, lhs_accum[0], lhs_sum)
    new_rhs, new_rhs_accum = adagrad(held_emb[0], held_accum[0], rhs_grad)
    new_rel, new_rel_accum = adagrad(rel_emb, rel_accum, rel_grad)
    return (
        new_lhs[None],
        new_lhs_accum[None],
        new_rhs[None],
        new_rhs_accum[None],
        new_rel,
        new_rel_accum,
    )


def solution(mesh):
    in_specs = (
        P("grp", "row", None),
        P("grp", "row"),
        P("grp", "row", None),
        P("grp", "row"),
        P(),
        P(),
        P("grp"),
        P("grp", "row", None),
        P("grp", "row", None),
        P("grp", "row", None),
        P("grp", "row"),
        P("grp", "row", None),
    )
    out_specs = (
        P("grp", "row", None),
        P("grp", "row"),
        P("grp", "row", None),
        P("grp", "row"),
        P(),
        P(),
    )
    return jax.shard_map(body, mesh=mesh, in_specs=in_specs, out_specs=out_specs, check_vma=False)
```

profile of v0, /device:TPU:1, one launch (start us, length us, event | category | flops | bytes accessed | tf_op | source)
XLA Modules:
  0.0 476.3 jit_solution(14952502996764694418)
XLA Ops:
  7.2 0.0 all-gather.4.cloned.1.call-start
  7.2 0.7 all-gather.4.cloned.1.call-update
  7.9 0.0 all-gather.6.cloned.1.call-start
  8.6 33.0 %all-gather.4.cloned.1.call-done = f32[8,256,400]{1,2,0:T(8,128)} async-done(((f32[1,256,400]{1,2,0:T(8,128)}), f32[8,256,400]{1,2,0:T(8,128)}) %all-gather.4.cloned.1.call-update) | async-done | bytes 3276816 | tf_op jit(solution)/shard_map/all_gather | solution.py:72
  41.6 1.8 fusion.27
  43.4 0.0 all-gather.6.cloned.1.call-update
  43.4 0.0 all-reduce.6.cloned.1.call-start
  44.1 2.1 copy.37
  46.2 0.2 copy.36
  46.6 49.8 %all-gather.6.cloned.1.call-done = bf16[1,4096,400]{1,2,0:T(8,128)(2,1)} async-done(((bf16[1,256,400]{1,2,0:T(8,128)(2,1)}), bf16[1,4096,400]{1,2,0:T(8,128)(2,1)}) %all-gather.6.cloned.1.call-update) | async-done | bytes 3276816 | tf_op jit(solution)/shard_map/all_gather | solution.py:88
  96.3 6.0 %copy.34 = bf16[4096,400]{1,0:T(8,128)(2,1)} copy(bf16[4096,400]{0,1:T(8,128)(2,1)} %bitcast.36) | data formatting | bytes 6553600 | tf_op jit(solution)/shard_map/squeeze | solution.py:88
  102.3 11.9 %gather_fusion.2 = bf16[2048,400]{1,0:T(8,128)(2,1)} fusion(bf16[4096,400]{1,0:T(8,128)(2,1)} %copy.34, s32[2048]{0:T(1024)S(1)} %broadcast_clamp_fusion), kind=kCustom, calls=%fused_computation.2 | custom fusion | bytes 3284992 | tf_op jit(solution)/shard_map/jit(_take)/gather | solution.py:89
  114.2 2.8 broadcast_select_fusion.2
  117.0 3.8 copy.38
  120.9 7.8 %gather_fusion.3 = bf16[1024,400]{1,0:T(8,128)(2,1)} fusion(bf16[4096,400]{1,0:T(8,128)(2,1)} %copy.34, s32[1024]{0:T(1024)S(1)} %broadcast_clamp_fusion.1), kind=kCustom, calls=%fused_computation.3 | custom fusion | bytes 1642496 | tf_op jit(solution)/shard_map/jit(_take)/gather | solution.py:90
  128.7 2.5 broadcast_select_fusion.3
  131.2 1.4 broadcast_in_dim.97
  132.6 1.4 broadcast_in_dim.98
  134.0 1.4 broadcast_in_dim.99
  135.3 0.8 broadcast_in_dim.96
  136.1 25.5 %while.18 = (s32[]{:T(128)}, f32[256,400]{0,1:T(8,128)}, f32[1000,400]{0,1:T(8,128)}, bf16[2048,400]{0,1:T(8,128)(2,1)}, f32[1024,400]{0,1:T(8,128)}, /*index=5*...) while((s32[]{:T(128)}, f32[256,400]{0,1:T(8,128)}, ...), condition=%wide.region_4.5_spmd, body=%wide.region_0.4_spmd.sunk | while | flops 4359209984 | bytes 64912776 | solution.py:126
  136.1 0.8 compare_and_fusion.5
  136.9 2.3 gather_fusion.1
  139.2 2.4 copy.42
  141.7 1.2 broadcast_select_fusion.9
  142.9 2.3 gather_fusion
  145.2 2.4 copy.41
  147.7 1.4 broadcast_select_fusion.8
  149.0 0.2 subtract_convert_fusion.2
  149.3 0.1 copy-done.7
  149.4 0.2 fusion.46
  149.5 0.1 copy-done
  149.6 0.8 fusion.45
  150.5 0.5 fusion.47
  151.0 0.7 convert_divide_fusion.2
  151.7 0.9 convolution_add_fusion.8
  152.6 1.2 copy-done.2
  153.7 0.9 fusion.49
  154.7 0.9 convolution_add_fusion.6
  155.5 0.3 multiply_add_fusion.7
  155.9 4.2 fusion.48
  160.1 0.7 convolution_add_fusion.7
  160.9 0.0 copy-start.5
  160.9 0.7 copy-done.5
  161.6 0.0 all-reduce.6.cloned.1.call-update
  161.6 0.2 reduce-scatter.2.cloned.1.call-start
  161.9 1.2 copy-done.3
  163.0 0.1 convert_element_type.56
  163.2 0.4 copy-done.10
  163.5 12.3 %fusion.19 = bf16[4096,400]{0,1:T(8,128)(2,1)} fusion(s32[3072]{0:T(1024)S(1)} %pad_add_fusion, bf16[1024,400]{0,1:T(8,128)(2,1)S(1)} %convert_element_type.56, bf16[2048,400]{0,1:T(8,128)(2,1)S(1)} %copy-done.10), kind=kOutput, calls=%fused_computation.53 | convolution fusion | flops 10085466112 | bytes 5746688 | tf_op jit(solution)/shard_map/dot_general | solution.py:135
  175.8 0.0 reduce-scatter.2.cloned.1.call-update
  175.9 0.6 copy-done.17
  176.5 88.3 %all-gather = f32[8,1,256]{2,1,0:T(1,128)S(1)} all-gather(f32[1,1,256]{2,1,0:T(1,128)S(1)} %bitcast.50), channel_id=1, replica_groups=mesh['grp'=8,'row'=16] {'grp'}, dimensions={0}, use_global_device_ids=true | all-gather | bytes 9216 | tf_op jit(solution)/shard_map/all_gather | solution.py:73
  264.8 0.1 multiply_reduce_fusion.1
  264.9 0.6 add.235
  265.5 0.8 subtract_bitcast_fusion
  266.3 121.6 %all-reduce.6.cloned.1.call-done = f32[1000,400]{0,1:T(8,128)} async-done(((f32[1000,400]{0,1:T(8,128)}), f32[1000,400]{0,1:T(8,128)}) %all-reduce.6.cloned.1.call-update) | async-done | bytes 1600016 | tf_op jit(solution)/shard_map/psum | solution.py:140
  387.9 1.7 multiply_reduce_fusion
  389.6 0.6 sqrt_add_fusion
  390.2 1.6 divide_subtract_fusion
  391.8 74.5 %reduce-scatter.2.cloned.1.call-done = bf16[256,400]{0,1:T(8,128)(2,1)} async-done(((bf16[4096,400]{0,1:T(8,128)(2,1)}), bf16[256,400]{0,1:T(8,128)(2,1)}) %reduce-scatter.2.cloned.1.call-update) | async-done | bytes 204816 | tf_op jit(solution)/shard_map/reduce_scatter | solution.py:134
  466.3 1.0 fusion.26
  467.3 0.6 bitcast_add_fusion
  467.9 1.9 fusion.25
  (43 shorter events, 0.2 us)
Async XLA Ops:
  7.2 34.4 %all-gather.4.cloned.1.call-start = ((), (), s32[]{:S(2)}) async-start(), calls=%async_computation.1 | async-start | bytes 3686400 | tf_op jit(solution)/shard_map/all_gather | solution.py:72
  7.9 88.4 %all-gather.6.cloned.1.call-start = ((), (), s32[]{:S(2)}) async-start(), calls=%async_computation.2 | async-start | bytes 3481600 | tf_op jit(solution)/shard_map/all_gather | solution.py:88
  41.6 4.6 copy-start.11
  43.4 344.5 %all-reduce.6.cloned.1.call-start = ((), (), s32[]{:S(2)}) async-start(), calls=%async_computation.4 | async-start | bytes 3276800 | tf_op jit(solution)/shard_map/psum | solution.py:140
  44.1 2.3 copy-start.13
  44.1 2.3 copy-start.14
  147.7 1.7 copy-start.7
  147.7 2.0 copy-start
  149.6 2.0 copy-start.1
  152.6 1.2 copy-start.2
  155.9 4.3 copy-start.4
  160.9 0.8 copy-start.5
  161.6 1.4 copy-start.3
  161.6 1.9 copy-start.10
  161.6 304.6 %reduce-scatter.2.cloned.1.call-start = ((), (), s32[]{:S(2)}) async-start(), calls=%async_computation.3 | async-start | bytes 3481600 | tf_op jit(solution)/shard_map/reduce_scatter | solution.py:134
  175.8 0.7 copy-start.17
  175.8 89.0 %copy-start.6 = (f32[256,400]{0,1:T(8,128)S(1)}, f32[256,400]{0,1:T(8,128)}, u32[]{:S(2)}) copy-start(f32[256,400]{0,1:T(8,128)} %get-tuple-element.173) | copy-start | bytes 1228804
  175.8 89.1 %copy-start.15 = (f32[1,256]{1,0:T(1,128)S(1)}, f32[1,256]{1,0:T(1,128)}, u32[]{:S(2)}) copy-start(f32[1,256]{1,0:T(1,128)} %param.15) | copy-start | bytes 3076
  175.8 89.7 %copy-start.12 = (f32[1,256,400]{1,2,0:T(8,128)S(1)}, f32[1,256,400]{1,2,0:T(8,128)}, u32[]{:S(2)}) copy-start(f32[1,256,400]{1,2,0:T(8,128)} %param.14) | copy-start | bytes 1228804
  175.8 213.8 %copy-start.16 = (f32[1000]{0:T(1024)S(1)}, f32[1000]{0:T(1024)}, u32[]{:S(2)}) copy-start(f32[1000]{0:T(1024)} %param.19) | copy-start | bytes 12004
  175.9 214.4 %copy-start.8 = (f32[1000,400]{0,1:T(8,128)S(1)}, f32[1000,400]{0,1:T(8,128)}, u32[]{:S(2)}) copy-start(f32[1000,400]{0,1:T(8,128)} %param.18) | copy-start | bytes 4800004
  387.9 2.3 copy-start.9
Sparse Core Ops, SparseCore 0:
  9.7 31.8 all-gather.3
  44.3 51.9 all-gather.5
  161.8 226.1 all-reduce.5
  391.2 74.9 reduce-scatter.1
where the time goes:
time: 478 us; the launch traced here: 476 us
  waiting for transfers between devices  280 us (59%)
  blocking collectives  88.3 us (18%)
  local copies, waits for them, and re-layouts  50.6 us (11%)
  other arithmetic  22.2 us (5%)
  matrix products  19.8 us (4%)
  between operations  15.3 us (3%)
    psum x1, waiting for transfers between devices, body(): rel_grad = lax.psum(rel_sum, ('grp', 'row'))  122 us
    all_gather x1, blocking collectives, body(): lax.all_gather(rhs_accum, 'grp', axis=0, tiled=True)  88.3 us
    reduce_scatter x1, waiting for transfers between devices, body(): lax.psum_scatter(jnp.dot(marks, every_grad, preferred_element_type=jnp.fl...  74.5 us
    all_gather x1, waiting for transfers between devices, body(): whole_table = lax.all_gather(right_low, 'row', axis=1, tiled=True)[0]  49.8 us
    all_gather x1, waiting for transfers between devices, body(): lax.all_gather(rhs_emb, 'grp', axis=0, tiled=True)  33 us
    dot_general x1, matrix products, body(): jnp.dot(marks, every_grad, preferred_element_type=jnp.float32)  12.3 us
    gather x1, local copies, waits for them, and re-layouts, body(): pos_rows = jnp.take(whole_table, pos_index, axis=0)  11.9 us
  transfers between devices with their start and end apart: 4, of which 4 were waited for; matrix products, arithmetic and copies ran while one was open for 4% of the time, Pallas kernels for 0%

commit v1 on v0

v1 whole, which is shorter than its diff:
```python
import functools

import jax
import jax.numpy as jnp
from jax import lax
from jax.experimental import pallas as pl
from jax.experimental.pallas import tpu as pltpu
from jax.sharding import PartitionSpec as P

LEARN = 0.25
TINY = 1e-10
BF = jnp.bfloat16
F32 = jnp.float32
D = 400
HALF = 200
REL = 1000
RELP = 1024
LOCAL = 256
EDGES = 2048
NEG = 1024
OWNERS = 16
PER = 128
FOLD = 208
SEND = D + FOLD
CHUNK = 256
STEPS = EDGES // CHUNK
VMEM = 50 * 1024 * 1024


def onehot(index, count):
    rows = lax.broadcasted_iota(jnp.int32, (count, index.shape[1]), 0)
    return jnp.where(rows == index, 1.0, 0.0).astype(BF)


def dot(a, b):
    return jnp.dot(a, b, preferred_element_type=F32)


def dot_t(a, b):
    return lax.dot_general(a, b, (((1,), (1,)), ((), ())), preferred_element_type=F32)


def split(value):
    high = value.astype(BF)
    return high, (value - high.astype(F32)).astype(BF)


def lhs_of(packed):
    return jnp.bitwise_and(jnp.right_shift(packed, 1), LOCAL - 1)


def rel_of(packed):
    return jnp.bitwise_and(jnp.right_shift(packed, 9), RELP - 1)


def query_kernel(packed_ref, lhs_ref, rel_ref, l_ref, w_ref, q_ref, lhs_two, rel_two):
    @pl.when(pl.program_id(0) == 0)
    def _():
        high, low = split(lhs_ref[...])
        lhs_two[0:D, :] = high
        lhs_two[D : 2 * D, :] = low
        rel_two[...] = jnp.zeros_like(rel_two)
        high, low = split(rel_ref[...])
        rel_two[0:D, 0:REL] = high
        rel_two[D : 2 * D, 0:REL] = low

    packed = packed_ref[...]
    both = dot(lhs_two[...], onehot(lhs_of(packed), LOCAL))
    left = both[0:D] + both[D : 2 * D]
    both = dot(rel_two[...], onehot(rel_of(packed), RELP))
    weight = both[0:D] + both[D : 2 * D]
    l_ref[...] = left
    w_ref[...] = weight
    la, lb, wa, wb = left[:HALF], left[HALF:], weight[:HALF], weight[HALF:]
    q_ref[...] = jnp.concatenate([la * wa - lb * wb, la * wb + lb * wa], 0).astype(BF)


def make_query(packed, lhs_t, rel_t):
    wide = pl.BlockSpec((D, CHUNK), lambda i: (0, i))
    return pl.pallas_call(
        query_kernel,
        grid=(STEPS,),
        in_specs=[
            pl.BlockSpec((1, CHUNK), lambda i: (0, i)),
            pl.BlockSpec((D, LOCAL), lambda i: (0, 0)),
            pl.BlockSpec((D, REL), lambda i: (0, 0)),
        ],
        out_specs=[wide, wide, wide],
        out_shape=[
            jax.ShapeDtypeStruct((D, EDGES), F32),
            jax.ShapeDtypeStruct((D, EDGES), F32),
            jax.ShapeDtypeStruct((D, EDGES), BF),
        ],
        scratch_shapes=[pltpu.VMEM((2 * D, LOCAL), BF), pltpu.VMEM((2 * D, RELP), BF)],
        compiler_params=pltpu.CompilerParams(vmem_limit_bytes=VMEM),
        cost_estimate=pl.CostEstimate(flops=5_000_000_000, bytes_accessed=10_000_000, transcendentals=0),
        name="make_query",
    )(packed, lhs_t, rel_t)


def fold_marks(index):
    marks = onehot(index, LOCAL)
    first = lax.broadcasted_iota(jnp.int32, marks.shape, 1) < 64
    none = jnp.zeros_like(marks)
    return jnp.where(first, marks, none), jnp.where(first, none, marks)


def serve_kernel(partner_ref, table_ref, asked_ref, rhs_ref, accum_ref, out_ref, ext_ref, two):
    del partner_ref
    table = table_ref[0]
    two[:, 0:LOCAL] = table[0:FOLD]
    two[0 : D - FOLD, LOCAL : 2 * LOCAL] = table[FOLD:D]
    two[D - FOLD : FOLD, LOCAL : 2 * LOCAL] = jnp.zeros((2 * FOLD - D, LOCAL), BF)
    for s in range(0, OWNERS, 2):
        pos = jnp.concatenate([asked_ref[s, 0:1, :], asked_ref[s + 1, 0:1, :]], 1)
        rows = dot(table, onehot(pos, LOCAL)).astype(BF)
        out_ref[s, 0:D, :] = rows[:, 0:PER]
        out_ref[s + 1, 0:D, :] = rows[:, PER:]
        marks = [jnp.concatenate(fold_marks(asked_ref[t, 1:2, :]), 0) for t in (s, s + 1)]
        rows = dot(two[...], jnp.concatenate(marks, 1)).astype(BF)
        out_ref[s, D:SEND, :] = rows[:, 0:PER]
        out_ref[s + 1, D:SEND, :] = rows[:, PER:]
    ext_ref[0:D, :] = rhs_ref[...]
    ext_ref[D : D + 8, :] = jnp.broadcast_to(accum_ref[...], (8, LOCAL))


def serve(partner, tables, asked, rhs_t, accum):
    whole = lambda shape: pl.BlockSpec(shape, lambda i, p: (0,) * len(shape))
    return pl.pallas_call(
        serve_kernel,
        grid_spec=pltpu.PrefetchScalarGridSpec(
            num_scalar_prefetch=1,
            grid=(1,),
            in_specs=[
                pl.BlockSpec((1, D, LOCAL), lambda i, p: (p[0], 0, 0)),
                whole((OWNERS, 8, PER)),
                whole((D, LOCAL)),
                whole((1, LOCAL)),
            ],
            out_specs=[whole((OWNERS, SEND, PER)), whole((D + 8, LOCAL))],
            scratch_shapes=[pltpu.VMEM((FOLD, 2 * LOCAL), BF)],
        ),
        out_shape=[
            jax.ShapeDtypeStruct((OWNERS, SEND, PER), BF),
            jax.ShapeDtypeStruct((D + 8, LOCAL), F32),
        ],
        compiler_params=pltpu.CompilerParams(vmem_limit_bytes=VMEM),
        cost_estimate=pl.CostEstimate(flops=2_000_000_000, bytes_accessed=5_000_000, transcendentals=0),
        name="serve_rows",
    )(partner, tables, asked, rhs_t, accum)


def edge_kernel(packed_ref, got_ref, q_ref, l_ref, w_ref, back_ref, rel_ref, lhs_ref, neg_t, neg_n, weights, lhs_g, lhs_lo, rel_g, q_all, m_lhs, m_rel):
    step = pl.program_id(0)

    @pl.when(step == 0)
    def _():
        for k in range(0, OWNERS, 2):
            a, b = got_ref[k, D:SEND, :].astype(F32), got_ref[k + 1, D:SEND, :].astype(F32)
            first = lax.broadcasted_iota(jnp.int32, a.shape, 1) < 64
            top = jnp.where(first, a, pltpu.roll(b, 64, 1))
            low = jnp.where(first, pltpu.roll(a, 64, 1), b)
            both = jnp.concatenate([top, low[0 : D - FOLD]], 0)
            lanes = slice(k * 64, k * 64 + PER)
            neg_t[:, lanes] = both.astype(BF)
            neg_n[lanes, :] = both.T.astype(BF)

    lanes = pl.ds(pl.multiple_of(step * CHUNK, CHUNK), CHUNK)
    packed = packed_ref[...]
    live = jnp.bitwise_and(packed, 1).astype(F32)
    query = q_ref[...]
    query_wide = query.astype(F32)
    pos = jnp.concatenate([got_ref[2 * step, 0:D, :], got_ref[2 * step + 1, 0:D, :]], 1).astype(F32)
    scores = dot(neg_n[...], query)
    pos_score = jnp.sum(query_wide * pos, 0, keepdims=True)
    highest = jnp.maximum(pos_score, jnp.max(scores, 0, keepdims=True))
    neg_exp = jnp.exp(scores - highest)
    pos_exp = jnp.exp(pos_score - highest)
    total = pos_exp + jnp.sum(neg_exp, 0, keepdims=True)
    pos_weight = live * (pos_exp / total - 1.0)
    weight = (neg_exp * (live / total)).astype(BF)
    weights[:, lanes] = weight
    grad = pos_weight * pos + dot(neg_t[...], weight)
    pos_grad = (pos_weight * query_wide).astype(BF)
    back_ref[2 * step, 0:D, :] = pos_grad[:, 0:PER]
    back_ref[2 * step + 1, 0:D, :] = pos_grad[:, PER:]
    ga, gb = grad[:HALF], grad[HALF:]
    left, rel = l_ref[...], w_ref[...]
    la, lb, wa, wb = left[:HALF], left[HALF:], rel[:HALF], rel[HALF:]
    high, low = split(jnp.concatenate([ga * wa + gb * wb, gb * wa - ga * wb], 0))
    lhs_g[:, lanes] = high
    lhs_lo[:, lanes] = low
    rel_g[:, lanes] = jnp.concatenate([ga * la + gb * lb, gb * la - ga * lb], 0).astype(BF)
    q_all[:, lanes] = query
    m_lhs[:, lanes] = onehot(lhs_of(packed), LOCAL)
    m_rel[:, lanes] = onehot(rel_of(packed), RELP)

    @pl.when(step == STEPS - 1)
    def _():
        for t in range(0, RELP // PER, 2):
            part = dot_t(rel_g[...], m_rel[t * PER : (t + 2) * PER, :]).astype(BF)
            rel_ref[t, 0:D, :] = part[:, 0:PER]
            rel_ref[t + 1, 0:D, :] = part[:, PER:]
            rel_ref[t, D:512, :] = jnp.zeros((112, PER), BF)
            rel_ref[t + 1, D:512, :] = jnp.zeros((112, PER), BF)
        for k in range(0, OWNERS, 4):
            part = dot_t(q_all[...], weights[k * 64 : (k + 4) * 64, :])
            for h in (0, 2):
                both = part[:, h * 64 : (h + 2) * 64]
                top = both[0:FOLD]
                low = jnp.concatenate([both[FOLD:D], jnp.zeros((2 * FOLD - D, PER), F32)], 0)
                first = lax.broadcasted_iota(jnp.int32, top.shape, 1) < 64
                back_ref[k + h, D:SEND, :] = jnp.where(first, top, pltpu.roll(low, 64, 1)).astype(BF)
                back_ref[k + h + 1, D:SEND, :] = jnp.where(first, pltpu.roll(top, 64, 1), low).astype(BF)
        lhs_ref[...] = dot_t(lhs_g[...], m_lhs[...]) + dot_t(lhs_lo[...], m_lhs[...])


def edges(packed, got, query, left, weight):
    wide = pl.BlockSpec((D, CHUNK), lambda i: (0, i))
    whole = lambda shape: pl.BlockSpec(shape, lambda i: (0,) * len(shape))
    return pl.pallas_call(
        edge_kernel,
        grid=(STEPS,),
        in_specs=[
            pl.BlockSpec((1, CHUNK), lambda i: (0, i)),
            whole((OWNERS, SEND, PER)),
            wide,
            wide,
            wide,
        ],
        out_specs=[whole((OWNERS, SEND, PER)), whole((RELP // PER, 512, PER)), whole((D, LOCAL))],
        out_shape=[
            jax.ShapeDtypeStruct((OWNERS, SEND, PER), BF),
            jax.ShapeDtypeStruct((RELP // PER, 512, PER), BF),
            jax.ShapeDtypeStruct((D, LOCAL), F32),
        ],
        scratch_shapes=[
            pltpu.VMEM((D, NEG), BF),
            pltpu.VMEM((NEG, D), BF),
            pltpu.VMEM((NEG, EDGES), BF),
            pltpu.VMEM((D, EDGES), BF),
            pltpu.VMEM((D, EDGES), BF),
            pltpu.VMEM((D, EDGES), BF),
            pltpu.VMEM((D, EDGES), BF),
            pltpu.VMEM((LOCAL, EDGES), BF),
            pltpu.VMEM((RELP, EDGES), BF),
        ],
        compiler_params=pltpu.CompilerParams(vmem_limit_bytes=VMEM),
        cost_estimate=pl.CostEstimate(flops=10_000_000_000, bytes_accessed=20_000_000, transcendentals=2_100_000),
        name="edges",
    )(packed, got, query, left, weight)


def adagrad(table, accum, grad):
    new_accum = accum + jnp.mean(grad * grad, 0, keepdims=True)
    return table - LEARN * grad / (jnp.sqrt(new_accum) + TINY), new_accum


def right_kernel(partner_ref, ext_ref, asked_ref, back_ref, new_ref, accum_ref, pos, neg, m_pos, m_one, m_two):
    del partner_ref
    for s in range(OWNERS):
        lanes = slice(s * PER, (s + 1) * PER)
        pos[:, lanes] = back_ref[s, 0:D, :]
        neg[:, lanes] = back_ref[s, D:SEND, :]
        m_pos[:, lanes] = onehot(asked_ref[s, 0:1, :], LOCAL)
        one, two = fold_marks(asked_ref[s, 1:2, :])
        m_one[:, lanes] = one
        m_two[:, lanes] = two
    low = dot_t(neg[...], m_two[...])[0 : D - FOLD]
    grad = dot_t(pos[...], m_pos[...]) + jnp.concatenate([dot_t(neg[...], m_one[...]), low], 0)
    new_ref[...], accum_ref[...] = adagrad(ext_ref[0, 0:D, :], ext_ref[0, D : D + 1, :], grad)


def right_update(partner, ext_all, asked, back):
    whole = lambda shape: pl.BlockSpec(shape, lambda i, p: (0,) * len(shape))
    marks = pltpu.VMEM((LOCAL, OWNERS * PER), BF)
    return pl.pallas_call(
        right_kernel,
        grid_spec=pltpu.PrefetchScalarGridSpec(
            num_scalar_prefetch=1,
            grid=(1,),
            in_specs=[
                pl.BlockSpec((1, D + 8, LOCAL), lambda i, p: (p[0], 0, 0)),
                whole((OWNERS, 8, PER)),
                whole((OWNERS, SEND, PER)),
            ],
            out_specs=[whole((D, LOCAL)), whole((1, LOCAL))],
            scratch_shapes=[
                pltpu.VMEM((D, OWNERS * PER), BF),
                pltpu.VMEM((FOLD, OWNERS * PER), BF),
                marks,
                marks,
                marks,
            ],
        ),
        out_shape=[jax.ShapeDtypeStruct((D, LOCAL), F32), jax.ShapeDtypeStruct((1, LOCAL), F32)],
        compiler_params=pltpu.CompilerParams(vmem_limit_bytes=VMEM),
        cost_estimate=pl.CostEstimate(flops=2_000_000_000, bytes_accessed=5_000_000, transcendentals=0),
        name="right_update",
    )(partner, ext_all, asked, back)


def left_kernel(table_ref, accum_ref, grad_ref, new_ref, new_accum_ref):
    new_ref[...], new_accum_ref[...] = adagrad(table_ref[...], accum_ref[...], grad_ref[...])


def left_update(table, accum, grad):
    return pl.pallas_call(
        left_kernel,
        out_shape=[jax.ShapeDtypeStruct((D, LOCAL), F32), jax.ShapeDtypeStruct((1, LOCAL), F32)],
        name="left_update",
    )(table, accum, grad)


def relation_kernel(table_ref, accum_ref, grad_ref, new_ref, new_accum_ref):
    grad = grad_ref[0, 0:D, :].astype(F32)
    new_ref[...], new_accum_ref[...] = adagrad(table_ref[...], accum_ref[...], grad)


def relation_update(table, accum, grad):
    tall = pl.BlockSpec((D, PER), lambda i: (0, i))
    flat = pl.BlockSpec((1, PER), lambda i: (0, i))
    return pl.pallas_call(
        relation_kernel,
        grid=(RELP // PER,),
        in_specs=[tall, flat, pl.BlockSpec((1, 512, PER), lambda i: (i, 0, 0))],
        out_specs=[tall, flat],
        out_shape=[jax.ShapeDtypeStruct((D, REL), F32), jax.ShapeDtypeStruct((1, REL), F32)],
        name="relation_update",
    )(table, accum, grad)


def body(
    lhs_emb,
    lhs_accum,
    rhs_emb,
    rhs_accum,
    rel_emb,
    rel_accum,
    partner,
    edge_lhs,
    edge_rhs,
    edge_rel,
    edge_count,
    neg_rhs,
):
    lhs_t, rhs_t, rel_t = lhs_emb[0].T, rhs_emb[0].T, rel_emb.T
    tables = lax.all_gather(rhs_t.astype(BF), "grp", axis=0, tiled=False)

    live = (jnp.arange(EDGES, dtype=jnp.int32) < edge_count[0, 0]).astype(jnp.int32)
    packed = lax.sort(
        (edge_rhs[0, 0] << 19) | (edge_rel[0, 0] << 9) | (edge_lhs[0, 0] << 1) | live, is_stable=False
    )
    neg_index = lax.sort(neg_rhs[0, 0], is_stable=False)
    pos_ask = ((packed >> 19) & (LOCAL - 1)).reshape(OWNERS, 1, PER)
    neg_ask = (neg_index & (LOCAL - 1)).reshape(OWNERS, 1, 64)
    ask = jnp.concatenate(
        [pos_ask, jnp.concatenate([neg_ask, neg_ask], 2), jnp.zeros((OWNERS, 6, PER), jnp.int32)], 1
    )
    asked = lax.all_to_all(ask, "row", 0, 0, tiled=True)
    packed = packed.reshape(1, EDGES)
    left, weight, query = make_query(packed, lhs_t, rel_t)

    rows, ext = serve(partner, tables, asked, rhs_t, rhs_accum)
    ext_all = lax.all_gather(ext, "grp", axis=0, tiled=False)
    got = lax.all_to_all(rows, "row", 0, 0, tiled=True)
    back, rel_sum, lhs_sum = edges(packed, got, query, left, weight)

    parts = lax.all_to_all(rel_sum.reshape(128, 32, PER), ("grp", "row"), 0, 0, tiled=True)
    returned = lax.all_to_all(back, "row", 0, 0, tiled=True)
    shard = jnp.sum(parts.astype(F32), 0).astype(BF)
    rel_grad = lax.all_to_all(jnp.broadcast_to(shard[None], (128, 32, PER)), ("grp", "row"), 0, 0, tiled=True)

    new_lhs, new_lhs_accum = left_update(lhs_t, lhs_accum, lhs_sum)
    new_rhs, new_rhs_accum = right_update(partner, ext_all, asked, returned)
    new_rel, new_rel_accum = relation_update(rel_t, rel_accum[None], rel_grad.reshape(RELP // PER, 512, PER))
    return (
        new_lhs.T[None],
        new_lhs_accum,
        new_rhs.T[None],
        new_rhs_accum,
        new_rel.T,
        new_rel_accum[0],
    )


def solution(mesh):
    rows = P("grp", "row", None)
    in_specs = (
        rows,
        P("grp", "row"),
        rows,
        P("grp", "row"),
        P(),
        P(),
        P("grp"),
        rows,
        rows,
        rows,
        P("grp", "row"),
        rows,
    )
    out_specs = (rows, P("grp", "row"), rows, P("grp", "row"), P(), P())
    return jax.shard_map(body, mesh=mesh, in_specs=in_specs, out_specs=out_specs, check_vma=False)
```

time: 478 us -> 216 us (0.45)
  waiting for transfers between devices: 280 us -> 66.2 us
  Pallas kernels: 0 us -> 45.5 us
  local copies, waits for them, and re-layouts: 50.6 us -> 6.83 us
  blocking collectives: 88.3 us -> 48.4 us
  matrix products: 19.8 us -> 0 us
  starting transfers between devices: 0.34 us -> 19.3 us
  other arithmetic: 22.2 us -> 11.9 us
    psum x1 -> x0, waiting for transfers between devices: 122 us -> none  [body(): rel_grad = lax.psum(rel_sum, ('grp', 'row'))]
    all_gather x1 -> x0, blocking collectives: 88.3 us -> none  [body(): lax.all_gather(rhs_accum, 'grp', axis=0, tiled=True)]
    all_gather x2, waiting for transfers between devices: 82.8 us -> 3.4 us  [the longest x1 3.4 us: body(): tables = lax.all_gather(rhs_t.astype(BF), 'grp', axis=0, tiled=False)]
    reduce_scatter x1 -> x0, waiting for transfers between devices: 74.5 us -> none  [body(): lax.psum_scatter(jnp.dot(marks, every_grad, preferred_element_type=jnp.fl...]
    all_to_all x0 -> x3, waiting for transfers between devices: none -> 62.1 us  [the longest x1 29.1 us: body(): got = lax.all_to_all(rows, 'row', 0, 0, tiled=True)]
    all_to_all x0 -> x2, blocking collectives: none -> 48.4 us  [the longest x1 24.7 us: body(): lax.all_to_all(rel_sum.reshape(128, 32, PER), ('grp', 'row'), 0, 0, tiled...]
    pallas_call x0 -> x6, Pallas kernels: none -> 45.5 us  [the longest x1 24.1 us: edges(): pl.pallas_call(edge_kernel, grid=(STEPS,), in_specs=[pl.BlockSpec((1, CHU...]
    gather x6 -> x0, local copies, waits for them, and re-layouts: 29.3 us -> none  [the longest x1 11.9 us: body(): pos_rows = jnp.take(whole_table, pos_index, axis=0)]
  transfers between devices with their start and end apart: 4 -> 5, of which waited for: 4 -> 4; matrix products, arithmetic and copies ran while one was open for 4% -> 5% of each run, Pallas kernels for 0% -> 19%
where the time goes in v1:
time: 216 us; the launch traced here: 214 us
  waiting for transfers between devices  66.2 us (31%)
  blocking collectives  48.4 us (22%)
  Pallas kernels  45.5 us (21%)
  starting transfers between devices  19.3 us (9%)
  between operations  15.4 us (7%)
  other arithmetic  11.9 us (6%)
  local copies, waits for them, and re-layouts  6.83 us (3%)
    all_to_all x1, waiting for transfers between devices, body(): got = lax.all_to_all(rows, 'row', 0, 0, tiled=True)  29.1 us
    all_to_all x1, waiting for transfers between devices, body(): returned = lax.all_to_all(back, 'row', 0, 0, tiled=True)  27.1 us
    all_to_all x1, blocking collectives, body(): lax.all_to_all(rel_sum.reshape(128, 32, PER), ('grp', 'row'), 0, 0, tiled...  24.7 us
    pallas_call x1, Pallas kernels, edges(): pl.pallas_call(edge_kernel, grid=(STEPS,), in_specs=[pl.BlockSpec((1, CHU...  24.1 us
    all_to_all x1, blocking collectives, body(): lax.all_to_all(jnp.broadcast_to(shard[None], (128, 32, PER)), ('grp', 'ro...  23.7 us
    all_to_all x1, starting transfers between devices, body(): asked = lax.all_to_all(ask, 'row', 0, 0, tiled=True)  8.6 us
    pallas_call x1, Pallas kernels, make_query(): pl.pallas_call(query_kernel, grid=(STEPS,), in_specs=[pl.BlockSpec((1, CH...  7.22 us
    all_to_all x1, starting transfers between devices, body(): got = lax.all_to_all(rows, 'row', 0, 0, tiled=True)  6.87 us
  transfers between devices with their start and end apart: 5, of which 4 were waited for; matrix products, arithmetic and copies ran while one was open for 5% of the time, Pallas kernels for 19%

profile of v1, /device:TPU:1, one launch (start us, length us, event | category | flops | bytes accessed | tf_op | source)
XLA Modules:
  0.0 213.6 jit_solution(949964020629718206)
XLA Ops:
  7.2 0.0 all-gather.5.cloned.1.call-start
  7.2 1.7 bitcast_convert_fusion
  8.9 0.0 all-gather.5.cloned.1.call-update
  9.6 0.8 shift-left_or_fusion
  10.4 4.3 %sort.14 = s32[2048]{0:T(1024)S(1)} sort(s32[2048]{0:T(1024)S(1)} %convert_or_fusion), dimensions={0}, to_apply=%region_0.0 | sort | flops 22528 | bytes 16384 | tf_op jit(solution)/shard_map/sort | solution.py:351
  14.6 4.3 %sort.15 = s32[1024]{0:T(1024)S(1)} sort(s32[1024]{0:T(1024)} %bitcast.40), dimensions={0}, to_apply=%region_1.0 | sort | flops 10240 | bytes 8192 | tf_op jit(solution)/shard_map/sort | solution.py:354
  18.9 0.1 reshape.38
  19.0 0.1 pad.3.clone
  19.1 0.7 add_add_fusion
  19.8 8.6 %all-to-all-start = ((s32[16,8,128]{2,1,0:T(8,128)}), s32[16,8,128]{2,1,0:T(8,128)S(1)}, u32[]{:S(2)}, u32[]{:S(2)}) async-start(s32[16,8,128]{2,1,0:T(8,128)} %add_add_fusion), calls=%async_computation | async-start | bytes 131072 | tf_op jit(solution)/shard_map/all_to_all | solution.py:360
  29.1 5.9 %all-to-all-done.asked_ref = s32[16,8,128]{2,1,0:T(8,128)S(1)} async-done(((s32[16,8,128]{2,1,0:T(8,128)}), s32[16,8,128]{2,1,0:T(8,128)S(1)}, u32[]{:S(2)}, u32[]{:S(2)}) %all-to-all-start) | async-done | bytes 65568 | tf_op jit(solution)/shard_map/all_to_all | solution.py:360
  35.0 3.4 %all-gather.5.cloned.1.call-done = bf16[3200,256]{1,0:T(8,128)(2,1)} async-done(((bf16[400,256]{1,0:T(8,128)(2,1)}), bf16[3200,256]{1,0:T(8,128)(2,1)}) %all-gather.5.cloned.1.call-update) | async-done | bytes 1638416 | tf_op jit(solution)/shard_map/all_gather | solution.py:348
  38.4 0.0 copy-start.1
  38.4 1.0 copy-done.1
  39.4 0.0 copy-start.4
  39.4 1.4 copy-done.4
  40.8 0.0 copy-start.5
  40.8 0.7 copy-done.5
  41.5 2.6 %serve_rows.1 = (bf16[16,608,128]{2,1,0:T(8,128)(2,1)}, f32[408,256]{1,0:T(8,128)}) custom-call(s32[1]{0:T(128)S(6)} %copy.18.partner_ref, bf16[8,400,256]{2,1,0:T(8,128)(2,1)S(1)} %bitcast.35, s32[16,8,128]{2,1,0:T(8,128)S(1)} %all-to-all-done.asked_ref, f32[400,256]{1,0:T(8,128)S(1)} %bitcast.30, f32[1,256]{1,0:T(1,128)S(1)} %copy-done.5), custom_call_target="tpu_custom_call" | custom-call | flops 2000000000 | bytes 5000000 | tf_op jit(solution)/shard_map/serve_rows/pallas_call | solution.py:129
  44.1 0.0 copy-start
  44.1 0.0 copy-start.2
  44.1 6.9 %all-to-all-start.1 = ((bf16[16,608,128]{2,1,0:T(8,128)(2,1)}), bf16[16,608,128]{2,1,0:T(8,128)(2,1)}, u32[]{:S(2)}, u32[]{:S(2)}) async-start(bf16[16,608,128]{2,1,0:T(8,128)(2,1)} %get-tuple-element.20), calls=%async_computation.1 | async-start | bytes 4980736 | tf_op jit(solution)/shard_map/all_to_all | solution.py:366
  50.9 0.0 all-gather.7.cloned.1.call-start
  51.0 0.7 all-gather.7.cloned.1.call-update
  51.7 0.0 copy-done
  51.7 0.0 copy-done.2
  51.7 7.2 %make_query.1 = (f32[400,2048]{1,0:T(8,128)}, f32[400,2048]{1,0:T(8,128)}, bf16[400,2048]{1,0:T(8,128)(2,1)S(1)}) custom-call(s32[1,2048]{1,0:T(1,128)S(1)} %bitcast.33, f32[400,256]{1,0:T(8,128)S(1)} %bitcast.32, f32[400,1000]{1,0:T(8,128)S(1)} %bitcast.28), custom_call_target="tpu_custom_call" | custom-call | flops 5000000000 | bytes 10000000 | tf_op jit(solution)/shard_map/make_query/pallas_call | solution.py:80
  58.9 0.0 copy-start.6
  58.9 1.2 copy-done.6
  60.1 29.1 %all-to-all-done.1.got_ref = bf16[16,608,128]{2,1,0:T(8,128)(2,1)} async-done(((bf16[16,608,128]{2,1,0:T(8,128)(2,1)}), bf16[16,608,128]{2,1,0:T(8,128)(2,1)}, u32[]{:S(2)}, u32[]{:S(2)}) %all-to-all-start.1) | async-done | bytes 2490400 | tf_op jit(solution)/shard_map/all_to_all | solution.py:366
  89.2 0.0 copy-start.7
  89.2 1.4 copy-done.7
  90.7 24.1 %edges.1 = (bf16[16,608,128]{2,1,0:T(8,128)(2,1)}, bf16[8,512,128]{2,1,0:T(8,128)(2,1)S(1)}, f32[400,256]{1,0:T(8,128)S(1)}) custom-call(s32[1,2048]{1,0:T(1,128)S(1)} %bitcast.34, bf16[16,608,128]{2,1,0:T(8,128)(2,1)} %all-to-all-done.1.got_ref, bf16[400,2048]{1,0:T(8,128)(2,1)S(1)} %copy-done.7, f32[400,2048]{1,0:T(8,128)} %get-tuple-element.22.l_ref, ...), custom_call_target="tpu_custom_call" | custom-call | flops 10000000000 | bytes 20000000 | tf_op jit(solution)/shard_map/edges/pallas_call | solution.py:221
  114.8 0.0 copy-start.3
  114.8 0.7 copy-done.3
  115.5 24.7 %all_to_all.25 = bf16[128,32,128]{2,1,0:T(8,128)(2,1)S(1)} all-to-all(bf16[128,32,128]{2,1,0:T(8,128)(2,1)S(1)} %bitcast.29), channel_id=1, replica_groups=mesh['grp'=8,'row'=16] {'grp','row'}, dimensions={0} | all-to-all | bytes 2097152 | tf_op jit(solution)/shard_map/all_to_all | solution.py:369
  140.2 0.2 reduce_sum.12
  140.4 0.1 broadcast_in_dim.22
  140.6 23.7 %all_to_all.26 = bf16[128,32,128]{2,1,0:T(8,128)(2,1)} all-to-all(bf16[128,32,128]{2,1,0:T(8,128)(2,1)S(1)} %broadcast_in_dim.22), channel_id=1, replica_groups=mesh['grp'=8,'row'=16] {'grp','row'}, dimensions={0} | all-to-all | bytes 2097152 | tf_op jit(solution)/shard_map/all_to_all | solution.py:372
  164.3 3.7 %all-to-all-start.2 = ((bf16[16,608,128]{2,1,0:T(8,128)(2,1)}), bf16[16,608,128]{2,1,0:T(8,128)(2,1)S(1)}, u32[]{:S(2)}, u32[]{:S(2)}) async-start(bf16[16,608,128]{2,1,0:T(8,128)(2,1)} %get-tuple-element.28), calls=%async_computation.2 | async-start | bytes 4980736 | tf_op jit(solution)/shard_map/all_to_all | solution.py:370
  168.0 2.0 left_update.1
  170.0 6.2 %relation_update.1 = (f32[400,1000]{1,0:T(8,128)}, f32[1,1000]{1,0:T(1,128)}) custom-call(f32[400,1000]{1,0:T(8,128)} %bitcast.27, f32[1,1000]{1,0:T(1,128)} %bitcast.39, bf16[8,512,128]{2,1,0:T(8,128)(2,1)} %bitcast.36), custom_call_target="tpu_custom_call" | custom-call | tf_op jit(solution)/shard_map/relation_update/pallas_call | solution.py:323
  176.2 27.1 %all-to-all-done.2.back_ref = bf16[16,608,128]{2,1,0:T(8,128)(2,1)S(1)} async-done(((bf16[16,608,128]{2,1,0:T(8,128)(2,1)}), bf16[16,608,128]{2,1,0:T(8,128)(2,1)S(1)}, u32[]{:S(2)}, u32[]{:S(2)}) %all-to-all-start.2) | async-done | bytes 2490400 | tf_op jit(solution)/shard_map/all_to_all | solution.py:370
  203.3 0.0 all-gather.7.cloned.1.call-done
  203.3 3.4 %right_update.1 = (f32[400,256]{1,0:T(8,128)}, f32[1,256]{1,0:T(1,128)}) custom-call(s32[1]{0:T(128)S(6)} %copy.18.partner_ref, f32[8,408,256]{2,1,0:T(8,128)} %bitcast.41, s32[16,8,128]{2,1,0:T(8,128)S(1)} %all-to-all-done.asked_ref, bf16[16,608,128]{2,1,0:T(8,128)(2,1)S(1)} %all-to-all-done.2.back_ref), custom_call_target="tpu_custom_call" | custom-call | flops 2000000000 | bytes 5000000 | tf_op jit(solution)/shard_map/right_update/pallas_call | solution.py:277
  (4 shorter events, 0.0 us)
Async XLA Ops:
  7.2 31.2 %all-gather.5.cloned.1.call-start = ((), (), s32[]{:S(2)}) async-start(), calls=%async_computation.5 | async-start | bytes 1843200 | tf_op jit(solution)/shard_map/all_gather | solution.py:348
  19.8 15.1 %all-to-all-start = ((s32[16,8,128]{2,1,0:T(8,128)}), s32[16,8,128]{2,1,0:T(8,128)S(1)}, u32[]{:S(2)}, u32[]{:S(2)}) async-start(s32[16,8,128]{2,1,0:T(8,128)} %add_add_fusion), calls=%async_computation | async-start | bytes 131072 | tf_op jit(solution)/shard_map/all_to_all | solution.py:360
  38.4 1.0 copy-start.1
  39.4 1.4 copy-start.4
  40.8 0.7 copy-start.5
  44.1 7.6 %copy-start = (f32[1000,400]{0,1:T(8,128)S(1)}, f32[1000,400]{0,1:T(8,128)}, u32[]{:S(2)}) copy-start(f32[1000,400]{0,1:T(8,128)} %param.16) | copy-start | bytes 4800004
  44.1 7.6 %copy-start.2 = (f32[1,256,400]{1,2,0:T(8,128)S(1)}, f32[1,256,400]{1,2,0:T(8,128)}, u32[]{:S(2)}) copy-start(f32[1,256,400]{1,2,0:T(8,128)} %param.12) | copy-start | bytes 1228804
  44.1 45.2 %all-to-all-start.1 = ((bf16[16,608,128]{2,1,0:T(8,128)(2,1)}), bf16[16,608,128]{2,1,0:T(8,128)(2,1)}, u32[]{:S(2)}, u32[]{:S(2)}) async-start(bf16[16,608,128]{2,1,0:T(8,128)(2,1)} %get-tuple-element.20), calls=%async_computation.1 | async-start | bytes 4980736 | tf_op jit(solution)/shard_map/all_to_all | solution.py:366
  50.9 152.4 %all-gather.7.cloned.1.call-start = ((), (), s32[]{:S(2)}) async-start(), calls=%async_computation.6 | async-start | bytes 3760128 | tf_op jit(solution)/shard_map/all_gather | solution.py:365
  58.9 1.2 copy-start.6
  89.2 1.4 copy-start.7
  114.8 0.8 copy-start.3
  164.3 39.1 %all-to-all-start.2 = ((bf16[16,608,128]{2,1,0:T(8,128)(2,1)}), bf16[16,608,128]{2,1,0:T(8,128)(2,1)S(1)}, u32[]{:S(2)}, u32[]{:S(2)}) async-start(bf16[16,608,128]{2,1,0:T(8,128)(2,1)} %get-tuple-element.28), calls=%async_computation.2 | async-start | bytes 4980736 | tf_op jit(solution)/shard_map/all_to_all | solution.py:370
Sparse Core Ops, SparseCore 0:
  10.3 28.0 all-gather.4
  53.5 29.1 all-gather.6

commit v2 on v1

v2 whole, which is shorter than its diff:
```python
import jax
import jax.numpy as jnp
from jax import lax
from jax.experimental import pallas as pl
from jax.experimental.pallas import tpu as pltpu
from jax.sharding import PartitionSpec as P

LEARN = 0.25
TINY = 1e-10
BF = jnp.bfloat16
F32 = jnp.float32
D = 400
HALF = 200
REL = 1000
RELP = 1024
LOCAL = 256
EDGES = 2048
NEG = 1024
OWNERS = 16
PER = 128
FOLD = 208
SEND = D + FOLD
BACK = SEND + 16
CHUNK = 256
STEPS = EDGES // CHUNK
SUB = 2
MIB = 1024 * 1024


def onehot(index, count):
    rows = lax.broadcasted_iota(jnp.int32, (count, index.shape[1]), 0)
    return jnp.where(rows == index, 1.0, 0.0).astype(BF)


def dot(a, b):
    return jnp.dot(a, b, preferred_element_type=F32)


def dot_t(a, b):
    return lax.dot_general(a, b, (((1,), (1,)), ((), ())), preferred_element_type=F32)


def split(value):
    high = value.astype(BF)
    return high, (value - high.astype(F32)).astype(BF)


def lhs_of(packed):
    return jnp.bitwise_and(jnp.right_shift(packed, 1), LOCAL - 1)


def rel_of(packed):
    return jnp.bitwise_and(jnp.right_shift(packed, 9), RELP - 1)


def query_kernel(packed_ref, lhs_ref, rel_ref, l_ref, w_ref, q_ref, lhs_two, rel_two):
    @pl.when(pl.program_id(0) == 0)
    def _():
        high, low = split(lhs_ref[...])
        lhs_two[0:D, :] = high
        lhs_two[D : 2 * D, :] = low
        rel_two[...] = jnp.zeros_like(rel_two)
        high, low = split(rel_ref[...])
        rel_two[0:D, 0:REL] = high
        rel_two[D : 2 * D, 0:REL] = low

    packed = packed_ref[...]
    both = dot(lhs_two[...], onehot(lhs_of(packed), LOCAL))
    left = both[0:D] + both[D : 2 * D]
    both = dot(rel_two[...], onehot(rel_of(packed), RELP))
    weight = both[0:D] + both[D : 2 * D]
    l_ref[...] = left
    w_ref[...] = weight
    la, lb, wa, wb = left[:HALF], left[HALF:], weight[:HALF], weight[HALF:]
    q_ref[...] = jnp.concatenate([la * wa - lb * wb, la * wb + lb * wa], 0).astype(BF)


def make_query(packed, lhs_t, rel_t):
    wide = pl.BlockSpec((D, CHUNK), lambda i: (0, i))
    return pl.pallas_call(
        query_kernel,
        grid=(STEPS,),
        in_specs=[
            pl.BlockSpec((1, CHUNK), lambda i: (0, i)),
            pl.BlockSpec((D, LOCAL), lambda i: (0, 0)),
            pl.BlockSpec((D, REL), lambda i: (0, 0)),
        ],
        out_specs=[wide, wide, wide],
        out_shape=[
            jax.ShapeDtypeStruct((D, EDGES), F32),
            jax.ShapeDtypeStruct((D, EDGES), F32),
            jax.ShapeDtypeStruct((D, EDGES), BF),
        ],
        scratch_shapes=[pltpu.VMEM((2 * D, LOCAL), BF), pltpu.VMEM((2 * D, RELP), BF)],
        compiler_params=pltpu.CompilerParams(vmem_limit_bytes=58 * MIB),
        cost_estimate=pl.CostEstimate(flops=5_000_000_000, bytes_accessed=10_000_000, transcendentals=0),
        name="make_query",
    )(packed, lhs_t, rel_t)


def fold_marks(marks):
    first = lax.broadcasted_iota(jnp.int32, marks.shape, 1) < 64
    none = jnp.zeros_like(marks)
    return jnp.where(first, marks, none), jnp.where(first, none, marks)


def twice(row):
    first = lax.broadcasted_iota(jnp.int32, row.shape, 1) < 64
    turned = pltpu.roll(row, 64, 1)
    return jnp.where(first, row, turned), jnp.where(first, turned, row)


def labels(pos, neg):
    row = lax.broadcasted_iota(jnp.int32, (16, PER), 0)
    return jnp.where(row == 0, pos, jnp.where(row == 1, neg, 0)).astype(F32).astype(BF)


def edge_kernel(
    place_ref, packed_ref, neg_ref, a0, a1, a2, a3, b0, b1, b2, b3, q_ref, l_ref, w_ref,
    back_ref, lhs_g, lhs_lo, rel_g, table, neg_t, neg_n, weights, q_all,
):
    step = pl.program_id(0)

    @pl.when(step == 0)
    def _():
        for z, a in enumerate((a0, a1, a2, a3)):
            for y, b in enumerate((b0, b1, b2, b3)):
                table[4 * z + y, :, 0:PER] = a[y]
                table[4 * z + y, :, PER:LOCAL] = b[z]
        for c in range(STEPS):
            here = jnp.bitwise_and(neg_ref[c : c + 1, :], LOCAL - 1)
            one, two = fold_marks(onehot(here, LOCAL))
            rows = dot(table[2 * c], one) + dot(table[2 * c + 1], two)
            lanes = slice(c * PER, (c + 1) * PER)
            neg_t[:, lanes] = rows.astype(BF)
            neg_n[lanes, :] = rows.T.astype(BF)

    for h in range(SUB):
        part = step * SUB + h
        lanes = pl.ds(pl.multiple_of(part * CHUNK, CHUNK), CHUNK)
        own = slice(h * CHUNK, (h + 1) * CHUNK)
        packed = packed_ref[:, own]
        live = jnp.bitwise_and(packed, 1).astype(F32)
        query = q_ref[:, own]
        query_wide = query.astype(F32)
        asked = jnp.bitwise_and(jnp.right_shift(packed, 19), LOCAL - 1)
        marks = onehot(asked, LOCAL)
        pos = jnp.concatenate([dot(table[2 * part], marks[:, 0:PER]), dot(table[2 * part + 1], marks[:, PER:])], 1)
        scores = dot(neg_n[...], query)
        pos_score = jnp.sum(query_wide * pos, 0, keepdims=True)
        highest = jnp.maximum(pos_score, jnp.max(scores, 0, keepdims=True))
        neg_exp = jnp.exp(scores - highest)
        pos_exp = jnp.exp(pos_score - highest)
        total = pos_exp + jnp.sum(neg_exp, 0, keepdims=True)
        pos_weight = live * (pos_exp / total - 1.0)
        weight = (neg_exp * (live / total)).astype(BF)
        weights[:, lanes] = weight
        grad = pos_weight * pos + dot(neg_t[...], weight)
        pos_grad = (pos_weight * query_wide).astype(BF)
        one, two = twice(jnp.bitwise_and(neg_ref[pl.ds(part, 1), :], LOCAL - 1))
        k, m = place_ref[2 * part], place_ref[2 * part + 1]
        back_ref[k, 0:D, :] = pos_grad[:, 0:PER]
        back_ref[m, 0:D, :] = pos_grad[:, PER:]
        back_ref[k, SEND:BACK, :] = labels(asked[:, 0:PER], one)
        back_ref[m, SEND:BACK, :] = labels(asked[:, PER:], two)
        ga, gb = grad[:HALF], grad[HALF:]
        left, rel = l_ref[:, own], w_ref[:, own]
        la, lb, wa, wb = left[:HALF], left[HALF:], rel[:HALF], rel[HALF:]
        lhs_g[:, own], lhs_lo[:, own] = split(jnp.concatenate([ga * wa + gb * wb, gb * wa - ga * wb], 0))
        rel_g[:, own] = jnp.concatenate([ga * la + gb * lb, gb * la - ga * lb], 0).astype(BF)
        q_all[:, lanes] = query

    @pl.when(step == STEPS // SUB - 1)
    def _():
        for c in range(0, STEPS, 2):
            part = dot_t(q_all[...], weights[c * PER : (c + 2) * PER, :])
            for h in (0, 1):
                both = part[:, h * PER : (h + 1) * PER]
                top = both[0:FOLD]
                low = jnp.concatenate([both[FOLD:D], jnp.zeros((2 * FOLD - D, PER), F32)], 0)
                first = lax.broadcasted_iota(jnp.int32, top.shape, 1) < 64
                at = 2 * (c + h)
                back_ref[place_ref[at], D:SEND, :] = jnp.where(first, top, pltpu.roll(low, 64, 1)).astype(BF)
                back_ref[place_ref[at + 1], D:SEND, :] = jnp.where(first, pltpu.roll(top, 64, 1), low).astype(BF)


def edges(place, packed, neg, halves, query, left, weight):
    wide = pl.BlockSpec((D, SUB * CHUNK), lambda i, p: (0, i))
    whole = lambda shape: pl.BlockSpec(shape, lambda i, p: (0,) * len(shape))
    return pl.pallas_call(
        edge_kernel,
        grid_spec=pltpu.PrefetchScalarGridSpec(
            num_scalar_prefetch=1,
            grid=(STEPS // SUB,),
            in_specs=[pl.BlockSpec((1, SUB * CHUNK), lambda i, p: (0, i)), whole((STEPS, PER))]
            + [whole((4, D, PER))] * 8
            + [wide, wide, wide],
            out_specs=[whole((OWNERS, BACK, PER)), wide, wide, wide],
            scratch_shapes=[
                pltpu.VMEM((OWNERS, D, LOCAL), BF),
                pltpu.VMEM((D, NEG), BF),
                pltpu.VMEM((NEG, D), BF),
                pltpu.VMEM((NEG, EDGES), BF),
                pltpu.VMEM((D, EDGES), BF),
            ],
        ),
        out_shape=[
            jax.ShapeDtypeStruct((OWNERS, BACK, PER), BF),
            jax.ShapeDtypeStruct((D, EDGES), BF),
            jax.ShapeDtypeStruct((D, EDGES), BF),
            jax.ShapeDtypeStruct((D, EDGES), BF),
        ],
        compiler_params=pltpu.CompilerParams(vmem_limit_bytes=58 * MIB),
        cost_estimate=pl.CostEstimate(flops=8_000_000_000, bytes_accessed=20_000_000, transcendentals=2_100_000),
        name="edges",
    )(place, packed, neg, *halves, query, left, weight)


def sums_kernel(core_ref, packed_ref, lhs_g, lhs_lo, rel_g, rel_ref, lhs_ref, m_lhs, m_rel):
    step = pl.program_id(0)
    lanes = pl.ds(pl.multiple_of(step * CHUNK, CHUNK), CHUNK)
    packed = packed_ref[...]
    m_lhs[:, lanes] = onehot(lhs_of(packed), LOCAL)
    m_rel[:, lanes] = onehot(rel_of(packed), RELP)

    @pl.when(step == STEPS - 1)
    def _():
        for t in range(0, RELP // PER, 2):
            part = dot_t(rel_g[...], m_rel[t * PER : (t + 2) * PER, :]).astype(BF)
            side, at = jnp.bitwise_xor(core_ref[0], t // 4), t % 4
            rel_ref[side, at, 0:D, :] = part[:, 0:PER]
            rel_ref[side, at + 1, 0:D, :] = part[:, PER:]
            rel_ref[side, at, D:512, :] = jnp.zeros((112, PER), BF)
            rel_ref[side, at + 1, D:512, :] = jnp.zeros((112, PER), BF)
        lhs_ref[...] = dot_t(lhs_g[...], m_lhs[...]) + dot_t(lhs_lo[...], m_lhs[...])


def sums(core, packed, lhs_g, lhs_lo, rel_g):
    whole = lambda shape: pl.BlockSpec(shape, lambda i, p: (0,) * len(shape))
    return pl.pallas_call(
        sums_kernel,
        grid_spec=pltpu.PrefetchScalarGridSpec(
            num_scalar_prefetch=1,
            grid=(STEPS,),
            in_specs=[pl.BlockSpec((1, CHUNK), lambda i, p: (0, i))] + [whole((D, EDGES))] * 3,
            out_specs=[whole((2, 4, 512, PER)), whole((D, LOCAL))],
            scratch_shapes=[pltpu.VMEM((LOCAL, EDGES), BF), pltpu.VMEM((RELP, EDGES), BF)],
        ),
        out_shape=[
            jax.ShapeDtypeStruct((2, 4, 512, PER), BF),
            jax.ShapeDtypeStruct((D, LOCAL), F32),
        ],
        compiler_params=pltpu.CompilerParams(vmem_limit_bytes=58 * MIB),
        cost_estimate=pl.CostEstimate(flops=3_000_000_000, bytes_accessed=6_000_000, transcendentals=0),
        name="edge_sums",
    )(core, packed, lhs_g, lhs_lo, rel_g)


def total_kernel(parts_ref, out_ref):
    total = jnp.sum(parts_ref[...].astype(F32), 0).astype(BF)
    out_ref[...] = jnp.broadcast_to(total[None], out_ref.shape)


def total_for_all(parts):
    return pl.pallas_call(
        total_kernel,
        out_shape=jax.ShapeDtypeStruct(parts.shape, BF),
        name="total_for_all",
    )(parts)


def adagrad(table, accum, grad):
    new_accum = accum + jnp.mean(grad * grad, 0, keepdims=True)
    return table - grad * (LEARN / (jnp.sqrt(new_accum) + TINY)), new_accum


def right_kernel(partner_ref, ext_ref, back_ref, new_ref, accum_ref, pos, neg, m_pos, m_one, m_two):
    del partner_ref
    for s in range(OWNERS):
        lanes = slice(s * PER, (s + 1) * PER)
        pos[:, lanes] = back_ref[s, 0:D, :]
        neg[:, lanes] = back_ref[s, D:SEND, :]
        named = back_ref[s, SEND:BACK, :].astype(F32).astype(jnp.int32)
        m_pos[:, lanes] = onehot(named[0:1], LOCAL)
        m_one[:, lanes], m_two[:, lanes] = fold_marks(onehot(named[1:2], LOCAL))
    low = dot_t(neg[...], m_two[...])[0 : D - FOLD]
    grad = dot_t(pos[...], m_pos[...]) + jnp.concatenate([dot_t(neg[...], m_one[...]), low], 0)
    new_ref[...], accum_ref[...] = adagrad(ext_ref[0, 0:D, :], ext_ref[0, D : D + 1, :], grad)


def right_update(partner, ext_all, back):
    whole = lambda shape: pl.BlockSpec(shape, lambda i, p: (0,) * len(shape))
    marks = pltpu.VMEM((LOCAL, OWNERS * PER), BF)
    return pl.pallas_call(
        right_kernel,
        grid_spec=pltpu.PrefetchScalarGridSpec(
            num_scalar_prefetch=1,
            grid=(1,),
            in_specs=[
                pl.BlockSpec((1, D + 8, LOCAL), lambda i, p: (p[0], 0, 0)),
                whole((OWNERS, BACK, PER)),
            ],
            out_specs=[whole((D, LOCAL)), whole((1, LOCAL))],
            scratch_shapes=[
                pltpu.VMEM((D, OWNERS * PER), BF),
                pltpu.VMEM((FOLD, OWNERS * PER), BF),
                marks,
                marks,
                marks,
            ],
        ),
        out_shape=[jax.ShapeDtypeStruct((D, LOCAL), F32), jax.ShapeDtypeStruct((1, LOCAL), F32)],
        compiler_params=pltpu.CompilerParams(vmem_limit_bytes=20 * MIB),
        cost_estimate=pl.CostEstimate(flops=2_000_000_000, bytes_accessed=5_000_000, transcendentals=0),
        name="right_update",
    )(partner, ext_all, back)


def left_kernel(table_ref, accum_ref, grad_ref, new_ref, new_accum_ref):
    new_ref[...], new_accum_ref[...] = adagrad(table_ref[...], accum_ref[...], grad_ref[...])


def left_update(table, accum, grad):
    return pl.pallas_call(
        left_kernel,
        out_shape=[jax.ShapeDtypeStruct((D, LOCAL), F32), jax.ShapeDtypeStruct((1, LOCAL), F32)],
        name="left_update",
    )(table, accum, grad)


def relation_kernel(core_ref, table_ref, accum_ref, own_ref, other_ref, new_ref, new_accum_ref):
    owned = pl.program_id(0) // 2 == core_ref[0]
    first, second = jnp.where(owned, own_ref[0, 0:D, :], other_ref[0, 0:D, :]), jnp.where(owned, own_ref[1, 0:D, :], other_ref[1, 0:D, :])
    grad = jnp.concatenate([first, second], 1).astype(F32)
    new_ref[...], new_accum_ref[...] = adagrad(table_ref[...], accum_ref[...], grad)


def relation_update(core, table, accum, own, other):
    tall = pl.BlockSpec((D, 2 * PER), lambda i, p: (0, i))
    flat = pl.BlockSpec((1, 2 * PER), lambda i, p: (0, i))
    half = pl.BlockSpec((2, 512, PER), lambda i, p: (i % 2, 0, 0))
    return pl.pallas_call(
        relation_kernel,
        grid_spec=pltpu.PrefetchScalarGridSpec(
            num_scalar_prefetch=1,
            grid=(4,),
            in_specs=[tall, flat, half, half],
            out_specs=[tall, flat],
        ),
        out_shape=[jax.ShapeDtypeStruct((D, REL), F32), jax.ShapeDtypeStruct((1, REL), F32)],
        name="relation_update",
    )(core, table, accum, own, other)


CORES = [(0, 1), (1, 0)]
GRP, ROW, CHIPS = ("x", "core"), ("z", "y"), ("x", "z", "y")


def shift(value, axis, distance):
    return lax.ppermute(value, axis, [(i, (i + distance) & 3) for i in range(4)])


def other_core(value):
    return lax.ppermute(value, "core", CORES)


def pick(near, target, group):
    back = ((group >> 1) - (target >> 1)) & 3
    return jnp.where(back < 2, jnp.where(back == 0, near[0], near[1]), jnp.where(back == 2, near[2], near[3]))


def relative(owner, z, y):
    return (((z - (owner >> 2)) & 3) << 2) | ((y - (owner & 3)) & 3)


def gather_rows(first, second):
    lines = [[first] + [shift(first, "y", d) for d in (2, 1, 3)], [second] + [shift(second, "z", d) for d in (2, 1, 3)]]
    (f0, f2, f1, f3), (s0, s2, s1, s3) = lax.optimization_barrier(lines)
    first, second = jnp.stack([f0, f1, f2, f3]), jnp.stack([s0, s1, s2, s3])
    f2, s2 = shift(first, "z", 2), shift(second, "y", 2)
    f1, s1 = shift(first, "z", 1), shift(second, "y", 1)
    f3, s3 = shift(first, "z", 3), shift(second, "y", 3)
    return [first, f1, f2, f3, second, s1, s2, s3]


def body(
    lhs_emb,
    lhs_accum,
    rhs_emb,
    rhs_accum,
    rel_emb,
    rel_accum,
    partner,
    edge_lhs,
    edge_rhs,
    edge_rel,
    edge_count,
    neg_rhs,
):
    lhs_t, rhs_t, rel_t = lhs_emb[0].T, rhs_emb[0].T, rel_emb.T
    core, z, y = lax.axis_index("core"), lax.axis_index("z"), lax.axis_index("y")
    group = 2 * lax.axis_index("x") + core

    mine = rhs_t.astype(BF)
    target = partner[0]
    other = other_core(partner)[0]
    near = [mine] + [shift(mine, "x", d) for d in (1, 2, 3)]
    here = pick(near, target, group)
    across = other_core(pick(near, other, group))
    held = jnp.where((target & 1) == (group & 1), here, across)
    order = jnp.arange(OWNERS, dtype=jnp.int32)
    place = relative(order, z, y)
    live = (jnp.arange(EDGES, dtype=jnp.int32) < edge_count[0, 0]).astype(jnp.int32)
    pos_key = (relative(edge_rhs[0, 0] >> 8, z, y) << 27) | ((edge_rhs[0, 0] & (LOCAL - 1)) << 19)
    pos_key = pos_key | (edge_rel[0, 0] << 9) | (edge_lhs[0, 0] << 1) | live
    neg_key = (relative(neg_rhs[0, 0] >> 8, z, y) << 8) | (neg_rhs[0, 0] & (LOCAL - 1))
    spare = jnp.full((EDGES - NEG,), 1 << 30, jnp.int32)
    keys = jnp.stack([pos_key, jnp.concatenate([neg_key, spare])])
    exact = jnp.concatenate([rhs_t, jnp.broadcast_to(rhs_accum, (8, LOCAL))], 0)
    exact, held, keys = lax.optimization_barrier((exact, held, keys))
    ext_all = lax.all_gather(exact, GRP, axis=0, tiled=False)
    halves = gather_rows(held[:, :PER], held[:, PER:])
    packed, neg_index = lax.sort(keys, is_stable=False)
    neg_index = neg_index[:NEG].reshape(STEPS, PER)
    packed = packed.reshape(1, EDGES)
    left, weight, query = make_query(packed, lhs_t, rel_t)

    back, lhs_g, lhs_lo, rel_g = edges(place, packed, neg_index, halves, query, left, weight)
    returned = lax.all_to_all(back, ROW, 0, 0, tiled=True)
    at_core = core.astype(jnp.int32).reshape(1)
    rel_sums, lhs_sum = sums(at_core, packed, lhs_g, lhs_lo, rel_g)
    rel_sum = (rel_sums[0].astype(F32) + other_core(rel_sums[1]).astype(F32)).astype(BF)
    rel_sum, returned = lax.optimization_barrier((rel_sum, returned))
    parts = lax.all_to_all(rel_sum.reshape(64, 32, PER), CHIPS, 0, 0, tiled=True)
    own = lax.all_to_all(total_for_all(parts), CHIPS, 0, 0, tiled=True).reshape(4, 512, PER)

    new_lhs, new_lhs_accum = left_update(lhs_t, lhs_accum, lhs_sum)
    new_rhs, new_rhs_accum = right_update(partner, ext_all, returned)
    own, new_rhs = lax.optimization_barrier((own, new_rhs))
    new_rel, new_rel_accum = relation_update(at_core, rel_t, rel_accum[None], own, other_core(own))
    return (
        new_lhs.T[None],
        new_lhs_accum,
        new_rhs.T[None],
        new_rhs_accum,
        new_rel.T,
        new_rel_accum[0],
    )


def solution(mesh):
    fine = jax.sharding.Mesh(mesh.devices.reshape(4, 2, 4, 4), ("x", "core", "z", "y"))
    rows = P(GRP, ROW, None)
    in_specs = (rows, P(GRP, ROW), rows, P(GRP, ROW), P(), P(), P(GRP), rows, rows, rows, P(GRP, ROW), rows)
    out_specs = (rows, P(GRP, ROW), rows, P(GRP, ROW), P(), P())
    return jax.shard_map(body, mesh=fine, in_specs=in_specs, out_specs=out_specs, check_vma=False)
```

time: 216 us -> 188 us (0.87)
  blocking collectives: 48.4 us -> 20.1 us
  waiting for transfers between devices: 66.2 us -> 41.4 us
  starting transfers between devices: 19.3 us -> 44.1 us
  other arithmetic: 11.9 us -> 6.97 us
  Pallas kernels: 45.5 us -> 48.9 us
  between operations: 15.4 us -> 17.6 us
    all_to_all x3 -> x2, waiting for transfers between devices: 62.1 us -> 25.6 us  [the longest x1 19.3 us: body(): returned = lax.all_to_all(back, ROW, 0, 0, tiled=True)]
    ppermute x0 -> x19, starting transfers between devices: none -> 31 us  [the longest x15 22.1 us: shift(): return lax.ppermute(value, axis, [(i, i + distance & 3) for i in range(4)])]
    all_to_all x2 -> x1, blocking collectives: 48.4 us -> 20.1 us  [body(): lax.all_to_all(rel_sum.reshape(64, 32, PER), CHIPS, 0, 0, tiled=True)]
    ppermute x0 -> x19, waiting for transfers between devices: none -> 15.2 us  [the longest x15 13.2 us: shift(): return lax.ppermute(value, axis, [(i, i + distance & 3) for i in range(4)])]
    sort x2 -> x0, other arithmetic: 8.51 us -> none  [the longest x1 4.26 us: body(): neg_index = lax.sort(neg_rhs[0, 0], is_stable=False)]
    all_to_all x3 -> x2, starting transfers between devices: 19.2 us -> 13.1 us  [the longest x1 8.12 us: body(): returned = lax.all_to_all(back, ROW, 0, 0, tiled=True)]
    all_gather x2 -> x1, waiting for transfers between devices: 3.4 us -> 0.03 us  [body(): ext_all = lax.all_gather(exact, GRP, axis=0, tiled=False)]
    unnamed x16 -> x25, local copies, waits for them, and re-layouts: 6.46 us -> 3.56 us
  transfers between devices with their start and end apart: 5 -> 22, of which waited for: 4 -> 12; matrix products, arithmetic and copies ran while one was open for 5% -> 5% of each run, Pallas kernels for 19% -> 24%
where the time goes in v2:
time: 188 us; the launch traced here: 187 us
  Pallas kernels  48.9 us (26%)
  starting transfers between devices  44.1 us (23%)
  waiting for transfers between devices  41.4 us (22%)
  blocking collectives  20.1 us (11%)
  between operations  17.6 us (9%)
  local copies, waits for them, and re-layouts  7.99 us (4%)
  other arithmetic  6.97 us (4%)
    ppermute x15, starting transfers between devices, shift(): return lax.ppermute(value, axis, [(i, i + distance & 3) for i in range(4)])  22.1 us
    pallas_call x1, Pallas kernels, edges(): pl.pallas_call(edge_kernel, grid_spec=pltpu.PrefetchScalarGridSpec(num_sc...  20.6 us
    all_to_all x1, blocking collectives, body(): lax.all_to_all(rel_sum.reshape(64, 32, PER), CHIPS, 0, 0, tiled=True)  20.1 us
    all_to_all x1, waiting for transfers between devices, body(): returned = lax.all_to_all(back, ROW, 0, 0, tiled=True)  19.3 us
    ppermute x15, waiting for transfers between devices, shift(): return lax.ppermute(value, axis, [(i, i + distance & 3) for i in range(4)])  13.2 us
    pallas_call x1, Pallas kernels, sums(): pl.pallas_call(sums_kernel, grid_spec=pltpu.PrefetchScalarGridSpec(num_sc...  9.02 us
    ppermute x4, starting transfers between devices, other_core(): return lax.ppermute(value, 'core', CORES)  8.87 us
    pallas_call x1, Pallas kernels, make_query(): pl.pallas_call(query_kernel, grid=(STEPS,), in_specs=[pl.BlockSpec((1, CH...  8.77 us
  transfers between devices with their start and end apart: 22, of which 12 were waited for; matrix products, arithmetic and copies ran while one was open for 5% of the time, Pallas kernels for 24%

profile of v2, /device:TPU:1, one launch (start us, length us, event | category | flops | bytes accessed | tf_op | source)
XLA Modules:
  0.0 187.1 jit_solution(10409814829078303627)
XLA Ops:
  8.0 0.0 copy-start.1
  8.0 0.0 sort.9.cloned.1.call-start
  8.1 1.1 bitcast_convert_fusion
  9.1 2.1 %collective-permute-start = (bf16[400,256]{1,0:T(8,128)(2,1)S(1)}, bf16[400,256]{1,0:T(8,128)(2,1)S(1)}, u32[]{:S(2)}, u32[]{:S(2)}) collective-permute-start(bf16[400,256]{1,0:T(8,128)(2,1)S(1)} %bitcast_convert_fusion), channel_id=1, source_target_pairs={{0,32},{32,64},{64,96},{96,0},{1,33},{33,65},{65,97},{97,1},{2,34}... | collective-permute-start | bytes 614408 | tf_op jit(solution)/shard_map/ppermute | solution.py:360
  11.2 2.5 %collective-permute-start.1 = (bf16[400,256]{1,0:T(8,128)(2,1)S(1)}, bf16[400,256]{1,0:T(8,128)(2,1)S(1)}, u32[]{:S(2)}, u32[]{:S(2)}) collective-permute-start(bf16[400,256]{1,0:T(8,128)(2,1)S(1)} %bitcast_convert_fusion), channel_id=1, source_target_pairs={{0,64},{32,96},{64,0},{96,32},{1,65},{33,97},{65,1},{97,33},{2,66}... | collective-permute-start | bytes 614408 | tf_op jit(solution)/shard_map/ppermute | solution.py:360
  13.7 1.2 collective-permute-start.2
  14.8 1.5 collective-permute-start.3
  17.0 0.8 fusion.1
  17.8 0.7 shift-left_or_fusion
  19.2 0.7 broadcast_in_dim.18
  19.9 1.8 pad_maximum_fusion
  22.3 0.2 collective-permute-done.1
  22.6 0.1 select_select_fusion
  22.6 1.6 collective-permute-start.4
  24.2 0.6 pad_add_fusion
  24.9 0.5 collective-permute-done.4
  25.3 0.1 select_select_fusion.1
  25.4 0.0 sort.9.cloned.1.call-update
  25.4 0.0 all-gather.3.cloned.1.call-start
  25.5 0.5 all-gather.3.cloned.1.call-update
  26.0 3.8 %collective-permute-start.10 = (bf16[400,128]{1,0:T(8,128)(2,1)S(1)}, bf16[400,128]{1,0:T(8,128)(2,1)S(1)}, u32[]{:S(2)}, u32[]{:S(2)}) collective-permute-start(bf16[400,128]{1,0:T(8,128)(2,1)S(1)} %get-tuple-element.42), channel_id=1, source_target_pairs={{0,12},{4,0},{8,4},{12,8},{1,13},{5,1},{9,5},{13,9},{2,14},{6,2},{... | collective-permute-start | bytes 307208 | tf_op jit(solution)/shard_map/ppermute | solution.py:360
  29.9 2.9 %collective-permute-start.5 = (bf16[400,128]{1,0:T(8,128)(2,1)S(1)}, bf16[400,128]{1,0:T(8,128)(2,1)S(1)}, u32[]{:S(2)}, u32[]{:S(2)}) collective-permute-start(bf16[400,128]{1,0:T(8,128)(2,1)S(1)} %get-tuple-element.38), channel_id=1, source_target_pairs={{0,2},{1,3},{2,0},{3,1},{4,6},{5,7},{6,4},{7,5},{8,10},{9,11},{10,... | collective-permute-start | bytes 307208 | tf_op jit(solution)/shard_map/ppermute | solution.py:360
  32.8 0.4 collective-permute-start.6
  33.2 2.3 %collective-permute-start.7 = (bf16[400,128]{1,0:T(8,128)(2,1)S(1)}, bf16[400,128]{1,0:T(8,128)(2,1)S(1)}, u32[]{:S(2)}, u32[]{:S(2)}) collective-permute-start(bf16[400,128]{1,0:T(8,128)(2,1)S(1)} %get-tuple-element.38), channel_id=1, source_target_pairs={{0,3},{1,0},{2,1},{3,2},{4,7},{5,4},{6,5},{7,6},{8,11},{9,8},{10,9... | collective-permute-start | bytes 307208 | tf_op jit(solution)/shard_map/ppermute | solution.py:360
  35.5 0.7 collective-permute-start.9
  36.2 1.3 collective-permute-done.6
  37.5 0.3 collective-permute-done.7
  37.8 2.8 %collective-permute-done.8 = bf16[400,128]{1,0:T(8,128)(2,1)S(1)} collective-permute-done((bf16[400,128]{1,0:T(8,128)(2,1)S(1)}, bf16[400,128]{1,0:T(8,128)(2,1)S(1)}, u32[]{:S(2)}, u32[]{:S(2)}) %collective-permute-start.8) | collective-permute-done | bytes 102432 | tf_op jit(solution)/shard_map/ppermute | solution.py:360
  40.6 1.2 collective-permute-done.9
  41.8 0.1 pad_maximum_fusion.2.b0
  41.9 0.1 collective-permute-start.14
  42.0 0.6 and_or_fusion.place_ref
  42.5 1.3 unstack.6.packed_ref
  43.8 1.3 slice.22
  45.1 2.5 %collective-permute-start.15 = (bf16[4,400,128]{2,1,0:T(8,128)(2,1)S(1)}, bf16[4,400,128]{2,1,0:T(8,128)(2,1)S(1)}, u32[]{:S(2)}, u32[]{:S(2)}) collective-permute-start(bf16[4,400,128]{2,1,0:T(8,128)(2,1)S(1)} %pad_maximum_fusion.2.b0), channel_id=1, source_target_pairs={{0,2},{1,3},{2,0},{3,1},{4,6},{5,7},{6,4},{7,5},{8,10},{9,11},{10,... | collective-permute-start | bytes 1228808 | tf_op jit(solution)/shard_map/ppermute | solution.py:360
  47.7 0.8 collective-permute-start.16
  48.4 0.1 pad_maximum_fusion.1.a0
  48.5 0.1 collective-permute-start.11
  48.6 1.1 collective-permute-start.12
  49.7 2.2 %collective-permute-done.14.b1 = bf16[4,400,128]{2,1,0:T(8,128)(2,1)S(1)} collective-permute-done((bf16[4,400,128]{2,1,0:T(8,128)(2,1)S(1)}, bf16[4,400,128]{2,1,0:T(8,128)(2,1)S(1)}, u32[]{:S(2)}, u32[]{:S(2)}) %collective-permute-start.14) | collective-permute-done | bytes 409632 | tf_op jit(solution)/shard_map/ppermute | solution.py:360
  51.9 1.8 collective-permute-start.13
  53.6 8.8 %make_query.1 = (f32[400,2048]{1,0:T(8,128)}, f32[400,2048]{1,0:T(8,128)}, bf16[400,2048]{1,0:T(8,128)(2,1)}) custom-call(s32[1,2048]{1,0:T(1,128)} %unstack.6.packed_ref, f32[400,256]{1,0:T(8,128)} %bitcast.58, f32[400,1000]{1,0:T(8,128)} %bitcast.54), custom_call_target="tpu_custom_call" | custom-call | flops 5000000000 | bytes 10000000 | tf_op jit(solution)/shard_map/make_query/pallas_call | solution.py:80
  62.5 3.6 %collective-permute-done.16.b3 = bf16[4,400,128]{2,1,0:T(8,128)(2,1)S(1)} collective-permute-done((bf16[4,400,128]{2,1,0:T(8,128)(2,1)S(1)}, bf16[4,400,128]{2,1,0:T(8,128)(2,1)S(1)}, u32[]{:S(2)}, u32[]{:S(2)}) %collective-permute-start.16) | collective-permute-done | bytes 409632 | tf_op jit(solution)/shard_map/ppermute | solution.py:360
  66.1 1.5 collective-permute-done.13.a3
  67.6 0.7 copy-done.11
  68.4 20.6 %edges.1 = (bf16[16,624,128]{2,1,0:T(8,128)(2,1)}, bf16[400,2048]{1,0:T(8,128)(2,1)}, bf16[400,2048]{1,0:T(8,128)(2,1)}, bf16[400,2048]{1,0:T(8,128)(2,1)}) custom-call(s32[16]{0:T(128)} %and_or_fusion.place_ref, s32[1,2048]{1,0:T(1,128)} %unstack.6.packed_ref, s32[8,128]{1,0:T(8,128)} %bitcast.69, bf16[4,400,128]{2,1,0:T(8,128)(2,1)} %copy-done.5, ...), custom_call_target="tpu_custom_call" | custom-call | flops 8000000000 | bytes 20000000 | tf_op jit(solution)/shard_map/edges/pallas_call | solution.py:190
  88.9 8.1 %all-to-all-start = ((bf16[16,624,128]{2,1,0:T(8,128)(2,1)}), bf16[16,624,128]{2,1,0:T(8,128)(2,1)S(1)}, u32[]{:S(2)}, u32[]{:S(2)}) async-start(bf16[16,624,128]{2,1,0:T(8,128)(2,1)} %get-tuple-element.56), calls=%async_computation | async-start | bytes 5111808 | tf_op jit(solution)/shard_map/all_to_all | solution.py:429
  97.1 9.0 %edge_sums.1 = (bf16[2,4,512,128]{3,2,1,0:T(8,128)(2,1)}, f32[400,256]{1,0:T(8,128)}) custom-call(s32[1]{0:T(128)} %bitcast.2.core_ref, s32[1,2048]{1,0:T(1,128)} %unstack.6.packed_ref, bf16[400,2048]{1,0:T(8,128)(2,1)} %get-tuple-element.49.lhs_g, bf16[400,2048]{1,0:T(8,128)(2,1)} %get-tuple-element.50.lhs_lo, bf16[400,2048]{1,0:T(8,128)(2,1)} %get-tuple-element.51.rel_g), custom_call_target="tpu_custom_call" | custom-call | flops 3000000000 | bytes 6000000 | tf_op jit(solution)/shard_map/edge_sums/pallas_call | solution.py:240
  106.1 1.1 slice_bitcast_fusion
  107.2 2.1 %collective-permute-start.17 = (bf16[4,512,128]{2,1,0:T(8,128)(2,1)S(1)}, bf16[4,512,128]{2,1,0:T(8,128)(2,1)S(1)}, u32[]{:S(2)}, u32[]{:S(2)}) collective-permute-start(bf16[4,512,128]{2,1,0:T(8,128)(2,1)S(1)} %slice_bitcast_fusion), channel_id=1, source_target_pairs={{0,16},{16,0},{1,17},{17,1},{2,18},{18,2},{3,19},{19,3},{4,20},{20... | collective-permute-start | bytes 1572872 | tf_op jit(solution)/shard_map/ppermute | solution.py:364
  109.3 1.5 collective-permute-done.17
  110.8 1.2 fusion
  112.0 19.3 %all-to-all-done.back_ref = bf16[16,624,128]{2,1,0:T(8,128)(2,1)S(1)} async-done(((bf16[16,624,128]{2,1,0:T(8,128)(2,1)}), bf16[16,624,128]{2,1,0:T(8,128)(2,1)S(1)}, u32[]{:S(2)}, u32[]{:S(2)}) %all-to-all-start) | async-done | bytes 2555936 | tf_op jit(solution)/shard_map/all_to_all | solution.py:429
  131.3 20.1 %all_to_all.15.parts_ref = bf16[64,32,128]{2,1,0:T(8,128)(2,1)} all-to-all(bf16[64,32,128]{2,1,0:T(8,128)(2,1)S(1)} %bitcast.51), channel_id=1, replica_groups=mesh['x'=4,'core'=2,'z'=4,'y'=4] {'x','z','y'}, dimensions={0} | all-to-all | bytes 1048576 | tf_op jit(solution)/shard_map/all_to_all | solution.py:434
  151.4 1.9 %total_for_all.1 = bf16[64,32,128]{2,1,0:T(8,128)(2,1)} custom-call(bf16[64,32,128]{2,1,0:T(8,128)(2,1)} %all_to_all.15.parts_ref), custom_call_target="tpu_custom_call" | custom-call | tf_op jit(solution)/shard_map/total_for_all/pallas_call | solution.py:265
  153.3 4.9 %all-to-all-start.2 = ((bf16[64,32,128]{2,1,0:T(8,128)(2,1)}), bf16[64,32,128]{2,1,0:T(8,128)(2,1)S(1)}, u32[]{:S(2)}, u32[]{:S(2)}) async-start(bf16[64,32,128]{2,1,0:T(8,128)(2,1)} %total_for_all.1), calls=%async_computation.2 | async-start | bytes 1048576 | tf_op jit(solution)/shard_map/all_to_all | solution.py:435
  158.3 0.0 all-gather.3.cloned.1.call-done
  158.3 1.9 %copy-done = f32[3264,256]{1,0:T(8,128)S(1)} copy-done((f32[3264,256]{1,0:T(8,128)S(1)}, f32[3264,256]{1,0:T(8,128)}, u32[]{:S(2)}) %copy-start) | copy-done | bytes 3342360
  160.2 2.4 %right_update.1 = (f32[400,256]{1,0:T(8,128)}, f32[1,256]{1,0:T(1,128)}) custom-call(s32[1]{0:T(128)S(6)} %copy.18.partner_ref, f32[8,408,256]{2,1,0:T(8,128)S(1)} %bitcast.49, bf16[16,624,128]{2,1,0:T(8,128)(2,1)S(1)} %all-to-all-done.back_ref), custom_call_target="tpu_custom_call" | custom-call | flops 2000000000 | bytes 5000000 | tf_op jit(solution)/shard_map/right_update/pallas_call | solution.py:294
  162.6 6.4 %all-to-all-done.2 = bf16[64,32,128]{2,1,0:T(8,128)(2,1)S(1)} async-done(((bf16[64,32,128]{2,1,0:T(8,128)(2,1)}), bf16[64,32,128]{2,1,0:T(8,128)(2,1)S(1)}, u32[]{:S(2)}, u32[]{:S(2)}) %all-to-all-start.2) | async-done | bytes 524320 | tf_op jit(solution)/shard_map/all_to_all | solution.py:435
  169.0 3.6 %collective-permute-start.18 = (bf16[4,512,128]{2,1,0:T(8,128)(2,1)S(1)}, bf16[4,512,128]{2,1,0:T(8,128)(2,1)S(1)}, u32[]{:S(2)}, u32[]{:S(2)}) collective-permute-start(bf16[4,512,128]{2,1,0:T(8,128)(2,1)S(1)} %bitcast.52), channel_id=1, source_target_pairs={{0,16},{16,0},{1,17},{17,1},{2,18},{18,2},{3,19},{19,3},{4,20},{20... | collective-permute-start | bytes 1572872 | tf_op jit(solution)/shard_map/ppermute | solution.py:364
  172.6 2.0 %left_update.1 = (f32[400,256]{1,0:T(8,128)}, f32[1,256]{1,0:T(1,128)}) custom-call(f32[400,256]{1,0:T(8,128)} %bitcast.59, f32[1,256]{1,0:T(1,128)} %accum_ref.1, f32[400,256]{1,0:T(8,128)} %get-tuple-element.52.grad_ref), custom_call_target="tpu_custom_call" | custom-call | tf_op jit(solution)/shard_map/left_update/pallas_call | solution.py:324
  174.6 0.8 copy-done.3
  175.4 4.2 %relation_update.1 = (f32[400,1000]{1,0:T(8,128)}, f32[1,1000]{1,0:T(1,128)}) custom-call(s32[1]{0:T(128)} %bitcast.2.core_ref, f32[400,1000]{1,0:T(8,128)} %bitcast.55, f32[1,1000]{1,0:T(1,128)} %bitcast.68, bf16[4,512,128]{2,1,0:T(8,128)(2,1)} %bitcast.53, bf16[4,512,128]{2,1,0:T(8,128)(2,1)} %copy-done.3), custom_call_target="tpu_custom_call" | custom-call | tf_op jit(solution)/shard_map/relation_update/pallas_call | solution.py:342
  (33 shorter events, 0.1 us)
Async XLA Ops:
  8.0 14.6 %copy-start.1 = (f32[1,256,400]{1,2,0:T(8,128)S(1)}, f32[1,256,400]{1,2,0:T(8,128)}, u32[]{:S(2)}) copy-start(f32[1,256,400]{1,2,0:T(8,128)} %param.14) | copy-start | bytes 1228804
  8.0 34.5 %sort.9.cloned.1.call-start = ((), (), s32[]{:S(2)}) async-start(), calls=%async_computation.4 | async-start | bytes 49184 | tf_op jit(solution)/shard_map/sort | solution.py:423
  9.1 13.2 %collective-permute-start = (bf16[400,256]{1,0:T(8,128)(2,1)S(1)}, bf16[400,256]{1,0:T(8,128)(2,1)S(1)}, u32[]{:S(2)}, u32[]{:S(2)}) collective-permute-start(bf16[400,256]{1,0:T(8,128)(2,1)S(1)} %bitcast_convert_fusion), channel_id=1, source_target_pairs={{0,32},{32,64},{64,96},{96,0},{1,33},{33,65},{65,97},{97,1},{2,34}... | collective-permute-start | bytes 614408 | tf_op jit(solution)/shard_map/ppermute | solution.py:360
  11.2 11.3 %collective-permute-start.1 = (bf16[400,256]{1,0:T(8,128)(2,1)S(1)}, bf16[400,256]{1,0:T(8,128)(2,1)S(1)}, u32[]{:S(2)}, u32[]{:S(2)}) collective-permute-start(bf16[400,256]{1,0:T(8,128)(2,1)S(1)} %bitcast_convert_fusion), channel_id=1, source_target_pairs={{0,64},{32,96},{64,0},{96,32},{1,65},{33,97},{65,1},{97,33},{2,66}... | collective-permute-start | bytes 614408 | tf_op jit(solution)/shard_map/ppermute | solution.py:360
  13.7 8.9 %collective-permute-start.2 = (bf16[400,256]{1,0:T(8,128)(2,1)S(1)}, bf16[400,256]{1,0:T(8,128)(2,1)S(1)}, u32[]{:S(2)}, u32[]{:S(2)}) collective-permute-start(bf16[400,256]{1,0:T(8,128)(2,1)S(1)} %bitcast_convert_fusion), channel_id=1, source_target_pairs={{0,96},{32,0},{64,32},{96,64},{1,97},{33,1},{65,33},{97,65},{2,98}... | collective-permute-start | bytes 614408 | tf_op jit(solution)/shard_map/ppermute | solution.py:360
  14.8 6.8 %collective-permute-start.3 = (s32[1]{0:T(128)}, s32[1]{0:T(128)}, u32[]{:S(2)}, u32[]{:S(2)}) collective-permute-start(s32[1]{0:T(128)} %param.18), channel_id=1, source_target_pairs={{0,16},{16,0},{1,17},{17,1},{2,18},{18,2},{3,19},{19,3},{4,20},{20... | collective-permute-start | bytes 20 | tf_op jit(solution)/shard_map/ppermute | solution.py:364
  22.6 2.7 %collective-permute-start.4 = (bf16[400,256]{1,0:T(8,128)(2,1)S(1)}, bf16[400,256]{1,0:T(8,128)(2,1)S(1)}, u32[]{:S(2)}, u32[]{:S(2)}) collective-permute-start(bf16[400,256]{1,0:T(8,128)(2,1)S(1)} %select_select_fusion), channel_id=1, source_target_pairs={{0,16},{16,0},{1,17},{17,1},{2,18},{18,2},{3,19},{19,3},{4,20},{20... | collective-permute-start | bytes 614408 | tf_op jit(solution)/shard_map/ppermute | solution.py:364
  25.4 132.8 %all-gather.3.cloned.1.call-start = ((), (), s32[]{:S(2)}) async-start(), calls=%async_computation.3 | async-start | bytes 3760128 | tf_op jit(solution)/shard_map/all_gather | solution.py:421
  26.0 9.4 %collective-permute-start.10 = (bf16[400,128]{1,0:T(8,128)(2,1)S(1)}, bf16[400,128]{1,0:T(8,128)(2,1)S(1)}, u32[]{:S(2)}, u32[]{:S(2)}) collective-permute-start(bf16[400,128]{1,0:T(8,128)(2,1)S(1)} %get-tuple-element.42), channel_id=1, source_target_pairs={{0,12},{4,0},{8,4},{12,8},{1,13},{5,1},{9,5},{13,9},{2,14},{6,2},{... | collective-permute-start | bytes 307208 | tf_op jit(solution)/shard_map/ppermute | solution.py:360
  29.9 6.3 %collective-permute-start.5 = (bf16[400,128]{1,0:T(8,128)(2,1)S(1)}, bf16[400,128]{1,0:T(8,128)(2,1)S(1)}, u32[]{:S(2)}, u32[]{:S(2)}) collective-permute-start(bf16[400,128]{1,0:T(8,128)(2,1)S(1)} %get-tuple-element.38), channel_id=1, source_target_pairs={{0,2},{1,3},{2,0},{3,1},{4,6},{5,7},{6,4},{7,5},{8,10},{9,11},{10,... | collective-permute-start | bytes 307208 | tf_op jit(solution)/shard_map/ppermute | solution.py:360
  32.8 4.7 %collective-permute-start.6 = (bf16[400,128]{1,0:T(8,128)(2,1)S(1)}, bf16[400,128]{1,0:T(8,128)(2,1)S(1)}, u32[]{:S(2)}, u32[]{:S(2)}) collective-permute-start(bf16[400,128]{1,0:T(8,128)(2,1)S(1)} %get-tuple-element.38), channel_id=1, source_target_pairs={{0,1},{1,2},{2,3},{3,0},{4,5},{5,6},{6,7},{7,4},{8,9},{9,10},{10,1... | collective-permute-start | bytes 307208 | tf_op jit(solution)/shard_map/ppermute | solution.py:360
  33.2 4.6 %collective-permute-start.7 = (bf16[400,128]{1,0:T(8,128)(2,1)S(1)}, bf16[400,128]{1,0:T(8,128)(2,1)S(1)}, u32[]{:S(2)}, u32[]{:S(2)}) collective-permute-start(bf16[400,128]{1,0:T(8,128)(2,1)S(1)} %get-tuple-element.38), channel_id=1, source_target_pairs={{0,3},{1,0},{2,1},{3,2},{4,7},{5,4},{6,5},{7,6},{8,11},{9,8},{10,9... | collective-permute-start | bytes 307208 | tf_op jit(solution)/shard_map/ppermute | solution.py:360
  35.5 5.1 %collective-permute-start.8 = (bf16[400,128]{1,0:T(8,128)(2,1)S(1)}, bf16[400,128]{1,0:T(8,128)(2,1)S(1)}, u32[]{:S(2)}, u32[]{:S(2)}) collective-permute-start(bf16[400,128]{1,0:T(8,128)(2,1)S(1)} %get-tuple-element.42), channel_id=1, source_target_pairs={{0,8},{4,12},{8,0},{12,4},{1,9},{5,13},{9,1},{13,5},{2,10},{6,14},... | collective-permute-start | bytes 307208 | tf_op jit(solution)/shard_map/ppermute | solution.py:360
  35.5 6.4 %collective-permute-start.9 = (bf16[400,128]{1,0:T(8,128)(2,1)S(1)}, bf16[400,128]{1,0:T(8,128)(2,1)S(1)}, u32[]{:S(2)}, u32[]{:S(2)}) collective-permute-start(bf16[400,128]{1,0:T(8,128)(2,1)S(1)} %get-tuple-element.42), channel_id=1, source_target_pairs={{0,4},{4,8},{8,12},{12,0},{1,5},{5,9},{9,13},{13,1},{2,6},{6,10},{... | collective-permute-start | bytes 307208 | tf_op jit(solution)/shard_map/ppermute | solution.py:360
  41.9 20.5 %copy-start.4 = (bf16[4,400,128]{2,1,0:T(8,128)(2,1)}, bf16[4,400,128]{2,1,0:T(8,128)(2,1)S(1)}, u32[]{:S(2)}) copy-start(bf16[4,400,128]{2,1,0:T(8,128)(2,1)S(1)} %pad_maximum_fusion.2.b0) | copy-start | bytes 1228804
  41.9 10.0 %collective-permute-start.14 = (bf16[4,400,128]{2,1,0:T(8,128)(2,1)S(1)}, bf16[4,400,128]{2,1,0:T(8,128)(2,1)S(1)}, u32[]{:S(2)}, u32[]{:S(2)}) collective-permute-start(bf16[4,400,128]{2,1,0:T(8,128)(2,1)S(1)} %pad_maximum_fusion.2.b0), channel_id=1, source_target_pairs={{0,1},{1,2},{2,3},{3,0},{4,5},{5,6},{6,7},{7,4},{8,9},{9,10},{10,1... | collective-permute-start | bytes 1228808 | tf_op jit(solution)/shard_map/ppermute | solution.py:360
  45.1 17.3 %collective-permute-start.15 = (bf16[4,400,128]{2,1,0:T(8,128)(2,1)S(1)}, bf16[4,400,128]{2,1,0:T(8,128)(2,1)S(1)}, u32[]{:S(2)}, u32[]{:S(2)}) collective-permute-start(bf16[4,400,128]{2,1,0:T(8,128)(2,1)S(1)} %pad_maximum_fusion.2.b0), channel_id=1, source_target_pairs={{0,2},{1,3},{2,0},{3,1},{4,6},{5,7},{6,4},{7,5},{8,10},{9,11},{10,... | collective-permute-start | bytes 1228808 | tf_op jit(solution)/shard_map/ppermute | solution.py:360
  47.7 18.4 %collective-permute-start.16 = (bf16[4,400,128]{2,1,0:T(8,128)(2,1)S(1)}, bf16[4,400,128]{2,1,0:T(8,128)(2,1)S(1)}, u32[]{:S(2)}, u32[]{:S(2)}) collective-permute-start(bf16[4,400,128]{2,1,0:T(8,128)(2,1)S(1)} %pad_maximum_fusion.2.b0), channel_id=1, source_target_pairs={{0,3},{1,0},{2,1},{3,2},{4,7},{5,4},{6,5},{7,6},{8,11},{9,8},{10,9... | collective-permute-start | bytes 1228808 | tf_op jit(solution)/shard_map/ppermute | solution.py:360
  48.5 13.9 %copy-start.5 = (bf16[4,400,128]{2,1,0:T(8,128)(2,1)}, bf16[4,400,128]{2,1,0:T(8,128)(2,1)S(1)}, u32[]{:S(2)}) copy-start(bf16[4,400,128]{2,1,0:T(8,128)(2,1)S(1)} %pad_maximum_fusion.1.a0) | copy-start | bytes 1228804
  48.5 17.5 %collective-permute-start.11 = (bf16[4,400,128]{2,1,0:T(8,128)(2,1)S(1)}, bf16[4,400,128]{2,1,0:T(8,128)(2,1)S(1)}, u32[]{:S(2)}, u32[]{:S(2)}) collective-permute-start(bf16[4,400,128]{2,1,0:T(8,128)(2,1)S(1)} %pad_maximum_fusion.1.a0), channel_id=1, source_target_pairs={{0,4},{4,8},{8,12},{12,0},{1,5},{5,9},{9,13},{13,1},{2,6},{6,10},{... | collective-permute-start | bytes 1228808 | tf_op jit(solution)/shard_map/ppermute | solution.py:360
  48.6 17.5 %collective-permute-start.12 = (bf16[4,400,128]{2,1,0:T(8,128)(2,1)S(1)}, bf16[4,400,128]{2,1,0:T(8,128)(2,1)S(1)}, u32[]{:S(2)}, u32[]{:S(2)}) collective-permute-start(bf16[4,400,128]{2,1,0:T(8,128)(2,1)S(1)} %pad_maximum_fusion.1.a0), channel_id=1, source_target_pairs={{0,8},{4,12},{8,0},{12,4},{1,9},{5,13},{9,1},{13,5},{2,10},{6,14},... | collective-permute-start | bytes 1228808 | tf_op jit(solution)/shard_map/ppermute | solution.py:360
  51.9 10.6 %copy-start.6 = (bf16[4,400,128]{2,1,0:T(8,128)(2,1)}, bf16[4,400,128]{2,1,0:T(8,128)(2,1)S(1)}, u32[]{:S(2)}) copy-start(bf16[4,400,128]{2,1,0:T(8,128)(2,1)S(1)} %collective-permute-done.14.b1) | copy-start | bytes 1228804
  51.9 15.7 %collective-permute-start.13 = (bf16[4,400,128]{2,1,0:T(8,128)(2,1)S(1)}, bf16[4,400,128]{2,1,0:T(8,128)(2,1)S(1)}, u32[]{:S(2)}, u32[]{:S(2)}) collective-permute-start(bf16[4,400,128]{2,1,0:T(8,128)(2,1)S(1)} %pad_maximum_fusion.1.a0), channel_id=1, source_target_pairs={{0,12},{4,0},{8,4},{12,8},{1,13},{5,1},{9,5},{13,9},{2,14},{6,2},{... | collective-permute-start | bytes 1228808 | tf_op jit(solution)/shard_map/ppermute | solution.py:360
  62.5 5.1 %copy-start.7 = (bf16[4,400,128]{2,1,0:T(8,128)(2,1)}, bf16[4,400,128]{2,1,0:T(8,128)(2,1)S(1)}, u32[]{:S(2)}) copy-start(bf16[4,400,128]{2,1,0:T(8,128)(2,1)S(1)} %collective-permute-done.15.b2) | copy-start | bytes 1228804
  66.0 1.6 copy-start.8
  66.0 1.6 copy-start.9
  66.0 1.6 copy-start.10
  67.6 0.8 copy-start.11
  88.9 42.3 %all-to-all-start = ((bf16[16,624,128]{2,1,0:T(8,128)(2,1)}), bf16[16,624,128]{2,1,0:T(8,128)(2,1)S(1)}, u32[]{:S(2)}, u32[]{:S(2)}) async-start(bf16[16,624,128]{2,1,0:T(8,128)(2,1)} %get-tuple-element.56), calls=%async_computation | async-start | bytes 5111808 | tf_op jit(solution)/shard_map/all_to_all | solution.py:429
  107.2 3.7 %collective-permute-start.17 = (bf16[4,512,128]{2,1,0:T(8,128)(2,1)S(1)}, bf16[4,512,128]{2,1,0:T(8,128)(2,1)S(1)}, u32[]{:S(2)}, u32[]{:S(2)}) collective-permute-start(bf16[4,512,128]{2,1,0:T(8,128)(2,1)S(1)} %slice_bitcast_fusion), channel_id=1, source_target_pairs={{0,16},{16,0},{1,17},{17,1},{2,18},{18,2},{3,19},{19,3},{4,20},{20... | collective-permute-start | bytes 1572872 | tf_op jit(solution)/shard_map/ppermute | solution.py:364
  153.3 15.7 %all-to-all-start.2 = ((bf16[64,32,128]{2,1,0:T(8,128)(2,1)}), bf16[64,32,128]{2,1,0:T(8,128)(2,1)S(1)}, u32[]{:S(2)}, u32[]{:S(2)}) async-start(bf16[64,32,128]{2,1,0:T(8,128)(2,1)} %total_for_all.1), calls=%async_computation.2 | async-start | bytes 1048576 | tf_op jit(solution)/shard_map/all_to_all | solution.py:435
  158.3 1.9 %copy-start = (f32[3264,256]{1,0:T(8,128)S(1)}, f32[3264,256]{1,0:T(8,128)}, u32[]{:S(2)}) copy-start(f32[3264,256]{1,0:T(8,128)} %all-gather.3.cloned.1.call-done) | copy-start | bytes 10027012
  169.0 5.6 %copy-start.2 = (bf16[64,32,128]{2,1,0:T(8,128)(2,1)}, bf16[64,32,128]{2,1,0:T(8,128)(2,1)S(1)}, u32[]{:S(2)}) copy-start(bf16[64,32,128]{2,1,0:T(8,128)(2,1)S(1)} %all-to-all-done.2) | copy-start | bytes 1572868
  169.0 5.6 %collective-permute-start.18 = (bf16[4,512,128]{2,1,0:T(8,128)(2,1)S(1)}, bf16[4,512,128]{2,1,0:T(8,128)(2,1)S(1)}, u32[]{:S(2)}, u32[]{:S(2)}) collective-permute-start(bf16[4,512,128]{2,1,0:T(8,128)(2,1)S(1)} %bitcast.52), channel_id=1, source_target_pairs={{0,16},{16,0},{1,17},{17,1},{2,18},{18,2},{3,19},{19,3},{4,20},{20... | collective-permute-start | bytes 1572872 | tf_op jit(solution)/shard_map/ppermute | solution.py:364
  174.6 0.8 copy-start.3
Sparse Core Ops, SparseCore 0:
  25.6 7.6 sort.11.cloned.1.call-done
  (1 shorter events, 0.0 us)
Sparse Core Ops, SparseCore 1:
  27.7 30.5 all-gather.2

commit v3 on v2

v3 whole, which is shorter than its diff:
```python
import functools

import jax
import jax.numpy as jnp
from jax import lax
from jax.experimental import pallas as pl
from jax.experimental.pallas import tpu as pltpu
from jax.sharding import PartitionSpec as P

LEARN = 0.25
TINY = 1e-10
BF = jnp.bfloat16
F32 = jnp.float32
D = 400
HALF = 200
SECOND = 208
TALL = 2 * SECOND
REL = 1000
RELP = 1024
LOCAL = 256
EDGES = 2048
NEG = 1024
OWNERS = 16
PER = 128
FOLD = 208
SEND = D + FOLD
BACK = SEND + 16
CHUNK = 256
STEPS = EDGES // CHUNK
MIB = 1024 * 1024


def onehot(index, count):
    rows = lax.broadcasted_iota(jnp.int32, (count, index.shape[1]), 0)
    return jnp.where(rows == index, 1.0, 0.0).astype(BF)


def dot(a, b):
    return jnp.dot(a, b, preferred_element_type=F32)


def dot_t(a, b):
    return lax.dot_general(a, b, (((1,), (1,)), ((), ())), preferred_element_type=F32)


def split(value):
    high = value.astype(BF)
    return high, (value - high.astype(F32)).astype(BF)


def lhs_of(packed):
    return jnp.bitwise_and(jnp.right_shift(packed, 1), LOCAL - 1)


def rel_of(packed):
    return jnp.bitwise_and(jnp.right_shift(packed, 9), RELP - 1)


def query_kernel(keys_ref, lhs_ref, rel_ref, l_ref, w_ref, q_ref, lhs_two, rel_two):
    @pl.when(pl.program_id(0) == 0)
    def _():
        high, low = split(lhs_ref[...])
        lhs_two[0:D, :] = high
        lhs_two[D : 2 * D, :] = low
        rel_two[...] = jnp.zeros_like(rel_two)
        high, low = split(rel_ref[...])
        rel_two[0:D, 0:REL] = high
        rel_two[D : 2 * D, 0:REL] = low

    packed = keys_ref[0:1, :]
    both = dot(lhs_two[...], onehot(lhs_of(packed), LOCAL))
    left = both[0:D] + both[D : 2 * D]
    both = dot(rel_two[...], onehot(rel_of(packed), RELP))
    weight = both[0:D] + both[D : 2 * D]
    none = jnp.zeros((SECOND - HALF, CHUNK), F32)
    l_ref[...] = jnp.concatenate([left[:HALF], none, left[HALF:], none], 0).astype(BF)
    w_ref[...] = jnp.concatenate([weight[:HALF], none, weight[HALF:], none], 0).astype(BF)
    la, lb, wa, wb = left[:HALF], left[HALF:], weight[:HALF], weight[HALF:]
    q_ref[...] = jnp.concatenate([la * wa - lb * wb, la * wb + lb * wa], 0).astype(BF)


def make_query(keys, lhs_t, rel_t):
    wide = pl.BlockSpec((D, CHUNK), lambda i: (0, i))
    tall = pl.BlockSpec((TALL, CHUNK), lambda i: (0, i))
    return pl.pallas_call(
        query_kernel,
        grid=(STEPS,),
        in_specs=[
            pl.BlockSpec((2, CHUNK), lambda i: (0, i)),
            pl.BlockSpec((D, LOCAL), lambda i: (0, 0)),
            pl.BlockSpec((D, REL), lambda i: (0, 0)),
        ],
        out_specs=[tall, tall, wide],
        out_shape=[
            jax.ShapeDtypeStruct((TALL, EDGES), BF),
            jax.ShapeDtypeStruct((TALL, EDGES), BF),
            jax.ShapeDtypeStruct((D, EDGES), BF),
        ],
        scratch_shapes=[pltpu.VMEM((2 * D, LOCAL), BF), pltpu.VMEM((2 * D, RELP), BF)],
        compiler_params=pltpu.CompilerParams(vmem_limit_bytes=58 * MIB),
        cost_estimate=pl.CostEstimate(flops=5_000_000_000, bytes_accessed=10_000_000, transcendentals=0),
        name="make_query",
    )(keys, lhs_t, rel_t)


def fold_marks(marks):
    first = lax.broadcasted_iota(jnp.int32, marks.shape, 1) < 64
    none = jnp.zeros_like(marks)
    return jnp.where(first, marks, none), jnp.where(first, none, marks)


def twice(row):
    first = lax.broadcasted_iota(jnp.int32, row.shape, 1) < 64
    turned = pltpu.roll(row, 64, 1)
    return jnp.where(first, row, turned), jnp.where(first, turned, row)


def labels(pos, neg):
    row = lax.broadcasted_iota(jnp.int32, (16, PER), 0)
    return jnp.where(row == 0, pos, jnp.where(row == 1, neg, 0)).astype(F32).astype(BF)


def edge_kernel(
    place_ref, keys_ref, a0, a1, a2, a3, b0, b1, b2, b3, q_hbm, l_hbm, w_hbm, back_hbm, lhs_hbm, rel_hbm,
    table, neg_t, neg_n, weights, q_ref, l_ref, w_ref, back_ref, lhs_g, rel_g, scores, pos, grad, sems,
):
    count = iter(range(COPIES))

    def move(source, target):
        copy = pltpu.make_async_copy(source, target, sems.at[next(count)])
        copy.start()
        return copy

    blocks, loads = [], []
    for z, a in enumerate((a0, a1, a2, a3)):
        for y, b in enumerate((b0, b1, b2, b3)):
            at = 4 * z + y
            blocks.append((move(a.at[y], table.at[at, :, 0:PER]), move(b.at[z], table.at[at, :, PER:LOCAL])))
    for hbm, ref in ((q_hbm, q_ref), (l_hbm, l_ref), (w_hbm, w_ref)):
        loads.append(move(hbm, ref))
    for pair in blocks:
        for copy in pair:
            copy.wait()

    for c in range(STEPS):
        here = jnp.bitwise_and(keys_ref[1:2, c * PER : (c + 1) * PER], LOCAL - 1)
        one, two = fold_marks(onehot(here, LOCAL))
        rows = dot(table[2 * c], one) + dot(table[2 * c + 1], two)
        lanes = slice(c * PER, (c + 1) * PER)
        neg_t[:, lanes] = rows.astype(BF)
        neg_n[lanes, :] = rows.T.astype(BF)

    loads[0].wait()
    for part in range(STEPS):
        h = part % BUFFERS
        lanes = own = slice(part * CHUNK, (part + 1) * CHUNK)
        packed = keys_ref[0:1, lanes]
        live = jnp.bitwise_and(packed, 1).astype(F32)
        query = q_ref[:, own]
        asked = jnp.bitwise_and(jnp.right_shift(packed, 19), LOCAL - 1)
        marks = onehot(asked, LOCAL)
        scores[h] = dot(neg_n[...], query)
        pos[h, :, 0:PER] = dot(table[2 * part], marks[:, 0:PER])
        pos[h, :, PER:] = dot(table[2 * part + 1], marks[:, PER:])
        pos_score = jnp.zeros((8, CHUNK), F32)
        for r in range(0, D, 80):
            product = q_ref[r : r + 80, own].astype(F32) * pos[h, r : r + 80]
            pos_score = pos_score + jnp.sum(product.reshape(10, 8, CHUNK), 0)
        pos_score = jnp.sum(pos_score, 0, keepdims=True)
        highest = jnp.broadcast_to(pos_score, (8, CHUNK))
        for r in range(0, NEG, 64):
            highest = jnp.maximum(highest, jnp.max(scores[h, r : r + 64].reshape(8, 8, CHUNK), 0))
        highest = jnp.max(highest, 0, keepdims=True)
        total = jnp.zeros((8, CHUNK), F32)
        for r in range(0, NEG, 64):
            neg_exp = jnp.exp(scores[h, r : r + 64] - highest)
            total = total + jnp.sum(neg_exp.reshape(8, 8, CHUNK), 0)
            scores[h, r : r + 64] = neg_exp
        pos_exp = jnp.exp(pos_score - highest)
        total = pos_exp + jnp.sum(total, 0, keepdims=True)
        pos_weight = live * (pos_exp / total - 1.0)
        scale = live / total
        for r in range(0, NEG, 64):
            weights[r : r + 64, lanes] = (scores[h, r : r + 64] * scale).astype(BF)
        grad[h] = dot(neg_t[...], weights[:, lanes])
        one, two = twice(jnp.bitwise_and(keys_ref[1:2, part * PER : (part + 1) * PER], LOCAL - 1))
        k, m = place_ref[2 * part], place_ref[2 * part + 1]
        back_ref[k, SEND:BACK, :] = labels(asked[:, 0:PER], one)
        back_ref[m, SEND:BACK, :] = labels(asked[:, PER:], two)
        for r in range(0, D, 80):
            pos_grad = (pos_weight * q_ref[r : r + 80, own].astype(F32)).astype(BF)
            back_ref[k, r : r + 80, :] = pos_grad[:, 0:PER]
            back_ref[m, r : r + 80, :] = pos_grad[:, PER:]
        if part == 0:
            loads[1].wait()
            loads[2].wait()
        for r in range(0, HALF, 48):
            n, e = min(48, HALF - r), min(48, SECOND - r)
            ga = grad[h, r : r + n] + pos_weight * pos[h, r : r + n]
            gb = grad[h, HALF + r : HALF + r + n] + pos_weight * pos[h, HALF + r : HALF + r + n]
            if e > n:
                none = jnp.zeros((e - n, CHUNK), F32)
                ga, gb = jnp.concatenate([ga, none], 0), jnp.concatenate([gb, none], 0)
            for factor, out in ((w_ref, lhs_g), (l_ref, rel_g)):
                fa = factor[r : r + e, own].astype(F32)
                fb = factor[SECOND + r : SECOND + r + e, own].astype(F32)
                out[r : r + e, own] = (ga * fa + gb * fb).astype(BF)
                out[SECOND + r : SECOND + r + e, own] = (gb * fa - ga * fb).astype(BF)

    stores = [move(back_ref.at[:, 0:D], back_hbm.at[:, 0:D]), move(rel_g, rel_hbm), move(lhs_g, lhs_hbm)]
    for c in range(0, STEPS, 2):
        part = dot_t(q_ref[...], weights[c * PER : (c + 2) * PER, :])
        for h in (0, 1):
            both = part[:, h * PER : (h + 1) * PER]
            top = both[0:FOLD]
            low = jnp.concatenate([both[FOLD:D], jnp.zeros((2 * FOLD - D, PER), F32)], 0)
            first = lax.broadcasted_iota(jnp.int32, top.shape, 1) < 64
            k, m = place_ref[2 * (c + h)], place_ref[2 * (c + h) + 1]
            back_ref[k, D:SEND, :] = jnp.where(first, top, pltpu.roll(low, 64, 1)).astype(BF)
            back_ref[m, D:SEND, :] = jnp.where(first, pltpu.roll(top, 64, 1), low).astype(BF)
    stores.append(move(back_ref.at[:, D:BACK], back_hbm.at[:, D:BACK]))
    for copy in stores:
        copy.wait()


BUFFERS = 4
COPIES = 2 * OWNERS + 7


def edges(place, keys, halves, query, left, weight):
    anywhere = pl.BlockSpec(memory_space=pl.ANY)
    return pl.pallas_call(
        edge_kernel,
        in_specs=[pl.BlockSpec(memory_space=pltpu.SMEM), pl.BlockSpec(memory_space=pltpu.VMEM)] + [anywhere] * 11,
        out_specs=[anywhere] * 3,
        out_shape=[
            jax.ShapeDtypeStruct((OWNERS, BACK, PER), BF),
            jax.ShapeDtypeStruct((TALL, EDGES), BF),
            jax.ShapeDtypeStruct((TALL, EDGES), BF),
        ],
        scratch_shapes=[
            pltpu.VMEM((OWNERS, D, LOCAL), BF),
            pltpu.VMEM((D, NEG), BF),
            pltpu.VMEM((NEG, D), BF),
            pltpu.VMEM((NEG, EDGES), BF),
            pltpu.VMEM((D, EDGES), BF),
            pltpu.VMEM((TALL, EDGES), BF),
            pltpu.VMEM((TALL, EDGES), BF),
            pltpu.VMEM((OWNERS, BACK, PER), BF),
            pltpu.VMEM((TALL, EDGES), BF),
            pltpu.VMEM((TALL, EDGES), BF),
            pltpu.VMEM((BUFFERS, NEG, CHUNK), F32),
            pltpu.VMEM((BUFFERS, D, CHUNK), F32),
            pltpu.VMEM((BUFFERS, D, CHUNK), F32),
            pltpu.SemaphoreType.DMA((COPIES,)),
        ],
        compiler_params=pltpu.CompilerParams(vmem_limit_bytes=58 * MIB),
        cost_estimate=pl.CostEstimate(flops=8_000_000_000, bytes_accessed=20_000_000, transcendentals=2_100_000),
        name="edges",
    )(place, keys, *halves, query, left, weight)


def sums_kernel(keys_ref, lhs_g, rel_g, own_ref, other_ref, lhs_ref, total):
    wide = 4 * PER
    for c in range(0, EDGES, wide):
        packed = keys_ref[0:1, c : c + wide]
        marks = onehot(rel_of(packed), RELP)
        for t in range(0, RELP, 2 * PER):
            part = dot_t(rel_g[:, c : c + wide], marks[t : t + 2 * PER])
            lanes = slice(t, t + 2 * PER)
            total[:, lanes] = part if c == 0 else total[:, lanes] + part
        part = dot_t(lhs_g[:, c : c + wide], onehot(lhs_of(packed), LOCAL))
        part = jnp.concatenate([part[:HALF], part[SECOND : SECOND + HALF]], 0)
        lhs_ref[...] = part if c == 0 else lhs_ref[...] + part
    own = pl.multiple_of(lax.axis_index("core") * (RELP // 2), RELP // 2)
    other = pl.multiple_of((1 - lax.axis_index("core")) * (RELP // 2), RELP // 2)
    for at in range(4):
        for ref, start in ((own_ref, own), (other_ref, other)):
            lanes = pl.ds(start + at * PER, PER)
            ref[at, 0:D, :] = jnp.concatenate([total[0:HALF, lanes], total[SECOND : SECOND + HALF, lanes]], 0).astype(BF)
            ref[at, D:512, :] = jnp.zeros((112, PER), BF)


def sums(keys, lhs_g, rel_g):
    return pl.pallas_call(
        sums_kernel,
        out_shape=[
            jax.ShapeDtypeStruct((4, 512, PER), BF),
            jax.ShapeDtypeStruct((4, 512, PER), BF),
            jax.ShapeDtypeStruct((D, LOCAL), F32),
        ],
        scratch_shapes=[pltpu.VMEM((TALL, RELP), F32)],
        compiler_params=pltpu.CompilerParams(vmem_limit_bytes=58 * MIB),
        cost_estimate=pl.CostEstimate(flops=3_000_000_000, bytes_accessed=6_000_000, transcendentals=0),
        name="edge_sums",
    )(keys, lhs_g, rel_g)


def spread_kernel(axis, *refs):
    ins, outs = refs[:-4], refs[-4:]
    n = outs[0].shape[0]
    for d in range(4):
        rows = pl.ds(jnp.bitwise_and(lax.axis_index(axis) + d, 3) * n, n)
        total = ins[0][rows].astype(F32)
        for ref in ins[1:]:
            total = total + ref[rows].astype(F32)
        outs[d][...] = total.astype(BF)


def spread(axis, parts):
    n = parts[0].shape[0]
    return pl.pallas_call(
        functools.partial(spread_kernel, axis),
        out_shape=[jax.ShapeDtypeStruct((n // 4, 32, PER), BF)] * 4,
        name="spread",
    )(*parts)


def add_four(parts):
    own, one, two, three = (part.astype(F32) for part in parts)
    return ((own + two) + (one + three)).astype(BF)


def adagrad(table, accum, grad):
    new_accum = accum + jnp.mean(grad * grad, 0, keepdims=True)
    return table - grad * (LEARN / (jnp.sqrt(new_accum) + TINY)), new_accum


def right_kernel(partner_ref, ext_ref, back_ref, new_ref, accum_ref, pos, neg, m_pos, m_one, m_two):
    del partner_ref
    for s in range(OWNERS):
        lanes = slice(s * PER, (s + 1) * PER)
        pos[:, lanes] = back_ref[s, 0:D, :]
        neg[:, lanes] = back_ref[s, D:SEND, :]
        named = back_ref[s, SEND:BACK, :].astype(F32).astype(jnp.int32)
        m_pos[:, lanes] = onehot(named[0:1], LOCAL)
        m_one[:, lanes], m_two[:, lanes] = fold_marks(onehot(named[1:2], LOCAL))
    low = dot_t(neg[...], m_two[...])[0 : D - FOLD]
    grad = dot_t(pos[...], m_pos[...]) + jnp.concatenate([dot_t(neg[...], m_one[...]), low], 0)
    new_ref[...], accum_ref[...] = adagrad(ext_ref[0, 0:D, :], ext_ref[0, D : D + 1, :], grad)


def right_update(partner, ext_all, back):
    whole = lambda shape: pl.BlockSpec(shape, lambda i, p: (0,) * len(shape))
    marks = pltpu.VMEM((LOCAL, OWNERS * PER), BF)
    return pl.pallas_call(
        right_kernel,
        grid_spec=pltpu.PrefetchScalarGridSpec(
            num_scalar_prefetch=1,
            grid=(1,),
            in_specs=[
                pl.BlockSpec((1, D + 8, LOCAL), lambda i, p: (p[0], 0, 0)),
                whole((OWNERS, BACK, PER)),
            ],
            out_specs=[whole((D, LOCAL)), whole((1, LOCAL))],
            scratch_shapes=[
                pltpu.VMEM((D, OWNERS * PER), BF),
                pltpu.VMEM((FOLD, OWNERS * PER), BF),
                marks,
                marks,
                marks,
            ],
        ),
        out_shape=[jax.ShapeDtypeStruct((D, LOCAL), F32), jax.ShapeDtypeStruct((1, LOCAL), F32)],
        compiler_params=pltpu.CompilerParams(vmem_limit_bytes=20 * MIB),
        cost_estimate=pl.CostEstimate(flops=2_000_000_000, bytes_accessed=5_000_000, transcendentals=0),
        name="right_update",
    )(partner, ext_all, back)


def left_kernel(table_ref, accum_ref, grad_ref, new_ref, new_accum_ref):
    new_ref[...], new_accum_ref[...] = adagrad(table_ref[...], accum_ref[...], grad_ref[...])


def left_update(table, accum, grad):
    return pl.pallas_call(
        left_kernel,
        out_shape=[jax.ShapeDtypeStruct((D, LOCAL), F32), jax.ShapeDtypeStruct((1, LOCAL), F32)],
        name="left_update",
    )(table, accum, grad)


def relation_kernel(table_ref, accum_ref, own_ref, other_ref, new_ref, new_accum_ref):
    for t in range(RELP // PER):
        owned = lax.axis_index("core") == t // 4
        back = jnp.bitwise_and(lax.axis_index("x") - t, 3)
        lanes = slice(t * PER, min((t + 1) * PER, REL))
        grad = jnp.where(owned, own_ref[back, 0:D, :], other_ref[back, 0:D, :]).astype(F32)
        grad = grad[:, : lanes.stop - lanes.start]
        new_ref[:, lanes], new_accum_ref[:, lanes] = adagrad(table_ref[:, lanes], accum_ref[:, lanes], grad)


def relation_update(table, accum, own, other):
    return pl.pallas_call(
        relation_kernel,
        out_shape=[jax.ShapeDtypeStruct((D, REL), F32), jax.ShapeDtypeStruct((1, REL), F32)],
        name="relation_update",
    )(table, accum, own, other)


CORES = [(0, 1), (1, 0)]
GRP, ROW, CHIPS = ("x", "core"), ("z", "y"), ("x", "z", "y")


def shift(value, axis, distance):
    return lax.ppermute(value, axis, [(i, (i + distance) & 3) for i in range(4)])


def other_core(value):
    return lax.ppermute(value, "core", CORES)


def pick(near, target, group):
    back = ((group >> 1) - (target >> 1)) & 3
    return jnp.where(back < 2, jnp.where(back == 0, near[0], near[1]), jnp.where(back == 2, near[2], near[3]))


def relative(owner, z, y):
    return (((z - (owner >> 2)) & 3) << 2) | ((y - (owner & 3)) & 3)


def gather_rows(first, second):
    lines = [[first] + [shift(first, "y", d) for d in (2, 1, 3)], [second] + [shift(second, "z", d) for d in (2, 1, 3)]]
    (f0, f2, f1, f3), (s0, s2, s1, s3) = lax.optimization_barrier(lines)
    first, second = jnp.stack([f0, f1, f2, f3]), jnp.stack([s0, s1, s2, s3])
    f2, s2 = shift(first, "z", 2), shift(second, "y", 2)
    f1, s1 = shift(first, "z", 1), shift(second, "y", 1)
    f3, s3 = shift(first, "z", 3), shift(second, "y", 3)
    return [first, f1, f2, f3, second, s1, s2, s3]


def body(
    lhs_emb,
    lhs_accum,
    rhs_emb,
    rhs_accum,
    rel_emb,
    rel_accum,
    partner,
    edge_lhs,
    edge_rhs,
    edge_rel,
    edge_count,
    neg_rhs,
):
    lhs_t, rhs_t, rel_t = lhs_emb[0].T, rhs_emb[0].T, rel_emb.T
    x, core, z, y = (lax.axis_index(axis) for axis in ("x", "core", "z", "y"))
    group = 2 * x + core

    mine = rhs_t.astype(BF)
    target = partner[0]
    other = other_core(partner)[0]
    near = [mine] + [shift(mine, "x", d) for d in (1, 2, 3)]
    here = pick(near, target, group)
    across = other_core(pick(near, other, group))
    held = jnp.where((target & 1) == (group & 1), here, across)
    order = jnp.arange(OWNERS, dtype=jnp.int32)
    place = relative(order, z, y)
    live = (jnp.arange(EDGES, dtype=jnp.int32) < edge_count[0, 0]).astype(jnp.int32)
    pos_key = (relative(edge_rhs[0, 0] >> 8, z, y) << 27) | ((edge_rhs[0, 0] & (LOCAL - 1)) << 19)
    pos_key = pos_key | (edge_rel[0, 0] << 9) | (edge_lhs[0, 0] << 1) | live
    neg_key = (relative(neg_rhs[0, 0] >> 8, z, y) << 8) | (neg_rhs[0, 0] & (LOCAL - 1))
    spare = jnp.full((EDGES - NEG,), 1 << 30, jnp.int32)
    keys = jnp.stack([pos_key, jnp.concatenate([neg_key, spare])])
    exact = jnp.concatenate([rhs_t, jnp.broadcast_to(rhs_accum, (8, LOCAL))], 0)
    exact, held, keys, place = lax.optimization_barrier((exact, held, keys, place))
    ext_all = lax.all_gather(exact, GRP, axis=0, tiled=False)
    halves = gather_rows(held[:, :PER], held[:, PER:])
    keys = lax.sort(keys, is_stable=False)
    left, weight, query = make_query(keys, lhs_t, rel_t)

    back, lhs_g, rel_g = edges(place, keys, halves, query, left, weight)
    returned = lax.all_to_all(back, ROW, 0, 0, tiled=True)
    own, other, lhs_sum = sums(keys, lhs_g, rel_g)
    pieces = spread("x", [own.reshape(64, 32, PER), other_core(other).reshape(64, 32, PER)])
    total = add_four([pieces[0]] + [shift(pieces[d], "x", d) for d in (1, 2, 3)])
    for axis in ("z", "y"):
        total = add_four([total] + [shift(total, axis, d) for d in (1, 2, 3)])
    own = jnp.stack([total] + [shift(total, "x", d) for d in (1, 2, 3)]).reshape(4, 512, PER)

    new_lhs, new_lhs_accum = left_update(lhs_t, lhs_accum, lhs_sum)
    new_rhs, new_rhs_accum = right_update(partner, ext_all, returned)
    own, new_rhs, new_lhs = lax.optimization_barrier((own, new_rhs, new_lhs))
    new_rel, new_rel_accum = relation_update(rel_t, rel_accum[None], own, other_core(own))
    return (
        new_lhs.T[None],
        new_lhs_accum,
        new_rhs.T[None],
        new_rhs_accum,
        new_rel.T,
        new_rel_accum[0],
    )


def solution(mesh):
    fine = jax.sharding.Mesh(mesh.devices.reshape(4, 2, 4, 4), ("x", "core", "z", "y"))
    rows = P(GRP, ROW, None)
    in_specs = (rows, P(GRP, ROW), rows, P(GRP, ROW), P(), P(), P(GRP), rows, rows, rows, P(GRP, ROW), rows)
    out_specs = (rows, P(GRP, ROW), rows, P(GRP, ROW), P(), P())
    return jax.shard_map(body, mesh=fine, in_specs=in_specs, out_specs=out_specs, check_vma=False)
```

time: 188 us -> 169 us (0.90)
  blocking collectives: 20.1 us -> 0 us
  starting transfers between devices: 44.1 us -> 60.7 us
  waiting for transfers between devices: 41.4 us -> 34 us
  Pallas kernels: 48.9 us -> 41.6 us
  local copies, waits for them, and re-layouts: 7.99 us -> 6.1 us
    all_to_all x1 -> x0, blocking collectives: 20.1 us -> none  [body(): lax.all_to_all(rel_sum.reshape(64, 32, PER), CHIPS, 0, 0, tiled=True)]
    ppermute x15 -> x27, starting transfers between devices: 22.1 us -> 41.5 us  [shift(): return lax.ppermute(value, axis, [(i, i + distance & 3) for i in range(4)])]
    all_to_all x1, waiting for transfers between devices: 19.3 us -> 0.01 us  [body(): returned = lax.all_to_all(back, ROW, 0, 0, tiled=True)]
    ppermute x15 -> x27, waiting for transfers between devices: 13.2 us -> 29.7 us  [shift(): return lax.ppermute(value, axis, [(i, i + distance & 3) for i in range(4)])]
    pallas_call x5, Pallas kernels: 44.5 us -> 37.2 us  [the longest x1 17.4 us: edges(): pl.pallas_call(edge_kernel, in_specs=[pl.BlockSpec(memory_space=pltpu.SME...]
    all_to_all x1 -> x0, waiting for transfers between devices: 6.39 us -> none  [body(): lax.all_to_all(total_for_all(parts), CHIPS, 0, 0, tiled=True)]
    all_to_all x1 -> x0, starting transfers between devices: 4.95 us -> none  [body(): lax.all_to_all(total_for_all(parts), CHIPS, 0, 0, tiled=True)]
    ppermute x4, starting transfers between devices: 8.87 us -> 10.8 us  [other_core(): return lax.ppermute(value, 'core', CORES)]
  transfers between devices with their start and end apart: 22 -> 33, of which waited for: 12 -> 17; matrix products, arithmetic and copies ran while one was open for 5% -> 4% of each run, Pallas kernels for 24% -> 21%
where the time goes in v3:
time: 169 us; the launch traced here: 168 us
  starting transfers between devices  60.7 us (36%)
  Pallas kernels  41.6 us (25%)
  waiting for transfers between devices  34 us (20%)
  between operations  17.7 us (10%)
  other arithmetic  7.81 us (5%)
  local copies, waits for them, and re-layouts  6.1 us (4%)
    ppermute x27, starting transfers between devices, shift(): return lax.ppermute(value, axis, [(i, i + distance & 3) for i in range(4)])  41.5 us
    ppermute x27, waiting for transfers between devices, shift(): return lax.ppermute(value, axis, [(i, i + distance & 3) for i in range(4)])  29.7 us
    pallas_call x1, Pallas kernels, edges(): pl.pallas_call(edge_kernel, in_specs=[pl.BlockSpec(memory_space=pltpu.SME...  17.4 us
    ppermute x4, starting transfers between devices, other_core(): return lax.ppermute(value, 'core', CORES)  10.8 us
    pallas_call x1, Pallas kernels, make_query(): pl.pallas_call(query_kernel, grid=(STEPS,), in_specs=[pl.BlockSpec((2, CH...  8.58 us
    all_to_all x1, starting transfers between devices, body(): returned = lax.all_to_all(back, ROW, 0, 0, tiled=True)  8.34 us
    pallas_call x1, Pallas kernels, sums(): pl.pallas_call(sums_kernel, out_shape=[jax.ShapeDtypeStruct((4, 512, PER)...  5.81 us
    unnamed x29, local copies, waits for them, and re-layouts  5.36 us
  transfers between devices with their start and end apart: 33, of which 17 were waited for; matrix products, arithmetic and copies ran while one was open for 4% of the time, Pallas kernels for 21%

profile of v3, /device:TPU:1, one launch (start us, length us, event | category | flops | bytes accessed | tf_op | source)
XLA Modules:
  0.0 167.8 jit_solution(18359953606940291167)
XLA Ops:
  8.1 1.1 bitcast_convert_fusion
  9.1 2.1 %collective-permute-start = (bf16[400,256]{1,0:T(8,128)(2,1)S(1)}, bf16[400,256]{1,0:T(8,128)(2,1)S(1)}, u32[]{:S(2)}, u32[]{:S(2)}) collective-permute-start(bf16[400,256]{1,0:T(8,128)(2,1)S(1)} %bitcast_convert_fusion), channel_id=1, source_target_pairs={{0,32},{32,64},{64,96},{96,0},{1,33},{33,65},{65,97},{97,1},{2,34}... | collective-permute-start | bytes 614408 | tf_op jit(solution)/shard_map/ppermute | solution.py:406
  11.2 2.5 %collective-permute-start.1 = (bf16[400,256]{1,0:T(8,128)(2,1)S(1)}, bf16[400,256]{1,0:T(8,128)(2,1)S(1)}, u32[]{:S(2)}, u32[]{:S(2)}) collective-permute-start(bf16[400,256]{1,0:T(8,128)(2,1)S(1)} %bitcast_convert_fusion), channel_id=1, source_target_pairs={{0,64},{32,96},{64,0},{96,32},{1,65},{33,97},{65,1},{97,33},{2,66}... | collective-permute-start | bytes 614408 | tf_op jit(solution)/shard_map/ppermute | solution.py:406
  13.7 1.2 collective-permute-start.2
  14.8 1.5 collective-permute-start.3
  17.7 0.7 shift-left_or_fusion
  18.4 0.8 fusion
  19.2 0.5 and_or_fusion.place_ref
  19.7 0.7 broadcast_in_dim.18
  20.4 1.8 %pad_maximum_fusion.1 = f32[408,256]{1,0:T(8,128)} fusion(f32[8,256]{1,0:T(8,128)S(1)} %broadcast_in_dim.18, f32[400,256]{1,0:T(8,128)} %bitcast.47), kind=kLoop, calls=%fused_computation.1 | loop fusion | flops 104448 | bytes 835584 | tf_op jit(solution)/shard_map/concatenate | solution.py:465
  22.9 1.3 collective-permute-start.4
  24.2 0.6 pad_add_fusion
  24.9 0.5 collective-permute-done.4
  25.5 0.5 all-gather.3.cloned.1.call-update
  26.0 3.8 %collective-permute-start.10 = (bf16[400,128]{1,0:T(8,128)(2,1)S(1)}, bf16[400,128]{1,0:T(8,128)(2,1)S(1)}, u32[]{:S(2)}, u32[]{:S(2)}) collective-permute-start(bf16[400,128]{1,0:T(8,128)(2,1)S(1)} %get-tuple-element.47), channel_id=1, source_target_pairs={{0,12},{4,0},{8,4},{12,8},{1,13},{5,1},{9,5},{13,9},{2,14},{6,2},{... | collective-permute-start | bytes 307208 | tf_op jit(solution)/shard_map/ppermute | solution.py:406
  29.9 2.9 %collective-permute-start.5 = (bf16[400,128]{1,0:T(8,128)(2,1)S(1)}, bf16[400,128]{1,0:T(8,128)(2,1)S(1)}, u32[]{:S(2)}, u32[]{:S(2)}) collective-permute-start(bf16[400,128]{1,0:T(8,128)(2,1)S(1)} %get-tuple-element.43), channel_id=1, source_target_pairs={{0,2},{1,3},{2,0},{3,1},{4,6},{5,7},{6,4},{7,5},{8,10},{9,11},{10,... | collective-permute-start | bytes 307208 | tf_op jit(solution)/shard_map/ppermute | solution.py:406
  32.8 0.4 collective-permute-start.6
  33.2 2.3 %collective-permute-start.7 = (bf16[400,128]{1,0:T(8,128)(2,1)S(1)}, bf16[400,128]{1,0:T(8,128)(2,1)S(1)}, u32[]{:S(2)}, u32[]{:S(2)}) collective-permute-start(bf16[400,128]{1,0:T(8,128)(2,1)S(1)} %get-tuple-element.43), channel_id=1, source_target_pairs={{0,3},{1,0},{2,1},{3,2},{4,7},{5,4},{6,5},{7,6},{8,11},{9,8},{10,9... | collective-permute-start | bytes 307208 | tf_op jit(solution)/shard_map/ppermute | solution.py:406
  35.5 0.7 collective-permute-start.9
  36.2 1.3 collective-permute-done.6
  37.8 2.8 %collective-permute-done.8 = bf16[400,128]{1,0:T(8,128)(2,1)S(1)} collective-permute-done((bf16[400,128]{1,0:T(8,128)(2,1)S(1)}, bf16[400,128]{1,0:T(8,128)(2,1)S(1)}, u32[]{:S(2)}, u32[]{:S(2)}) %collective-permute-start.8) | collective-permute-done | bytes 102432 | tf_op jit(solution)/shard_map/ppermute | solution.py:406
  40.6 1.2 collective-permute-done.9
  42.0 2.6 %collective-permute-start.15 = (bf16[4,400,128]{2,1,0:T(8,128)(2,1)S(1)}, bf16[4,400,128]{2,1,0:T(8,128)(2,1)S(1)}, u32[]{:S(2)}, u32[]{:S(2)}) collective-permute-start(bf16[4,400,128]{2,1,0:T(8,128)(2,1)S(1)} %pad_maximum_fusion.3.b0), channel_id=1, source_target_pairs={{0,2},{1,3},{2,0},{3,1},{4,6},{5,7},{6,4},{7,5},{8,10},{9,11},{10,... | collective-permute-start | bytes 1228808 | tf_op jit(solution)/shard_map/ppermute | solution.py:406
  44.5 0.8 collective-permute-start.16
  45.4 1.1 collective-permute-start.12
  46.5 5.3 %collective-permute-done.14.b1 = bf16[4,400,128]{2,1,0:T(8,128)(2,1)S(1)} collective-permute-done((bf16[4,400,128]{2,1,0:T(8,128)(2,1)S(1)}, bf16[4,400,128]{2,1,0:T(8,128)(2,1)S(1)}, u32[]{:S(2)}, u32[]{:S(2)}) %collective-permute-start.14) | collective-permute-done | bytes 409632 | tf_op jit(solution)/shard_map/ppermute | solution.py:406
  51.9 1.8 %collective-permute-start.13 = (bf16[4,400,128]{2,1,0:T(8,128)(2,1)S(1)}, bf16[4,400,128]{2,1,0:T(8,128)(2,1)S(1)}, u32[]{:S(2)}, u32[]{:S(2)}) collective-permute-start(bf16[4,400,128]{2,1,0:T(8,128)(2,1)S(1)} %pad_maximum_fusion.2.a0), channel_id=1, source_target_pairs={{0,12},{4,0},{8,4},{12,8},{1,13},{5,1},{9,5},{13,9},{2,14},{6,2},{... | collective-permute-start | bytes 1228808 | tf_op jit(solution)/shard_map/ppermute | solution.py:406
  53.6 8.6 %make_query.1 = (bf16[416,2048]{1,0:T(8,128)(2,1)}, bf16[416,2048]{1,0:T(8,128)(2,1)}, bf16[400,2048]{1,0:T(8,128)(2,1)}) custom-call(s32[2,2048]{1,0:T(2,128)} %sort.9.cloned.1.call-done.keys_ref, f32[400,256]{1,0:T(8,128)} %bitcast.55, f32[400,1000]{1,0:T(8,128)} %bitcast.48), custom_call_target="tpu_custom_call" | custom-call | flops 5000000000 | bytes 10000000 | tf_op jit(solution)/shard_map/make_query/pallas_call | solution.py:85
  62.3 0.6 collective-permute-done.16.b3
  63.1 0.6 copy-done.10
  64.0 17.4 %edges.1 = (bf16[16,624,128]{2,1,0:T(8,128)(2,1)}, bf16[416,2048]{1,0:T(8,128)(2,1)}, bf16[416,2048]{1,0:T(8,128)(2,1)}) custom-call(s32[16]{0:T(128)} %and_or_fusion.place_ref, s32[2,2048]{1,0:T(2,128)} %sort.9.cloned.1.call-done.keys_ref, bf16[4,400,128]{2,1,0:T(8,128)(2,1)} %copy-done.6, bf16[4,400,128]{2,1,0:T(8,128)(2,1)} %copy-done.11, ...), custom_call_target="tpu_custom_call" | custom-call | flops 8000000000 | bytes 20000000 | tf_op jit(solution)/shard_map/edges/pallas_call | solution.py:232
  81.4 8.3 %all-to-all-start = ((bf16[16,624,128]{2,1,0:T(8,128)(2,1)}), bf16[16,624,128]{2,1,0:T(8,128)(2,1)S(1)}, u32[]{:S(2)}, u32[]{:S(2)}) async-start(bf16[16,624,128]{2,1,0:T(8,128)(2,1)} %get-tuple-element.63), calls=%async_computation | async-start | bytes 5111808 | tf_op jit(solution)/shard_map/all_to_all | solution.py:473
  89.8 5.8 %edge_sums.1 = (bf16[4,512,128]{2,1,0:T(8,128)(2,1)}, bf16[4,512,128]{2,1,0:T(8,128)(2,1)}, f32[400,256]{1,0:T(8,128)}) custom-call(s32[2,2048]{1,0:T(2,128)} %sort.9.cloned.1.call-done.keys_ref, bf16[416,2048]{1,0:T(8,128)(2,1)} %get-tuple-element.54.lhs_g, bf16[416,2048]{1,0:T(8,128)(2,1)} %get-tuple-element.55.rel_g), custom_call_target="tpu_custom_call" | custom-call | flops 3000000000 | bytes 6000000 | tf_op jit(solution)/shard_map/edge_sums/pallas_call | solution.py:285
  95.6 6.2 %collective-permute-start.17 = (bf16[4,512,128]{2,1,0:T(8,128)(2,1)}, bf16[4,512,128]{2,1,0:T(8,128)(2,1)S(1)}, u32[]{:S(2)}, u32[]{:S(2)}) collective-permute-start(bf16[4,512,128]{2,1,0:T(8,128)(2,1)} %get-tuple-element.57), channel_id=1, source_target_pairs={{0,16},{16,0},{1,17},{17,1},{2,18},{18,2},{3,19},{19,3},{4,20},{20... | collective-permute-start | bytes 1572872 | tf_op jit(solution)/shard_map/ppermute | solution.py:410
  101.7 1.7 %collective-permute-done.17 = bf16[4,512,128]{2,1,0:T(8,128)(2,1)S(1)} collective-permute-done((bf16[4,512,128]{2,1,0:T(8,128)(2,1)}, bf16[4,512,128]{2,1,0:T(8,128)(2,1)S(1)}, u32[]{:S(2)}, u32[]{:S(2)}) %collective-permute-start.17) | collective-permute-done | bytes 524320 | tf_op jit(solution)/shard_map/ppermute | solution.py:410
  103.5 0.8 copy-done.3
  104.3 2.0 %spread.1 = (bf16[16,32,128]{2,1,0:T(8,128)(2,1)}, bf16[16,32,128]{2,1,0:T(8,128)(2,1)}, bf16[16,32,128]{2,1,0:T(8,128)(2,1)}, bf16[16,32,128]{2,1,0:T(8,128)(2,1)}) custom-call(bf16[64,32,128]{2,1,0:T(8,128)(2,1)} %bitcast.50, bf16[64,32,128]{2,1,0:T(8,128)(2,1)} %bitcast.51), custom_call_target="tpu_custom_call" | custom-call | tf_op jit(solution)/shard_map/spread/pallas_call | solution.py:312
  106.3 2.4 %collective-permute-start.18 = (bf16[16,32,128]{2,1,0:T(8,128)(2,1)}, bf16[16,32,128]{2,1,0:T(8,128)(2,1)S(1)}, u32[]{:S(2)}, u32[]{:S(2)}) collective-permute-start(bf16[16,32,128]{2,1,0:T(8,128)(2,1)} %get-tuple-element.59), channel_id=1, source_target_pairs={{0,64},{32,96},{64,0},{96,32},{1,65},{33,97},{65,1},{97,33},{2,66}... | collective-permute-start | bytes 393224 | tf_op jit(solution)/shard_map/ppermute | solution.py:406
  108.9 2.5 %collective-permute-start.20 = (bf16[16,32,128]{2,1,0:T(8,128)(2,1)}, bf16[16,32,128]{2,1,0:T(8,128)(2,1)S(1)}, u32[]{:S(2)}, u32[]{:S(2)}) collective-permute-start(bf16[16,32,128]{2,1,0:T(8,128)(2,1)} %get-tuple-element.61), channel_id=1, source_target_pairs={{0,96},{32,0},{64,32},{96,64},{1,97},{33,1},{65,33},{97,65},{2,98}... | collective-permute-start | bytes 393224 | tf_op jit(solution)/shard_map/ppermute | solution.py:406
  111.4 1.4 collective-permute-done.18
  112.8 3.1 %collective-permute-done.19 = bf16[16,32,128]{2,1,0:T(8,128)(2,1)S(1)} collective-permute-done((bf16[16,32,128]{2,1,0:T(8,128)(2,1)}, bf16[16,32,128]{2,1,0:T(8,128)(2,1)S(1)}, u32[]{:S(2)}, u32[]{:S(2)}) %collective-permute-start.19) | collective-permute-done | bytes 131104 | tf_op jit(solution)/shard_map/ppermute | solution.py:406
  115.8 1.0 add_convert_fusion.2
  116.8 2.9 %collective-permute-start.21 = (bf16[16,32,128]{2,1,0:T(8,128)(2,1)S(1)}, bf16[16,32,128]{2,1,0:T(8,128)(2,1)S(1)}, u32[]{:S(2)}, u32[]{:S(2)}) collective-permute-start(bf16[16,32,128]{2,1,0:T(8,128)(2,1)S(1)} %add_convert_fusion.2), channel_id=1, source_target_pairs={{0,8},{4,12},{8,0},{12,4},{1,9},{5,13},{9,1},{13,5},{2,10},{6,14},... | collective-permute-start | bytes 393224 | tf_op jit(solution)/shard_map/ppermute | solution.py:406
  120.1 2.4 %collective-permute-start.23 = (bf16[16,32,128]{2,1,0:T(8,128)(2,1)S(1)}, bf16[16,32,128]{2,1,0:T(8,128)(2,1)S(1)}, u32[]{:S(2)}, u32[]{:S(2)}) collective-permute-start(bf16[16,32,128]{2,1,0:T(8,128)(2,1)S(1)} %add_convert_fusion.2), channel_id=1, source_target_pairs={{0,12},{4,0},{8,4},{12,8},{1,13},{5,1},{9,5},{13,9},{2,14},{6,2},{... | collective-permute-start | bytes 393224 | tf_op jit(solution)/shard_map/ppermute | solution.py:406
  122.4 5.6 %collective-permute-done.22 = bf16[16,32,128]{2,1,0:T(8,128)(2,1)S(1)} collective-permute-done((bf16[16,32,128]{2,1,0:T(8,128)(2,1)S(1)}, bf16[16,32,128]{2,1,0:T(8,128)(2,1)S(1)}, u32[]{:S(2)}, u32[]{:S(2)}) %collective-permute-start.22) | collective-permute-done | bytes 131104 | tf_op jit(solution)/shard_map/ppermute | solution.py:406
  128.2 1.2 collective-permute-start.24
  129.3 0.8 collective-permute-start.25
  130.1 2.3 %collective-permute-start.26 = (bf16[16,32,128]{2,1,0:T(8,128)(2,1)S(1)}, bf16[16,32,128]{2,1,0:T(8,128)(2,1)S(1)}, u32[]{:S(2)}, u32[]{:S(2)}) collective-permute-start(bf16[16,32,128]{2,1,0:T(8,128)(2,1)S(1)} %add_convert_fusion.1), channel_id=1, source_target_pairs={{0,3},{1,0},{2,1},{3,2},{4,7},{5,4},{6,5},{7,6},{8,11},{9,8},{10,9... | collective-permute-start | bytes 393224 | tf_op jit(solution)/shard_map/ppermute | solution.py:406
  132.5 1.1 collective-permute-done.24
  133.6 4.0 %collective-permute-done.25 = bf16[16,32,128]{2,1,0:T(8,128)(2,1)S(1)} collective-permute-done((bf16[16,32,128]{2,1,0:T(8,128)(2,1)S(1)}, bf16[16,32,128]{2,1,0:T(8,128)(2,1)S(1)}, u32[]{:S(2)}, u32[]{:S(2)}) %collective-permute-start.25) | collective-permute-done | bytes 131104 | tf_op jit(solution)/shard_map/ppermute | solution.py:406
  137.7 1.9 %collective-permute-start.27 = (bf16[16,32,128]{2,1,0:T(8,128)(2,1)S(1)}, bf16[16,32,128]{2,1,0:T(8,128)(2,1)S(1)}, u32[]{:S(2)}, u32[]{:S(2)}) collective-permute-start(bf16[16,32,128]{2,1,0:T(8,128)(2,1)S(1)} %add_convert_fusion), channel_id=1, source_target_pairs={{0,32},{32,64},{64,96},{96,0},{1,33},{33,65},{65,97},{97,1},{2,34}... | collective-permute-start | bytes 393224 | tf_op jit(solution)/shard_map/ppermute | solution.py:406
  139.5 1.6 collective-permute-start.28
  141.1 0.9 collective-permute-start.29
  142.0 2.0 %left_update.1 = (f32[400,256]{1,0:T(8,128)}, f32[1,256]{1,0:T(1,128)}) custom-call(f32[400,256]{1,0:T(8,128)} %bitcast.56, f32[1,256]{1,0:T(1,128)} %accum_ref.1, f32[400,256]{1,0:T(8,128)} %get-tuple-element.65.grad_ref), custom_call_target="tpu_custom_call" | custom-call | tf_op jit(solution)/shard_map/left_update/pallas_call | solution.py:376
  144.0 2.3 %collective-permute-done.28 = bf16[16,32,128]{2,1,0:T(8,128)(2,1)S(1)} collective-permute-done((bf16[16,32,128]{2,1,0:T(8,128)(2,1)S(1)}, bf16[16,32,128]{2,1,0:T(8,128)(2,1)S(1)}, u32[]{:S(2)}, u32[]{:S(2)}) %collective-permute-start.28) | collective-permute-done | bytes 131104 | tf_op jit(solution)/shard_map/ppermute | solution.py:406
  146.3 0.4 collective-permute-done.29
  146.7 0.7 copy-done.7
  147.3 1.0 pad_maximum_fusion.own_ref
  148.4 2.1 %copy-done = f32[3264,256]{1,0:T(8,128)S(1)} copy-done((f32[3264,256]{1,0:T(8,128)S(1)}, f32[3264,256]{1,0:T(8,128)}, u32[]{:S(2)}) %copy-start) | copy-done | bytes 3342360
  150.4 2.4 %right_update.1 = (f32[400,256]{1,0:T(8,128)}, f32[1,256]{1,0:T(1,128)}) custom-call(s32[1]{0:T(128)S(6)} %copy.18.partner_ref, f32[8,408,256]{2,1,0:T(8,128)S(1)} %bitcast.46, bf16[16,624,128]{2,1,0:T(8,128)(2,1)S(1)} %all-to-all-done.back_ref), custom_call_target="tpu_custom_call" | custom-call | flops 2000000000 | bytes 5000000 | tf_op jit(solution)/shard_map/right_update/pallas_call | solution.py:346
  152.8 1.8 %collective-permute-start.30 = (bf16[4,512,128]{2,1,0:T(8,128)(2,1)S(1)}, bf16[4,512,128]{2,1,0:T(8,128)(2,1)S(1)}, u32[]{:S(2)}, u32[]{:S(2)}) collective-permute-start(bf16[4,512,128]{2,1,0:T(8,128)(2,1)S(1)} %pad_maximum_fusion.own_ref), channel_id=1, source_target_pairs={{0,16},{16,0},{1,17},{17,1},{2,18},{18,2},{3,19},{19,3},{4,20},{20... | collective-permute-start | bytes 1572872 | tf_op jit(solution)/shard_map/ppermute | solution.py:410
  154.6 1.5 collective-permute-done.30.other_ref
  156.1 0.8 copy-done.4
  156.9 3.4 %relation_update.1 = (f32[400,1000]{1,0:T(8,128)}, f32[1,1000]{1,0:T(1,128)}) custom-call(f32[400,1000]{1,0:T(8,128)} %bitcast.49, f32[1,1000]{1,0:T(1,128)} %bitcast.68, bf16[4,512,128]{2,1,0:T(8,128)(2,1)} %copy-done.2, bf16[4,512,128]{2,1,0:T(8,128)(2,1)} %copy-done.4), custom_call_target="tpu_custom_call" | custom-call | tf_op jit(solution)/shard_map/relation_update/pallas_call | solution.py:394
  (58 shorter events, 2.2 us)
Async XLA Ops:
  8.0 14.9 %copy-start.1 = (f32[1,256,400]{1,2,0:T(8,128)S(1)}, f32[1,256,400]{1,2,0:T(8,128)}, u32[]{:S(2)}) copy-start(f32[1,256,400]{1,2,0:T(8,128)} %param.14) | copy-start | bytes 1228804
  8.0 45.6 %sort.9.cloned.1.call-start = ((), (), s32[]{:S(2)}) async-start(), calls=%async_computation.2 | async-start | bytes 49184 | tf_op jit(solution)/shard_map/sort | solution.py:469
  9.1 13.7 %collective-permute-start = (bf16[400,256]{1,0:T(8,128)(2,1)S(1)}, bf16[400,256]{1,0:T(8,128)(2,1)S(1)}, u32[]{:S(2)}, u32[]{:S(2)}) collective-permute-start(bf16[400,256]{1,0:T(8,128)(2,1)S(1)} %bitcast_convert_fusion), channel_id=1, source_target_pairs={{0,32},{32,64},{64,96},{96,0},{1,33},{33,65},{65,97},{97,1},{2,34}... | collective-permute-start | bytes 614408 | tf_op jit(solution)/shard_map/ppermute | solution.py:406
  11.2 11.6 %collective-permute-start.1 = (bf16[400,256]{1,0:T(8,128)(2,1)S(1)}, bf16[400,256]{1,0:T(8,128)(2,1)S(1)}, u32[]{:S(2)}, u32[]{:S(2)}) collective-permute-start(bf16[400,256]{1,0:T(8,128)(2,1)S(1)} %bitcast_convert_fusion), channel_id=1, source_target_pairs={{0,64},{32,96},{64,0},{96,32},{1,65},{33,97},{65,1},{97,33},{2,66}... | collective-permute-start | bytes 614408 | tf_op jit(solution)/shard_map/ppermute | solution.py:406
  13.7 9.2 %collective-permute-start.2 = (bf16[400,256]{1,0:T(8,128)(2,1)S(1)}, bf16[400,256]{1,0:T(8,128)(2,1)S(1)}, u32[]{:S(2)}, u32[]{:S(2)}) collective-permute-start(bf16[400,256]{1,0:T(8,128)(2,1)S(1)} %bitcast_convert_fusion), channel_id=1, source_target_pairs={{0,96},{32,0},{64,32},{96,64},{1,97},{33,1},{65,33},{97,65},{2,98}... | collective-permute-start | bytes 614408 | tf_op jit(solution)/shard_map/ppermute | solution.py:406
  14.8 7.3 %collective-permute-start.3 = (s32[1]{0:T(128)}, s32[1]{0:T(128)}, u32[]{:S(2)}, u32[]{:S(2)}) collective-permute-start(s32[1]{0:T(128)} %param.18), channel_id=1, source_target_pairs={{0,16},{16,0},{1,17},{17,1},{2,18},{18,2},{3,19},{19,3},{4,20},{20... | collective-permute-start | bytes 20 | tf_op jit(solution)/shard_map/ppermute | solution.py:410
  22.9 2.4 %collective-permute-start.4 = (bf16[400,256]{1,0:T(8,128)(2,1)S(1)}, bf16[400,256]{1,0:T(8,128)(2,1)S(1)}, u32[]{:S(2)}, u32[]{:S(2)}) collective-permute-start(bf16[400,256]{1,0:T(8,128)(2,1)S(1)} %select_select_fusion), channel_id=1, source_target_pairs={{0,16},{16,0},{1,17},{17,1},{2,18},{18,2},{3,19},{19,3},{4,20},{20... | collective-permute-start | bytes 614408 | tf_op jit(solution)/shard_map/ppermute | solution.py:410
  25.4 122.9 %all-gather.3.cloned.1.call-start = ((), (), s32[]{:S(2)}) async-start(), calls=%async_computation.1 | async-start | bytes 3760128 | tf_op jit(solution)/shard_map/all_gather | solution.py:467
  26.0 9.4 %collective-permute-start.10 = (bf16[400,128]{1,0:T(8,128)(2,1)S(1)}, bf16[400,128]{1,0:T(8,128)(2,1)S(1)}, u32[]{:S(2)}, u32[]{:S(2)}) collective-permute-start(bf16[400,128]{1,0:T(8,128)(2,1)S(1)} %get-tuple-element.47), channel_id=1, source_target_pairs={{0,12},{4,0},{8,4},{12,8},{1,13},{5,1},{9,5},{13,9},{2,14},{6,2},{... | collective-permute-start | bytes 307208 | tf_op jit(solution)/shard_map/ppermute | solution.py:406
  29.9 6.3 %collective-permute-start.5 = (bf16[400,128]{1,0:T(8,128)(2,1)S(1)}, bf16[400,128]{1,0:T(8,128)(2,1)S(1)}, u32[]{:S(2)}, u32[]{:S(2)}) collective-permute-start(bf16[400,128]{1,0:T(8,128)(2,1)S(1)} %get-tuple-element.43), channel_id=1, source_target_pairs={{0,2},{1,3},{2,0},{3,1},{4,6},{5,7},{6,4},{7,5},{8,10},{9,11},{10,... | collective-permute-start | bytes 307208 | tf_op jit(solution)/shard_map/ppermute | solution.py:406
  32.8 4.7 %collective-permute-start.6 = (bf16[400,128]{1,0:T(8,128)(2,1)S(1)}, bf16[400,128]{1,0:T(8,128)(2,1)S(1)}, u32[]{:S(2)}, u32[]{:S(2)}) collective-permute-start(bf16[400,128]{1,0:T(8,128)(2,1)S(1)} %get-tuple-element.43), channel_id=1, source_target_pairs={{0,1},{1,2},{2,3},{3,0},{4,5},{5,6},{6,7},{7,4},{8,9},{9,10},{10,1... | collective-permute-start | bytes 307208 | tf_op jit(solution)/shard_map/ppermute | solution.py:406
  33.2 4.6 %collective-permute-start.7 = (bf16[400,128]{1,0:T(8,128)(2,1)S(1)}, bf16[400,128]{1,0:T(8,128)(2,1)S(1)}, u32[]{:S(2)}, u32[]{:S(2)}) collective-permute-start(bf16[400,128]{1,0:T(8,128)(2,1)S(1)} %get-tuple-element.43), channel_id=1, source_target_pairs={{0,3},{1,0},{2,1},{3,2},{4,7},{5,4},{6,5},{7,6},{8,11},{9,8},{10,9... | collective-permute-start | bytes 307208 | tf_op jit(solution)/shard_map/ppermute | solution.py:406
  35.5 5.1 %collective-permute-start.8 = (bf16[400,128]{1,0:T(8,128)(2,1)S(1)}, bf16[400,128]{1,0:T(8,128)(2,1)S(1)}, u32[]{:S(2)}, u32[]{:S(2)}) collective-permute-start(bf16[400,128]{1,0:T(8,128)(2,1)S(1)} %get-tuple-element.47), channel_id=1, source_target_pairs={{0,8},{4,12},{8,0},{12,4},{1,9},{5,13},{9,1},{13,5},{2,10},{6,14},... | collective-permute-start | bytes 307208 | tf_op jit(solution)/shard_map/ppermute | solution.py:406
  35.5 6.4 %collective-permute-start.9 = (bf16[400,128]{1,0:T(8,128)(2,1)S(1)}, bf16[400,128]{1,0:T(8,128)(2,1)S(1)}, u32[]{:S(2)}, u32[]{:S(2)}) collective-permute-start(bf16[400,128]{1,0:T(8,128)(2,1)S(1)} %get-tuple-element.47), channel_id=1, source_target_pairs={{0,4},{4,8},{8,12},{12,0},{1,5},{5,9},{9,13},{13,1},{2,6},{6,10},{... | collective-permute-start | bytes 307208 | tf_op jit(solution)/shard_map/ppermute | solution.py:406
  41.9 20.4 %copy-start.5 = (bf16[4,400,128]{2,1,0:T(8,128)(2,1)}, bf16[4,400,128]{2,1,0:T(8,128)(2,1)S(1)}, u32[]{:S(2)}) copy-start(bf16[4,400,128]{2,1,0:T(8,128)(2,1)S(1)} %pad_maximum_fusion.3.b0) | copy-start | bytes 1228804
  41.9 10.0 %collective-permute-start.14 = (bf16[4,400,128]{2,1,0:T(8,128)(2,1)S(1)}, bf16[4,400,128]{2,1,0:T(8,128)(2,1)S(1)}, u32[]{:S(2)}, u32[]{:S(2)}) collective-permute-start(bf16[4,400,128]{2,1,0:T(8,128)(2,1)S(1)} %pad_maximum_fusion.3.b0), channel_id=1, source_target_pairs={{0,1},{1,2},{2,3},{3,0},{4,5},{5,6},{6,7},{7,4},{8,9},{9,10},{10,1... | collective-permute-start | bytes 1228808 | tf_op jit(solution)/shard_map/ppermute | solution.py:406
  42.0 20.3 %collective-permute-start.15 = (bf16[4,400,128]{2,1,0:T(8,128)(2,1)S(1)}, bf16[4,400,128]{2,1,0:T(8,128)(2,1)S(1)}, u32[]{:S(2)}, u32[]{:S(2)}) collective-permute-start(bf16[4,400,128]{2,1,0:T(8,128)(2,1)S(1)} %pad_maximum_fusion.3.b0), channel_id=1, source_target_pairs={{0,2},{1,3},{2,0},{3,1},{4,6},{5,7},{6,4},{7,5},{8,10},{9,11},{10,... | collective-permute-start | bytes 1228808 | tf_op jit(solution)/shard_map/ppermute | solution.py:406
  44.5 18.4 %collective-permute-start.16 = (bf16[4,400,128]{2,1,0:T(8,128)(2,1)S(1)}, bf16[4,400,128]{2,1,0:T(8,128)(2,1)S(1)}, u32[]{:S(2)}, u32[]{:S(2)}) collective-permute-start(bf16[4,400,128]{2,1,0:T(8,128)(2,1)S(1)} %pad_maximum_fusion.3.b0), channel_id=1, source_target_pairs={{0,3},{1,0},{2,1},{3,2},{4,7},{5,4},{6,5},{7,6},{8,11},{9,8},{10,9... | collective-permute-start | bytes 1228808 | tf_op jit(solution)/shard_map/ppermute | solution.py:406
  45.3 16.9 %copy-start.6 = (bf16[4,400,128]{2,1,0:T(8,128)(2,1)}, bf16[4,400,128]{2,1,0:T(8,128)(2,1)S(1)}, u32[]{:S(2)}) copy-start(bf16[4,400,128]{2,1,0:T(8,128)(2,1)S(1)} %pad_maximum_fusion.2.a0) | copy-start | bytes 1228804
  45.4 17.5 %collective-permute-start.11 = (bf16[4,400,128]{2,1,0:T(8,128)(2,1)S(1)}, bf16[4,400,128]{2,1,0:T(8,128)(2,1)S(1)}, u32[]{:S(2)}, u32[]{:S(2)}) collective-permute-start(bf16[4,400,128]{2,1,0:T(8,128)(2,1)S(1)} %pad_maximum_fusion.2.a0), channel_id=1, source_target_pairs={{0,4},{4,8},{8,12},{12,0},{1,5},{5,9},{9,13},{13,1},{2,6},{6,10},{... | collective-permute-start | bytes 1228808 | tf_op jit(solution)/shard_map/ppermute | solution.py:406
  45.4 17.5 %collective-permute-start.12 = (bf16[4,400,128]{2,1,0:T(8,128)(2,1)S(1)}, bf16[4,400,128]{2,1,0:T(8,128)(2,1)S(1)}, u32[]{:S(2)}, u32[]{:S(2)}) collective-permute-start(bf16[4,400,128]{2,1,0:T(8,128)(2,1)S(1)} %pad_maximum_fusion.2.a0), channel_id=1, source_target_pairs={{0,8},{4,12},{8,0},{12,4},{1,9},{5,13},{9,1},{13,5},{2,10},{6,14},... | collective-permute-start | bytes 1228808 | tf_op jit(solution)/shard_map/ppermute | solution.py:406
  51.9 10.4 %copy-start.8 = (bf16[4,400,128]{2,1,0:T(8,128)(2,1)}, bf16[4,400,128]{2,1,0:T(8,128)(2,1)S(1)}, u32[]{:S(2)}) copy-start(bf16[4,400,128]{2,1,0:T(8,128)(2,1)S(1)} %collective-permute-done.14.b1) | copy-start | bytes 1228804
  51.9 11.2 %collective-permute-start.13 = (bf16[4,400,128]{2,1,0:T(8,128)(2,1)S(1)}, bf16[4,400,128]{2,1,0:T(8,128)(2,1)S(1)}, u32[]{:S(2)}, u32[]{:S(2)}) collective-permute-start(bf16[4,400,128]{2,1,0:T(8,128)(2,1)S(1)} %pad_maximum_fusion.2.a0), channel_id=1, source_target_pairs={{0,12},{4,0},{8,4},{12,8},{1,13},{5,1},{9,5},{13,9},{2,14},{6,2},{... | collective-permute-start | bytes 1228808 | tf_op jit(solution)/shard_map/ppermute | solution.py:406
  62.2 0.8 copy-start.9
  62.9 0.8 copy-start.10
  62.9 0.9 copy-start.11
  62.9 1.0 copy-start.12
  63.1 1.0 copy-start.13
  81.4 66.9 %all-to-all-start = ((bf16[16,624,128]{2,1,0:T(8,128)(2,1)}), bf16[16,624,128]{2,1,0:T(8,128)(2,1)S(1)}, u32[]{:S(2)}, u32[]{:S(2)}) async-start(bf16[16,624,128]{2,1,0:T(8,128)(2,1)} %get-tuple-element.63), calls=%async_computation | async-start | bytes 5111808 | tf_op jit(solution)/shard_map/all_to_all | solution.py:473
  95.6 7.9 %collective-permute-start.17 = (bf16[4,512,128]{2,1,0:T(8,128)(2,1)}, bf16[4,512,128]{2,1,0:T(8,128)(2,1)S(1)}, u32[]{:S(2)}, u32[]{:S(2)}) collective-permute-start(bf16[4,512,128]{2,1,0:T(8,128)(2,1)} %get-tuple-element.57), channel_id=1, source_target_pairs={{0,16},{16,0},{1,17},{17,1},{2,18},{18,2},{3,19},{19,3},{4,20},{20... | collective-permute-start | bytes 1572872 | tf_op jit(solution)/shard_map/ppermute | solution.py:410
  103.5 0.8 copy-start.3
  106.3 6.4 %collective-permute-start.18 = (bf16[16,32,128]{2,1,0:T(8,128)(2,1)}, bf16[16,32,128]{2,1,0:T(8,128)(2,1)S(1)}, u32[]{:S(2)}, u32[]{:S(2)}) collective-permute-start(bf16[16,32,128]{2,1,0:T(8,128)(2,1)} %get-tuple-element.59), channel_id=1, source_target_pairs={{0,64},{32,96},{64,0},{96,32},{1,65},{33,97},{65,1},{97,33},{2,66}... | collective-permute-start | bytes 393224 | tf_op jit(solution)/shard_map/ppermute | solution.py:406
  108.7 7.1 %collective-permute-start.19 = (bf16[16,32,128]{2,1,0:T(8,128)(2,1)}, bf16[16,32,128]{2,1,0:T(8,128)(2,1)S(1)}, u32[]{:S(2)}, u32[]{:S(2)}) collective-permute-start(bf16[16,32,128]{2,1,0:T(8,128)(2,1)} %get-tuple-element.60), channel_id=1, source_target_pairs={{0,32},{32,64},{64,96},{96,0},{1,33},{33,65},{65,97},{97,1},{2,34}... | collective-permute-start | bytes 393224 | tf_op jit(solution)/shard_map/ppermute | solution.py:406
  108.9 7.0 %collective-permute-start.20 = (bf16[16,32,128]{2,1,0:T(8,128)(2,1)}, bf16[16,32,128]{2,1,0:T(8,128)(2,1)S(1)}, u32[]{:S(2)}, u32[]{:S(2)}) collective-permute-start(bf16[16,32,128]{2,1,0:T(8,128)(2,1)} %get-tuple-element.61), channel_id=1, source_target_pairs={{0,96},{32,0},{64,32},{96,64},{1,97},{33,1},{65,33},{97,65},{2,98}... | collective-permute-start | bytes 393224 | tf_op jit(solution)/shard_map/ppermute | solution.py:406
  116.8 5.6 %collective-permute-start.21 = (bf16[16,32,128]{2,1,0:T(8,128)(2,1)S(1)}, bf16[16,32,128]{2,1,0:T(8,128)(2,1)S(1)}, u32[]{:S(2)}, u32[]{:S(2)}) collective-permute-start(bf16[16,32,128]{2,1,0:T(8,128)(2,1)S(1)} %add_convert_fusion.2), channel_id=1, source_target_pairs={{0,8},{4,12},{8,0},{12,4},{1,9},{5,13},{9,1},{13,5},{2,10},{6,14},... | collective-permute-start | bytes 393224 | tf_op jit(solution)/shard_map/ppermute | solution.py:406
  119.8 8.3 %collective-permute-start.22 = (bf16[16,32,128]{2,1,0:T(8,128)(2,1)S(1)}, bf16[16,32,128]{2,1,0:T(8,128)(2,1)S(1)}, u32[]{:S(2)}, u32[]{:S(2)}) collective-permute-start(bf16[16,32,128]{2,1,0:T(8,128)(2,1)S(1)} %add_convert_fusion.2), channel_id=1, source_target_pairs={{0,4},{4,8},{8,12},{12,0},{1,5},{5,9},{9,13},{13,1},{2,6},{6,10},{... | collective-permute-start | bytes 393224 | tf_op jit(solution)/shard_map/ppermute | solution.py:406
  120.1 8.0 %collective-permute-start.23 = (bf16[16,32,128]{2,1,0:T(8,128)(2,1)S(1)}, bf16[16,32,128]{2,1,0:T(8,128)(2,1)S(1)}, u32[]{:S(2)}, u32[]{:S(2)}) collective-permute-start(bf16[16,32,128]{2,1,0:T(8,128)(2,1)S(1)} %add_convert_fusion.2), channel_id=1, source_target_pairs={{0,12},{4,0},{8,4},{12,8},{1,13},{5,1},{9,5},{13,9},{2,14},{6,2},{... | collective-permute-start | bytes 393224 | tf_op jit(solution)/shard_map/ppermute | solution.py:406
  128.2 5.4 %collective-permute-start.24 = (bf16[16,32,128]{2,1,0:T(8,128)(2,1)S(1)}, bf16[16,32,128]{2,1,0:T(8,128)(2,1)S(1)}, u32[]{:S(2)}, u32[]{:S(2)}) collective-permute-start(bf16[16,32,128]{2,1,0:T(8,128)(2,1)S(1)} %add_convert_fusion.1), channel_id=1, source_target_pairs={{0,2},{1,3},{2,0},{3,1},{4,6},{5,7},{6,4},{7,5},{8,10},{9,11},{10,... | collective-permute-start | bytes 393224 | tf_op jit(solution)/shard_map/ppermute | solution.py:406
  129.3 8.3 %collective-permute-start.25 = (bf16[16,32,128]{2,1,0:T(8,128)(2,1)S(1)}, bf16[16,32,128]{2,1,0:T(8,128)(2,1)S(1)}, u32[]{:S(2)}, u32[]{:S(2)}) collective-permute-start(bf16[16,32,128]{2,1,0:T(8,128)(2,1)S(1)} %add_convert_fusion.1), channel_id=1, source_target_pairs={{0,1},{1,2},{2,3},{3,0},{4,5},{5,6},{6,7},{7,4},{8,9},{9,10},{10,1... | collective-permute-start | bytes 393224 | tf_op jit(solution)/shard_map/ppermute | solution.py:406
  130.1 7.4 %collective-permute-start.26 = (bf16[16,32,128]{2,1,0:T(8,128)(2,1)S(1)}, bf16[16,32,128]{2,1,0:T(8,128)(2,1)S(1)}, u32[]{:S(2)}, u32[]{:S(2)}) collective-permute-start(bf16[16,32,128]{2,1,0:T(8,128)(2,1)S(1)} %add_convert_fusion.1), channel_id=1, source_target_pairs={{0,3},{1,0},{2,1},{3,2},{4,7},{5,4},{6,5},{7,6},{8,11},{9,8},{10,9... | collective-permute-start | bytes 393224 | tf_op jit(solution)/shard_map/ppermute | solution.py:406
  137.7 6.4 %collective-permute-start.27 = (bf16[16,32,128]{2,1,0:T(8,128)(2,1)S(1)}, bf16[16,32,128]{2,1,0:T(8,128)(2,1)S(1)}, u32[]{:S(2)}, u32[]{:S(2)}) collective-permute-start(bf16[16,32,128]{2,1,0:T(8,128)(2,1)S(1)} %add_convert_fusion), channel_id=1, source_target_pairs={{0,32},{32,64},{64,96},{96,0},{1,33},{33,65},{65,97},{97,1},{2,34}... | collective-permute-start | bytes 393224 | tf_op jit(solution)/shard_map/ppermute | solution.py:406
  139.5 6.8 %collective-permute-start.28 = (bf16[16,32,128]{2,1,0:T(8,128)(2,1)S(1)}, bf16[16,32,128]{2,1,0:T(8,128)(2,1)S(1)}, u32[]{:S(2)}, u32[]{:S(2)}) collective-permute-start(bf16[16,32,128]{2,1,0:T(8,128)(2,1)S(1)} %add_convert_fusion), channel_id=1, source_target_pairs={{0,64},{32,96},{64,0},{96,32},{1,65},{33,97},{65,1},{97,33},{2,66}... | collective-permute-start | bytes 393224 | tf_op jit(solution)/shard_map/ppermute | solution.py:406
  141.1 5.5 %collective-permute-start.29 = (bf16[16,32,128]{2,1,0:T(8,128)(2,1)S(1)}, bf16[16,32,128]{2,1,0:T(8,128)(2,1)S(1)}, u32[]{:S(2)}, u32[]{:S(2)}) collective-permute-start(bf16[16,32,128]{2,1,0:T(8,128)(2,1)S(1)} %add_convert_fusion), channel_id=1, source_target_pairs={{0,96},{32,0},{64,32},{96,64},{1,97},{33,1},{65,33},{97,65},{2,98}... | collective-permute-start | bytes 393224 | tf_op jit(solution)/shard_map/ppermute | solution.py:406
  146.7 0.7 copy-start.7
  148.3 4.5 %copy-start.2 = (bf16[4,512,128]{2,1,0:T(8,128)(2,1)}, bf16[4,512,128]{2,1,0:T(8,128)(2,1)S(1)}, u32[]{:S(2)}) copy-start(bf16[4,512,128]{2,1,0:T(8,128)(2,1)S(1)} %pad_maximum_fusion.own_ref) | copy-start | bytes 1572868
  148.3 2.1 %copy-start = (f32[3264,256]{1,0:T(8,128)S(1)}, f32[3264,256]{1,0:T(8,128)}, u32[]{:S(2)}) copy-start(f32[3264,256]{1,0:T(8,128)} %all-gather.3.cloned.1.call-done) | copy-start | bytes 10027012
  152.8 3.3 %collective-permute-start.30 = (bf16[4,512,128]{2,1,0:T(8,128)(2,1)S(1)}, bf16[4,512,128]{2,1,0:T(8,128)(2,1)S(1)}, u32[]{:S(2)}, u32[]{:S(2)}) collective-permute-start(bf16[4,512,128]{2,1,0:T(8,128)(2,1)S(1)} %pad_maximum_fusion.own_ref), channel_id=1, source_target_pairs={{0,16},{16,0},{1,17},{17,1},{2,18},{18,2},{3,19},{19,3},{4,20},{20... | collective-permute-start | bytes 1572872 | tf_op jit(solution)/shard_map/ppermute | solution.py:410
  156.1 0.8 copy-start.4
Sparse Core Ops, SparseCore 0:
  25.6 7.6 sort.11.cloned.1.call-done
  (1 shorter events, 0.0 us)
Sparse Core Ops, SparseCore 1:
  27.7 30.5 all-gather.2

commit v4 on v3

--- a/solution.py
+++ b/solution.py
@@ -121,8 +121,8 @@
 
 
 def edge_kernel(
-    place_ref, keys_ref, a0, a1, a2, a3, b0, b1, b2, b3, q_hbm, l_hbm, w_hbm, back_hbm, lhs_hbm, rel_hbm,
-    table, neg_t, neg_n, weights, q_ref, l_ref, w_ref, back_ref, lhs_g, rel_g, scores, pos, grad, sems,
+    place_ref, keys_ref, a0, a1, a2, a3, b0, b1, b2, b3, q_hbm, l_hbm, w_hbm, back_hbm, own_hbm, other_hbm, lhs_ref,
+    table, neg_t, neg_n, weights, q_ref, l_ref, w_ref, back_ref, lhs_g, rel_g, scores, pos, grad, total_rel, own_ref, other_ref, sems,
 ):
     count = iter(range(COPIES))
 
@@ -207,7 +207,29 @@
                 out[r : r + e, own] = (ga * fa + gb * fb).astype(BF)
                 out[SECOND + r : SECOND + r + e, own] = (gb * fa - ga * fb).astype(BF)
 
-    stores = [move(back_ref.at[:, 0:D], back_hbm.at[:, 0:D]), move(rel_g, rel_hbm), move(lhs_g, lhs_hbm)]
+    stores = [move(back_ref.at[:, 0:D], back_hbm.at[:, 0:D])]
+    wide = 4 * PER
+    for c in range(0, EDGES, wide):
+        packed = keys_ref[0:1, c : c + wide]
+        marks = onehot(rel_of(packed), RELP)
+        for t in range(0, RELP, 2 * PER):
+            part = dot_t(rel_g[:, c : c + wide], marks[t : t + 2 * PER])
+            lanes = slice(t, t + 2 * PER)
+            total_rel[:, lanes] = part if c == 0 else total_rel[:, lanes] + part
+    own = pl.multiple_of(lax.axis_index("core") * (RELP // 2), RELP // 2)
+    other = pl.multiple_of((1 - lax.axis_index("core")) * (RELP // 2), RELP // 2)
+    for ref, start, hbm in ((other_ref, other, other_hbm), (own_ref, own, own_hbm)):
+        for at in range(4):
+            lanes = pl.ds(start + at * PER, PER)
+            both = jnp.concatenate([total_rel[0:HALF, lanes], total_rel[SECOND : SECOND + HALF, lanes]], 0)
+            ref[at, 0:D, :] = both.astype(BF)
+            ref[at, D:512, :] = jnp.zeros((512 - D, PER), BF)
+        stores.append(move(ref, hbm))
+    for c in range(0, EDGES, wide):
+        marks = onehot(lhs_of(keys_ref[0:1, c : c + wide]), LOCAL)
+        part = dot_t(lhs_g[:, c : c + wide], marks)
+        part = jnp.concatenate([part[:HALF], part[SECOND : SECOND + HALF]], 0)
+        lhs_ref[...] = part if c == 0 else lhs_ref[...] + part
     for c in range(0, STEPS, 2):
         part = dot_t(q_ref[...], weights[c * PER : (c + 2) * PER, :])
         for h in (0, 1):
@@ -232,11 +254,12 @@
     return pl.pallas_call(
         edge_kernel,
         in_specs=[pl.BlockSpec(memory_space=pltpu.SMEM), pl.BlockSpec(memory_space=pltpu.VMEM)] + [anywhere] * 11,
-        out_specs=[anywhere] * 3,
+        out_specs=[anywhere] * 3 + [pl.BlockSpec(memory_space=pltpu.VMEM)],
         out_shape=[
             jax.ShapeDtypeStruct((OWNERS, BACK, PER), BF),
-            jax.ShapeDtypeStruct((TALL, EDGES), BF),
-            jax.ShapeDtypeStruct((TALL, EDGES), BF),
+            jax.ShapeDtypeStruct((4, 512, PER), BF),
+            jax.ShapeDtypeStruct((4, 512, PER), BF),
+            jax.ShapeDtypeStruct((D, LOCAL), F32),
         ],
         scratch_shapes=[
             pltpu.VMEM((OWNERS, D, LOCAL), BF),
@@ -252,48 +275,15 @@
             pltpu.VMEM((BUFFERS, NEG, CHUNK), F32),
             pltpu.VMEM((BUFFERS, D, CHUNK), F32),
             pltpu.VMEM((BUFFERS, D, CHUNK), F32),
+            pltpu.VMEM((TALL, RELP), F32),
+            pltpu.VMEM((4, 512, PER), BF),
+            pltpu.VMEM((4, 512, PER), BF),
             pltpu.SemaphoreType.DMA((COPIES,)),
         ],
         compiler_params=pltpu.CompilerParams(vmem_limit_bytes=58 * MIB),
         cost_estimate=pl.CostEstimate(flops=8_000_000_000, bytes_accessed=20_000_000, transcendentals=2_100_000),
         name="edges",
     )(place, keys, *halves, query, left, weight)
-
-
-def sums_kernel(keys_ref, lhs_g, rel_g, own_ref, other_ref, lhs_ref, total):
-    wide = 4 * PER
-    for c in range(0, EDGES, wide):
-        packed = keys_ref[0:1, c : c + wide]
-        marks = onehot(rel_of(packed), RELP)
-        for t in range(0, RELP, 2 * PER):
-            part = dot_t(rel_g[:, c : c + wide], marks[t : t + 2 * PER])
-            lanes = slice(t, t + 2 * PER)
-            total[:, lanes] = part if c == 0 else total[:, lanes] + part
-        part = dot_t(lhs_g[:, c : c + wide], onehot(lhs_of(packed), LOCAL))
-        part = jnp.concatenate([part[:HALF], part[SECOND : SECOND + HALF]], 0)
-        lhs_ref[...] = part if c == 0 else lhs_ref[...] + part
-    own = pl.multiple_of(lax.axis_index("core") * (RELP // 2), RELP // 2)
-    other = pl.multiple_of((1 - lax.axis_index("core")) * (RELP // 2), RELP // 2)
-    for at in range(4):
-        for ref, start in ((own_ref, own), (other_ref, other)):
-            lanes = pl.ds(start + at * PER, PER)
-            ref[at, 0:D, :] = jnp.concatenate([total[0:HALF, lanes], total[SECOND : SECOND + HALF, lanes]], 0).astype(BF)
-            ref[at, D:512, :] = jnp.zeros((112, PER), BF)
-
-
-def sums(keys, lhs_g, rel_g):
-    return pl.pallas_call(
-        sums_kernel,
-        out_shape=[
-            jax.ShapeDtypeStruct((4, 512, PER), BF),
-            jax.ShapeDtypeStruct((4, 512, PER), BF),
-            jax.ShapeDtypeStruct((D, LOCAL), F32),
-        ],
-        scratch_shapes=[pltpu.VMEM((TALL, RELP), F32)],
-        compiler_params=pltpu.CompilerParams(vmem_limit_bytes=58 * MIB),
-        cost_estimate=pl.CostEstimate(flops=3_000_000_000, bytes_accessed=6_000_000, transcendentals=0),
-        name="edge_sums",
-    )(keys, lhs_g, rel_g)
 
 
 def spread_kernel(axis, *refs):
@@ -362,7 +352,7 @@
             ],
         ),
         out_shape=[jax.ShapeDtypeStruct((D, LOCAL), F32), jax.ShapeDtypeStruct((1, LOCAL), F32)],
-        compiler_params=pltpu.CompilerParams(vmem_limit_bytes=20 * MIB),
+        compiler_params=pltpu.CompilerParams(vmem_limit_bytes=58 * MIB),
         cost_estimate=pl.CostEstimate(flops=2_000_000_000, bytes_accessed=5_000_000, transcendentals=0),
         name="right_update",
     )(partner, ext_all, back)
@@ -394,6 +384,7 @@
     return pl.pallas_call(
         relation_kernel,
         out_shape=[jax.ShapeDtypeStruct((D, REL), F32), jax.ShapeDtypeStruct((1, REL), F32)],
+        compiler_params=pltpu.CompilerParams(vmem_limit_bytes=58 * MIB),
         name="relation_update",
     )(table, accum, own, other)
 
@@ -469,18 +460,18 @@
     keys = lax.sort(keys, is_stable=False)
     left, weight, query = make_query(keys, lhs_t, rel_t)
 
-    back, lhs_g, rel_g = edges(place, keys, halves, query, left, weight)
+    back, own, other, lhs_sum = edges(place, keys, halves, query, left, weight)
     returned = lax.all_to_all(back, ROW, 0, 0, tiled=True)
-    own, other, lhs_sum = sums(keys, lhs_g, rel_g)
+    new_lhs, new_lhs_accum = left_update(lhs_t, lhs_accum, lhs_sum)
+    new_rhs, new_rhs_accum = right_update(partner, ext_all, returned)
     pieces = spread("x", [own.reshape(64, 32, PER), other_core(other).reshape(64, 32, PER)])
     total = add_four([pieces[0]] + [shift(pieces[d], "x", d) for d in (1, 2, 3)])
-    for axis in ("z", "y"):
-        total = add_four([total] + [shift(total, axis, d) for d in (1, 2, 3)])
-    own = jnp.stack([total] + [shift(total, "x", d) for d in (1, 2, 3)]).reshape(4, 512, PER)
-
-    new_lhs, new_lhs_accum = left_update(lhs_t, lhs_accum, lhs_sum)
-    new_rhs, new_rhs_accum = right_update(partner, ext_all, returned)
-    own, new_rhs, new_lhs = lax.optimization_barrier((own, new_rhs, new_lhs))
+    total = add_four([total] + [shift(total, "z", d) for d in (1, 2, 3)])
+    pieces = [total] + [shift(total, "y", d) for d in (1, 2, 3)]
+    pieces, new_lhs, new_rhs = lax.optimization_barrier((pieces, new_lhs, new_rhs))
+    total = add_four(pieces)
+    pieces = [total] + [shift(total, "x", d) for d in (1, 2, 3)]
+    own = jnp.stack(pieces).reshape(4, 512, PER)
     new_rel, new_rel_accum = relation_update(rel_t, rel_accum[None], own, other_core(own))
     return (
         new_lhs.T[None],

time: 169 us -> 164 us (0.970)
  Pallas kernels: 41.6 us -> 39.1 us
    pallas_call x1 -> x0, Pallas kernels: 5.81 us -> none  [sums(): pl.pallas_call(sums_kernel, out_shape=[jax.ShapeDtypeStruct((4, 512, PER)...]
    pallas_call x1, Pallas kernels: 2.36 us -> 4.19 us  [right_update(): pl.pallas_call(right_kernel, grid_spec=pltpu.PrefetchScalarGridSpec(num_s...]
    unnamed x29 -> x27, local copies, waits for them, and re-layouts: 5.36 us -> 4.1 us
  transfers between devices with their start and end apart: 33 -> 33, of which waited for: 17 -> 17; matrix products, arithmetic and copies ran while one was open for 4% -> 4% of each run, Pallas kernels for 21% -> 22%
where the time goes in v4:
time: 164 us; the launch traced here: 163 us
  starting transfers between devices  62.1 us (38%)
  Pallas kernels  39.1 us (24%)
  waiting for transfers between devices  32.4 us (20%)
  between operations  17.7 us (11%)
  other arithmetic  6.91 us (4%)
  local copies, waits for them, and re-layouts  4.84 us (3%)
    ppermute x27, starting transfers between devices, shift(): return lax.ppermute(value, axis, [(i, i + distance & 3) for i in range(4)])  42.1 us
    ppermute x27, waiting for transfers between devices, shift(): return lax.ppermute(value, axis, [(i, i + distance & 3) for i in range(4)])  28.1 us
    pallas_call x1, Pallas kernels, edges(): pl.pallas_call(edge_kernel, in_specs=[pl.BlockSpec(memory_space=pltpu.SME...  18.8 us
    ppermute x4, starting transfers between devices, other_core(): return lax.ppermute(value, 'core', CORES)  11.6 us
    pallas_call x1, Pallas kernels, make_query(): pl.pallas_call(query_kernel, grid=(STEPS,), in_specs=[pl.BlockSpec((2, CH...  8.58 us
    all_to_all x1, starting transfers between devices, body(): returned = lax.all_to_all(back, ROW, 0, 0, tiled=True)  8.33 us
    pallas_call x1, Pallas kernels, right_update(): pl.pallas_call(right_kernel, grid_spec=pltpu.PrefetchScalarGridSpec(num_s...  4.19 us
    unnamed x27, local copies, waits for them, and re-layouts  4.1 us
  transfers between devices with their start and end apart: 33, of which 17 were waited for; matrix products, arithmetic and copies ran while one was open for 4% of the time, Pallas kernels for 22%

profile of v4, /device:TPU:1, one launch (start us, length us, event | category | flops | bytes accessed | tf_op | source)
XLA Modules:
  0.0 163.0 jit_solution(13278439497385474421)
XLA Ops:
  8.1 1.1 bitcast_convert_fusion
  9.1 2.1 %collective-permute-start = (bf16[400,256]{1,0:T(8,128)(2,1)S(1)}, bf16[400,256]{1,0:T(8,128)(2,1)S(1)}, u32[]{:S(2)}, u32[]{:S(2)}) collective-permute-start(bf16[400,256]{1,0:T(8,128)(2,1)S(1)} %bitcast_convert_fusion), channel_id=1, source_target_pairs={{0,32},{32,64},{64,96},{96,0},{1,33},{33,65},{65,97},{97,1},{2,34}... | collective-permute-start | bytes 614408 | tf_op jit(solution)/shard_map/ppermute | solution.py:397
  11.2 2.5 %collective-permute-start.1 = (bf16[400,256]{1,0:T(8,128)(2,1)S(1)}, bf16[400,256]{1,0:T(8,128)(2,1)S(1)}, u32[]{:S(2)}, u32[]{:S(2)}) collective-permute-start(bf16[400,256]{1,0:T(8,128)(2,1)S(1)} %bitcast_convert_fusion), channel_id=1, source_target_pairs={{0,64},{32,96},{64,0},{96,32},{1,65},{33,97},{65,1},{97,33},{2,66}... | collective-permute-start | bytes 614408 | tf_op jit(solution)/shard_map/ppermute | solution.py:397
  13.7 1.2 collective-permute-start.2
  14.8 1.5 collective-permute-start.3
  17.7 0.7 shift-left_or_fusion
  18.4 0.8 fusion
  19.2 0.5 and_or_fusion.place_ref
  19.7 0.7 broadcast_in_dim.18
  20.4 1.8 %pad_maximum_fusion.1 = f32[408,256]{1,0:T(8,128)} fusion(f32[8,256]{1,0:T(8,128)S(1)} %broadcast_in_dim.18, f32[400,256]{1,0:T(8,128)} %bitcast.46), kind=kLoop, calls=%fused_computation.1 | loop fusion | flops 104448 | bytes 835584 | tf_op jit(solution)/shard_map/concatenate | solution.py:456
  23.0 1.3 collective-permute-start.4
  24.2 0.6 pad_add_fusion
  24.9 0.5 collective-permute-done.4
  25.5 0.5 all-gather.3.cloned.1.call-update
  26.0 3.8 %collective-permute-start.10 = (bf16[400,128]{1,0:T(8,128)(2,1)S(1)}, bf16[400,128]{1,0:T(8,128)(2,1)S(1)}, u32[]{:S(2)}, u32[]{:S(2)}) collective-permute-start(bf16[400,128]{1,0:T(8,128)(2,1)S(1)} %get-tuple-element.48), channel_id=1, source_target_pairs={{0,12},{4,0},{8,4},{12,8},{1,13},{5,1},{9,5},{13,9},{2,14},{6,2},{... | collective-permute-start | bytes 307208 | tf_op jit(solution)/shard_map/ppermute | solution.py:397
  29.9 2.9 %collective-permute-start.5 = (bf16[400,128]{1,0:T(8,128)(2,1)S(1)}, bf16[400,128]{1,0:T(8,128)(2,1)S(1)}, u32[]{:S(2)}, u32[]{:S(2)}) collective-permute-start(bf16[400,128]{1,0:T(8,128)(2,1)S(1)} %get-tuple-element.44), channel_id=1, source_target_pairs={{0,2},{1,3},{2,0},{3,1},{4,6},{5,7},{6,4},{7,5},{8,10},{9,11},{10,... | collective-permute-start | bytes 307208 | tf_op jit(solution)/shard_map/ppermute | solution.py:397
  32.8 0.4 collective-permute-start.6
  33.2 2.3 %collective-permute-start.7 = (bf16[400,128]{1,0:T(8,128)(2,1)S(1)}, bf16[400,128]{1,0:T(8,128)(2,1)S(1)}, u32[]{:S(2)}, u32[]{:S(2)}) collective-permute-start(bf16[400,128]{1,0:T(8,128)(2,1)S(1)} %get-tuple-element.44), channel_id=1, source_target_pairs={{0,3},{1,0},{2,1},{3,2},{4,7},{5,4},{6,5},{7,6},{8,11},{9,8},{10,9... | collective-permute-start | bytes 307208 | tf_op jit(solution)/shard_map/ppermute | solution.py:397
  35.5 0.7 collective-permute-start.9
  36.2 1.3 collective-permute-done.6
  37.5 0.3 collective-permute-done.7
  37.8 2.8 %collective-permute-done.8 = bf16[400,128]{1,0:T(8,128)(2,1)S(1)} collective-permute-done((bf16[400,128]{1,0:T(8,128)(2,1)S(1)}, bf16[400,128]{1,0:T(8,128)(2,1)S(1)}, u32[]{:S(2)}, u32[]{:S(2)}) %collective-permute-start.8) | collective-permute-done | bytes 102432 | tf_op jit(solution)/shard_map/ppermute | solution.py:397
  40.6 1.2 collective-permute-done.9
  42.0 2.6 %collective-permute-start.15 = (bf16[4,400,128]{2,1,0:T(8,128)(2,1)S(1)}, bf16[4,400,128]{2,1,0:T(8,128)(2,1)S(1)}, u32[]{:S(2)}, u32[]{:S(2)}) collective-permute-start(bf16[4,400,128]{2,1,0:T(8,128)(2,1)S(1)} %pad_maximum_fusion.3.b0), channel_id=1, source_target_pairs={{0,2},{1,3},{2,0},{3,1},{4,6},{5,7},{6,4},{7,5},{8,10},{9,11},{10,... | collective-permute-start | bytes 1228808 | tf_op jit(solution)/shard_map/ppermute | solution.py:397
  44.5 0.8 collective-permute-start.16
  45.4 1.1 collective-permute-start.12
  46.5 5.3 %collective-permute-done.14.b1 = bf16[4,400,128]{2,1,0:T(8,128)(2,1)S(1)} collective-permute-done((bf16[4,400,128]{2,1,0:T(8,128)(2,1)S(1)}, bf16[4,400,128]{2,1,0:T(8,128)(2,1)S(1)}, u32[]{:S(2)}, u32[]{:S(2)}) %collective-permute-start.14) | collective-permute-done | bytes 409632 | tf_op jit(solution)/shard_map/ppermute | solution.py:397
  51.9 1.8 %collective-permute-start.13 = (bf16[4,400,128]{2,1,0:T(8,128)(2,1)S(1)}, bf16[4,400,128]{2,1,0:T(8,128)(2,1)S(1)}, u32[]{:S(2)}, u32[]{:S(2)}) collective-permute-start(bf16[4,400,128]{2,1,0:T(8,128)(2,1)S(1)} %pad_maximum_fusion.2.a0), channel_id=1, source_target_pairs={{0,12},{4,0},{8,4},{12,8},{1,13},{5,1},{9,5},{13,9},{2,14},{6,2},{... | collective-permute-start | bytes 1228808 | tf_op jit(solution)/shard_map/ppermute | solution.py:397
  53.6 8.6 %make_query.1 = (bf16[416,2048]{1,0:T(8,128)(2,1)}, bf16[416,2048]{1,0:T(8,128)(2,1)}, bf16[400,2048]{1,0:T(8,128)(2,1)}) custom-call(s32[2,2048]{1,0:T(2,128)} %sort.9.cloned.1.call-done.keys_ref, f32[400,256]{1,0:T(8,128)} %bitcast.54, f32[400,1000]{1,0:T(8,128)} %bitcast.47), custom_call_target="tpu_custom_call" | custom-call | flops 5000000000 | bytes 10000000 | tf_op jit(solution)/shard_map/make_query/pallas_call | solution.py:85
  62.3 0.6 collective-permute-done.16.b3
  62.9 0.2 collective-permute-done.13.a3
  63.1 0.5 copy-done.9
  64.1 18.8 %edges.1 = (bf16[16,624,128]{2,1,0:T(8,128)(2,1)}, bf16[4,512,128]{2,1,0:T(8,128)(2,1)}, bf16[4,512,128]{2,1,0:T(8,128)(2,1)}, f32[400,256]{1,0:T(8,128)}) custom-call(s32[16]{0:T(128)} %and_or_fusion.place_ref, s32[2,2048]{1,0:T(2,128)} %sort.9.cloned.1.call-done.keys_ref, bf16[4,400,128]{2,1,0:T(8,128)(2,1)} %copy-done.6, bf16[4,400,128]{2,1,0:T(8,128)(2,1)} %copy-done.10, ...), custom_call_target="tpu_custom_call" | custom-call | flops 8000000000 | bytes 20000000 | tf_op jit(solution)/shard_map/edges/pallas_call | solution.py:254
  82.9 8.3 %all-to-all-start = ((bf16[16,624,128]{2,1,0:T(8,128)(2,1)}), bf16[16,624,128]{2,1,0:T(8,128)(2,1)S(1)}, u32[]{:S(2)}, u32[]{:S(2)}) async-start(bf16[16,624,128]{2,1,0:T(8,128)(2,1)} %get-tuple-element.64), calls=%async_computation | async-start | bytes 5111808 | tf_op jit(solution)/shard_map/all_to_all | solution.py:464
  91.2 6.1 %collective-permute-start.17 = (bf16[4,512,128]{2,1,0:T(8,128)(2,1)}, bf16[4,512,128]{2,1,0:T(8,128)(2,1)S(1)}, u32[]{:S(2)}, u32[]{:S(2)}) collective-permute-start(bf16[4,512,128]{2,1,0:T(8,128)(2,1)} %get-tuple-element.56), channel_id=1, source_target_pairs={{0,16},{16,0},{1,17},{17,1},{2,18},{18,2},{3,19},{19,3},{4,20},{20... | collective-permute-start | bytes 1572872 | tf_op jit(solution)/shard_map/ppermute | solution.py:401
  97.3 1.7 %collective-permute-done.17 = bf16[4,512,128]{2,1,0:T(8,128)(2,1)S(1)} collective-permute-done((bf16[4,512,128]{2,1,0:T(8,128)(2,1)}, bf16[4,512,128]{2,1,0:T(8,128)(2,1)S(1)}, u32[]{:S(2)}, u32[]{:S(2)}) %collective-permute-start.17) | collective-permute-done | bytes 524320 | tf_op jit(solution)/shard_map/ppermute | solution.py:401
  99.0 0.8 copy-done.3
  99.8 2.1 %spread.1 = (bf16[16,32,128]{2,1,0:T(8,128)(2,1)}, bf16[16,32,128]{2,1,0:T(8,128)(2,1)}, bf16[16,32,128]{2,1,0:T(8,128)(2,1)}, bf16[16,32,128]{2,1,0:T(8,128)(2,1)}) custom-call(bf16[64,32,128]{2,1,0:T(8,128)(2,1)} %bitcast.49, bf16[64,32,128]{2,1,0:T(8,128)(2,1)} %bitcast.50), custom_call_target="tpu_custom_call" | custom-call | tf_op jit(solution)/shard_map/spread/pallas_call | solution.py:302
  101.9 2.4 %collective-permute-start.18 = (bf16[16,32,128]{2,1,0:T(8,128)(2,1)}, bf16[16,32,128]{2,1,0:T(8,128)(2,1)S(1)}, u32[]{:S(2)}, u32[]{:S(2)}) collective-permute-start(bf16[16,32,128]{2,1,0:T(8,128)(2,1)} %get-tuple-element.58), channel_id=1, source_target_pairs={{0,64},{32,96},{64,0},{96,32},{1,65},{33,97},{65,1},{97,33},{2,66}... | collective-permute-start | bytes 393224 | tf_op jit(solution)/shard_map/ppermute | solution.py:397
  104.3 0.2 collective-permute-start.19
  104.4 2.5 %collective-permute-start.20 = (bf16[16,32,128]{2,1,0:T(8,128)(2,1)}, bf16[16,32,128]{2,1,0:T(8,128)(2,1)S(1)}, u32[]{:S(2)}, u32[]{:S(2)}) collective-permute-start(bf16[16,32,128]{2,1,0:T(8,128)(2,1)} %get-tuple-element.60), channel_id=1, source_target_pairs={{0,96},{32,0},{64,32},{96,64},{1,97},{33,1},{65,33},{97,65},{2,98}... | collective-permute-start | bytes 393224 | tf_op jit(solution)/shard_map/ppermute | solution.py:397
  106.9 1.4 collective-permute-done.18
  108.3 3.1 %collective-permute-done.19 = bf16[16,32,128]{2,1,0:T(8,128)(2,1)S(1)} collective-permute-done((bf16[16,32,128]{2,1,0:T(8,128)(2,1)}, bf16[16,32,128]{2,1,0:T(8,128)(2,1)S(1)}, u32[]{:S(2)}, u32[]{:S(2)}) %collective-permute-start.19) | collective-permute-done | bytes 131104 | tf_op jit(solution)/shard_map/ppermute | solution.py:397
  111.4 1.0 add_convert_fusion.2
  112.4 3.1 %collective-permute-start.21 = (bf16[16,32,128]{2,1,0:T(8,128)(2,1)S(1)}, bf16[16,32,128]{2,1,0:T(8,128)(2,1)S(1)}, u32[]{:S(2)}, u32[]{:S(2)}) collective-permute-start(bf16[16,32,128]{2,1,0:T(8,128)(2,1)S(1)} %add_convert_fusion.2), channel_id=1, source_target_pairs={{0,8},{4,12},{8,0},{12,4},{1,9},{5,13},{9,1},{13,5},{2,10},{6,14},... | collective-permute-start | bytes 393224 | tf_op jit(solution)/shard_map/ppermute | solution.py:397
  115.5 0.3 collective-permute-start.22
  115.8 2.4 %collective-permute-start.23 = (bf16[16,32,128]{2,1,0:T(8,128)(2,1)S(1)}, bf16[16,32,128]{2,1,0:T(8,128)(2,1)S(1)}, u32[]{:S(2)}, u32[]{:S(2)}) collective-permute-start(bf16[16,32,128]{2,1,0:T(8,128)(2,1)S(1)} %add_convert_fusion.2), channel_id=1, source_target_pairs={{0,12},{4,0},{8,4},{12,8},{1,13},{5,1},{9,5},{13,9},{2,14},{6,2},{... | collective-permute-start | bytes 393224 | tf_op jit(solution)/shard_map/ppermute | solution.py:397
  118.1 2.0 %left_update.1 = (f32[400,256]{1,0:T(8,128)}, f32[1,256]{1,0:T(1,128)}) custom-call(f32[400,256]{1,0:T(8,128)} %bitcast.55, f32[1,256]{1,0:T(1,128)} %accum_ref.1, f32[400,256]{1,0:T(8,128)} %get-tuple-element.61.grad_ref), custom_call_target="tpu_custom_call" | custom-call | tf_op jit(solution)/shard_map/left_update/pallas_call | solution.py:366
  120.1 3.1 %collective-permute-done.21 = bf16[16,32,128]{2,1,0:T(8,128)(2,1)S(1)} collective-permute-done((bf16[16,32,128]{2,1,0:T(8,128)(2,1)S(1)}, bf16[16,32,128]{2,1,0:T(8,128)(2,1)S(1)}, u32[]{:S(2)}, u32[]{:S(2)}) %collective-permute-start.21) | collective-permute-done | bytes 131104 | tf_op jit(solution)/shard_map/ppermute | solution.py:397
  123.2 5.3 %collective-permute-done.22 = bf16[16,32,128]{2,1,0:T(8,128)(2,1)S(1)} collective-permute-done((bf16[16,32,128]{2,1,0:T(8,128)(2,1)S(1)}, bf16[16,32,128]{2,1,0:T(8,128)(2,1)S(1)}, u32[]{:S(2)}, u32[]{:S(2)}) %collective-permute-start.22) | collective-permute-done | bytes 131104 | tf_op jit(solution)/shard_map/ppermute | solution.py:397
  128.7 1.4 collective-permute-start.24
  130.0 2.4 %collective-permute-start.25 = (bf16[16,32,128]{2,1,0:T(8,128)(2,1)S(1)}, bf16[16,32,128]{2,1,0:T(8,128)(2,1)S(1)}, u32[]{:S(2)}, u32[]{:S(2)}) collective-permute-start(bf16[16,32,128]{2,1,0:T(8,128)(2,1)S(1)} %add_convert_fusion.1), channel_id=1, source_target_pairs={{0,2},{1,3},{2,0},{3,1},{4,6},{5,7},{6,4},{7,5},{8,10},{9,11},{10,... | collective-permute-start | bytes 393224 | tf_op jit(solution)/shard_map/ppermute | solution.py:397
  132.4 0.9 collective-permute-start.26
  133.3 1.5 copy-done.1
  134.8 4.2 %right_update.1 = (f32[400,256]{1,0:T(8,128)}, f32[1,256]{1,0:T(1,128)}) custom-call(s32[1]{0:T(128)S(6)} %copy.18.partner_ref, f32[8,408,256]{2,1,0:T(8,128)} %bitcast.69, bf16[16,624,128]{2,1,0:T(8,128)(2,1)} %copy-done.1), custom_call_target="tpu_custom_call" | custom-call | flops 2000000000 | bytes 5000000 | tf_op jit(solution)/shard_map/right_update/pallas_call | solution.py:336
  139.1 1.1 collective-permute-start.27
  140.2 2.1 %collective-permute-start.28 = (bf16[16,32,128]{2,1,0:T(8,128)(2,1)S(1)}, bf16[16,32,128]{2,1,0:T(8,128)(2,1)S(1)}, u32[]{:S(2)}, u32[]{:S(2)}) collective-permute-start(bf16[16,32,128]{2,1,0:T(8,128)(2,1)S(1)} %add_convert_fusion), channel_id=1, source_target_pairs={{0,64},{32,96},{64,0},{96,32},{1,65},{33,97},{65,1},{97,33},{2,66}... | collective-permute-start | bytes 393224 | tf_op jit(solution)/shard_map/ppermute | solution.py:397
  142.3 1.3 collective-permute-start.29
  143.6 0.6 collective-permute-done.27
  144.2 2.7 %collective-permute-done.28 = bf16[16,32,128]{2,1,0:T(8,128)(2,1)S(1)} collective-permute-done((bf16[16,32,128]{2,1,0:T(8,128)(2,1)S(1)}, bf16[16,32,128]{2,1,0:T(8,128)(2,1)S(1)}, u32[]{:S(2)}, u32[]{:S(2)}) %collective-permute-start.28) | collective-permute-done | bytes 131104 | tf_op jit(solution)/shard_map/ppermute | solution.py:397
  147.1 2.7 %collective-permute-start.30 = (bf16[4,512,128]{2,1,0:T(8,128)(2,1)S(1)}, bf16[4,512,128]{2,1,0:T(8,128)(2,1)S(1)}, u32[]{:S(2)}, u32[]{:S(2)}) collective-permute-start(bf16[4,512,128]{2,1,0:T(8,128)(2,1)S(1)} %pad_maximum_fusion.own_ref), channel_id=1, source_target_pairs={{0,16},{16,0},{1,17},{17,1},{2,18},{18,2},{3,19},{19,3},{4,20},{20... | collective-permute-start | bytes 1572872 | tf_op jit(solution)/shard_map/ppermute | solution.py:401
  149.8 1.5 collective-permute-done.30.other_ref
  151.4 0.8 copy-done.4
  152.1 3.4 %relation_update.1 = (f32[400,1000]{1,0:T(8,128)}, f32[1,1000]{1,0:T(1,128)}) custom-call(f32[400,1000]{1,0:T(8,128)} %bitcast.48, f32[1,1000]{1,0:T(1,128)} %bitcast.67, bf16[4,512,128]{2,1,0:T(8,128)(2,1)} %copy-done.2, bf16[4,512,128]{2,1,0:T(8,128)(2,1)} %copy-done.4), custom_call_target="tpu_custom_call" | custom-call | tf_op jit(solution)/shard_map/relation_update/pallas_call | solution.py:384
  (55 shorter events, 1.3 us)
Async XLA Ops:
  8.0 14.9 %copy-start = (f32[1,256,400]{1,2,0:T(8,128)S(1)}, f32[1,256,400]{1,2,0:T(8,128)}, u32[]{:S(2)}) copy-start(f32[1,256,400]{1,2,0:T(8,128)} %param.14) | copy-start | bytes 1228804
  8.0 45.6 %sort.9.cloned.1.call-start = ((), (), s32[]{:S(2)}) async-start(), calls=%async_computation.2 | async-start | bytes 49184 | tf_op jit(solution)/shard_map/sort | solution.py:460
  9.1 13.7 %collective-permute-start = (bf16[400,256]{1,0:T(8,128)(2,1)S(1)}, bf16[400,256]{1,0:T(8,128)(2,1)S(1)}, u32[]{:S(2)}, u32[]{:S(2)}) collective-permute-start(bf16[400,256]{1,0:T(8,128)(2,1)S(1)} %bitcast_convert_fusion), channel_id=1, source_target_pairs={{0,32},{32,64},{64,96},{96,0},{1,33},{33,65},{65,97},{97,1},{2,34}... | collective-permute-start | bytes 614408 | tf_op jit(solution)/shard_map/ppermute | solution.py:397
  11.2 11.6 %collective-permute-start.1 = (bf16[400,256]{1,0:T(8,128)(2,1)S(1)}, bf16[400,256]{1,0:T(8,128)(2,1)S(1)}, u32[]{:S(2)}, u32[]{:S(2)}) collective-permute-start(bf16[400,256]{1,0:T(8,128)(2,1)S(1)} %bitcast_convert_fusion), channel_id=1, source_target_pairs={{0,64},{32,96},{64,0},{96,32},{1,65},{33,97},{65,1},{97,33},{2,66}... | collective-permute-start | bytes 614408 | tf_op jit(solution)/shard_map/ppermute | solution.py:397
  13.7 9.2 %collective-permute-start.2 = (bf16[400,256]{1,0:T(8,128)(2,1)S(1)}, bf16[400,256]{1,0:T(8,128)(2,1)S(1)}, u32[]{:S(2)}, u32[]{:S(2)}) collective-permute-start(bf16[400,256]{1,0:T(8,128)(2,1)S(1)} %bitcast_convert_fusion), channel_id=1, source_target_pairs={{0,96},{32,0},{64,32},{96,64},{1,97},{33,1},{65,33},{97,65},{2,98}... | collective-permute-start | bytes 614408 | tf_op jit(solution)/shard_map/ppermute | solution.py:397
  14.8 7.3 %collective-permute-start.3 = (s32[1]{0:T(128)}, s32[1]{0:T(128)}, u32[]{:S(2)}, u32[]{:S(2)}) collective-permute-start(s32[1]{0:T(128)} %param.18), channel_id=1, source_target_pairs={{0,16},{16,0},{1,17},{17,1},{2,18},{18,2},{3,19},{19,3},{4,20},{20... | collective-permute-start | bytes 20 | tf_op jit(solution)/shard_map/ppermute | solution.py:401
  23.0 2.4 %collective-permute-start.4 = (bf16[400,256]{1,0:T(8,128)(2,1)S(1)}, bf16[400,256]{1,0:T(8,128)(2,1)S(1)}, u32[]{:S(2)}, u32[]{:S(2)}) collective-permute-start(bf16[400,256]{1,0:T(8,128)(2,1)S(1)} %select_select_fusion), channel_id=1, source_target_pairs={{0,16},{16,0},{1,17},{17,1},{2,18},{18,2},{3,19},{19,3},{4,20},{20... | collective-permute-start | bytes 614408 | tf_op jit(solution)/shard_map/ppermute | solution.py:401
  25.4 107.9 %all-gather.3.cloned.1.call-start = ((), (), s32[]{:S(2)}) async-start(), calls=%async_computation.1 | async-start | bytes 3760128 | tf_op jit(solution)/shard_map/all_gather | solution.py:458
  26.0 9.4 %collective-permute-start.10 = (bf16[400,128]{1,0:T(8,128)(2,1)S(1)}, bf16[400,128]{1,0:T(8,128)(2,1)S(1)}, u32[]{:S(2)}, u32[]{:S(2)}) collective-permute-start(bf16[400,128]{1,0:T(8,128)(2,1)S(1)} %get-tuple-element.48), channel_id=1, source_target_pairs={{0,12},{4,0},{8,4},{12,8},{1,13},{5,1},{9,5},{13,9},{2,14},{6,2},{... | collective-permute-start | bytes 307208 | tf_op jit(solution)/shard_map/ppermute | solution.py:397
  29.9 6.3 %collective-permute-start.5 = (bf16[400,128]{1,0:T(8,128)(2,1)S(1)}, bf16[400,128]{1,0:T(8,128)(2,1)S(1)}, u32[]{:S(2)}, u32[]{:S(2)}) collective-permute-start(bf16[400,128]{1,0:T(8,128)(2,1)S(1)} %get-tuple-element.44), channel_id=1, source_target_pairs={{0,2},{1,3},{2,0},{3,1},{4,6},{5,7},{6,4},{7,5},{8,10},{9,11},{10,... | collective-permute-start | bytes 307208 | tf_op jit(solution)/shard_map/ppermute | solution.py:397
  32.8 4.7 %collective-permute-start.6 = (bf16[400,128]{1,0:T(8,128)(2,1)S(1)}, bf16[400,128]{1,0:T(8,128)(2,1)S(1)}, u32[]{:S(2)}, u32[]{:S(2)}) collective-permute-start(bf16[400,128]{1,0:T(8,128)(2,1)S(1)} %get-tuple-element.44), channel_id=1, source_target_pairs={{0,1},{1,2},{2,3},{3,0},{4,5},{5,6},{6,7},{7,4},{8,9},{9,10},{10,1... | collective-permute-start | bytes 307208 | tf_op jit(solution)/shard_map/ppermute | solution.py:397
  33.2 4.6 %collective-permute-start.7 = (bf16[400,128]{1,0:T(8,128)(2,1)S(1)}, bf16[400,128]{1,0:T(8,128)(2,1)S(1)}, u32[]{:S(2)}, u32[]{:S(2)}) collective-permute-start(bf16[400,128]{1,0:T(8,128)(2,1)S(1)} %get-tuple-element.44), channel_id=1, source_target_pairs={{0,3},{1,0},{2,1},{3,2},{4,7},{5,4},{6,5},{7,6},{8,11},{9,8},{10,9... | collective-permute-start | bytes 307208 | tf_op jit(solution)/shard_map/ppermute | solution.py:397
  35.5 5.1 %collective-permute-start.8 = (bf16[400,128]{1,0:T(8,128)(2,1)S(1)}, bf16[400,128]{1,0:T(8,128)(2,1)S(1)}, u32[]{:S(2)}, u32[]{:S(2)}) collective-permute-start(bf16[400,128]{1,0:T(8,128)(2,1)S(1)} %get-tuple-element.48), channel_id=1, source_target_pairs={{0,8},{4,12},{8,0},{12,4},{1,9},{5,13},{9,1},{13,5},{2,10},{6,14},... | collective-permute-start | bytes 307208 | tf_op jit(solution)/shard_map/ppermute | solution.py:397
  35.5 6.4 %collective-permute-start.9 = (bf16[400,128]{1,0:T(8,128)(2,1)S(1)}, bf16[400,128]{1,0:T(8,128)(2,1)S(1)}, u32[]{:S(2)}, u32[]{:S(2)}) collective-permute-start(bf16[400,128]{1,0:T(8,128)(2,1)S(1)} %get-tuple-element.48), channel_id=1, source_target_pairs={{0,4},{4,8},{8,12},{12,0},{1,5},{5,9},{9,13},{13,1},{2,6},{6,10},{... | collective-permute-start | bytes 307208 | tf_op jit(solution)/shard_map/ppermute | solution.py:397
  41.9 20.4 %copy-start.5 = (bf16[4,400,128]{2,1,0:T(8,128)(2,1)}, bf16[4,400,128]{2,1,0:T(8,128)(2,1)S(1)}, u32[]{:S(2)}) copy-start(bf16[4,400,128]{2,1,0:T(8,128)(2,1)S(1)} %pad_maximum_fusion.3.b0) | copy-start | bytes 1228804
  41.9 10.0 %collective-permute-start.14 = (bf16[4,400,128]{2,1,0:T(8,128)(2,1)S(1)}, bf16[4,400,128]{2,1,0:T(8,128)(2,1)S(1)}, u32[]{:S(2)}, u32[]{:S(2)}) collective-permute-start(bf16[4,400,128]{2,1,0:T(8,128)(2,1)S(1)} %pad_maximum_fusion.3.b0), channel_id=1, source_target_pairs={{0,1},{1,2},{2,3},{3,0},{4,5},{5,6},{6,7},{7,4},{8,9},{9,10},{10,1... | collective-permute-start | bytes 1228808 | tf_op jit(solution)/shard_map/ppermute | solution.py:397
  42.0 20.3 %collective-permute-start.15 = (bf16[4,400,128]{2,1,0:T(8,128)(2,1)S(1)}, bf16[4,400,128]{2,1,0:T(8,128)(2,1)S(1)}, u32[]{:S(2)}, u32[]{:S(2)}) collective-permute-start(bf16[4,400,128]{2,1,0:T(8,128)(2,1)S(1)} %pad_maximum_fusion.3.b0), channel_id=1, source_target_pairs={{0,2},{1,3},{2,0},{3,1},{4,6},{5,7},{6,4},{7,5},{8,10},{9,11},{10,... | collective-permute-start | bytes 1228808 | tf_op jit(solution)/shard_map/ppermute | solution.py:397
  44.5 18.4 %collective-permute-start.16 = (bf16[4,400,128]{2,1,0:T(8,128)(2,1)S(1)}, bf16[4,400,128]{2,1,0:T(8,128)(2,1)S(1)}, u32[]{:S(2)}, u32[]{:S(2)}) collective-permute-start(bf16[4,400,128]{2,1,0:T(8,128)(2,1)S(1)} %pad_maximum_fusion.3.b0), channel_id=1, source_target_pairs={{0,3},{1,0},{2,1},{3,2},{4,7},{5,4},{6,5},{7,6},{8,11},{9,8},{10,9... | collective-permute-start | bytes 1228808 | tf_op jit(solution)/shard_map/ppermute | solution.py:397
  45.3 16.9 %copy-start.6 = (bf16[4,400,128]{2,1,0:T(8,128)(2,1)}, bf16[4,400,128]{2,1,0:T(8,128)(2,1)S(1)}, u32[]{:S(2)}) copy-start(bf16[4,400,128]{2,1,0:T(8,128)(2,1)S(1)} %pad_maximum_fusion.2.a0) | copy-start | bytes 1228804
  45.4 17.5 %collective-permute-start.11 = (bf16[4,400,128]{2,1,0:T(8,128)(2,1)S(1)}, bf16[4,400,128]{2,1,0:T(8,128)(2,1)S(1)}, u32[]{:S(2)}, u32[]{:S(2)}) collective-permute-start(bf16[4,400,128]{2,1,0:T(8,128)(2,1)S(1)} %pad_maximum_fusion.2.a0), channel_id=1, source_target_pairs={{0,4},{4,8},{8,12},{12,0},{1,5},{5,9},{9,13},{13,1},{2,6},{6,10},{... | collective-permute-start | bytes 1228808 | tf_op jit(solution)/shard_map/ppermute | solution.py:397
  45.4 17.5 %collective-permute-start.12 = (bf16[4,400,128]{2,1,0:T(8,128)(2,1)S(1)}, bf16[4,400,128]{2,1,0:T(8,128)(2,1)S(1)}, u32[]{:S(2)}, u32[]{:S(2)}) collective-permute-start(bf16[4,400,128]{2,1,0:T(8,128)(2,1)S(1)} %pad_maximum_fusion.2.a0), channel_id=1, source_target_pairs={{0,8},{4,12},{8,0},{12,4},{1,9},{5,13},{9,1},{13,5},{2,10},{6,14},... | collective-permute-start | bytes 1228808 | tf_op jit(solution)/shard_map/ppermute | solution.py:397
  51.9 10.4 %copy-start.7 = (bf16[4,400,128]{2,1,0:T(8,128)(2,1)}, bf16[4,400,128]{2,1,0:T(8,128)(2,1)S(1)}, u32[]{:S(2)}) copy-start(bf16[4,400,128]{2,1,0:T(8,128)(2,1)S(1)} %collective-permute-done.14.b1) | copy-start | bytes 1228804
  51.9 11.2 %collective-permute-start.13 = (bf16[4,400,128]{2,1,0:T(8,128)(2,1)S(1)}, bf16[4,400,128]{2,1,0:T(8,128)(2,1)S(1)}, u32[]{:S(2)}, u32[]{:S(2)}) collective-permute-start(bf16[4,400,128]{2,1,0:T(8,128)(2,1)S(1)} %pad_maximum_fusion.2.a0), channel_id=1, source_target_pairs={{0,12},{4,0},{8,4},{12,8},{1,13},{5,1},{9,5},{13,9},{2,14},{6,2},{... | collective-permute-start | bytes 1228808 | tf_op jit(solution)/shard_map/ppermute | solution.py:397
  62.2 0.8 copy-start.8
  62.9 0.7 copy-start.9
  62.9 0.9 copy-start.10
  62.9 1.0 copy-start.11
  63.1 1.0 copy-start.12
  82.9 50.4 %all-to-all-start = ((bf16[16,624,128]{2,1,0:T(8,128)(2,1)}), bf16[16,624,128]{2,1,0:T(8,128)(2,1)S(1)}, u32[]{:S(2)}, u32[]{:S(2)}) async-start(bf16[16,624,128]{2,1,0:T(8,128)(2,1)} %get-tuple-element.64), calls=%async_computation | async-start | bytes 5111808 | tf_op jit(solution)/shard_map/all_to_all | solution.py:464
  91.2 7.8 %collective-permute-start.17 = (bf16[4,512,128]{2,1,0:T(8,128)(2,1)}, bf16[4,512,128]{2,1,0:T(8,128)(2,1)S(1)}, u32[]{:S(2)}, u32[]{:S(2)}) collective-permute-start(bf16[4,512,128]{2,1,0:T(8,128)(2,1)} %get-tuple-element.56), channel_id=1, source_target_pairs={{0,16},{16,0},{1,17},{17,1},{2,18},{18,2},{3,19},{19,3},{4,20},{20... | collective-permute-start | bytes 1572872 | tf_op jit(solution)/shard_map/ppermute | solution.py:401
  99.0 0.8 copy-start.3
  101.9 6.4 %collective-permute-start.18 = (bf16[16,32,128]{2,1,0:T(8,128)(2,1)}, bf16[16,32,128]{2,1,0:T(8,128)(2,1)S(1)}, u32[]{:S(2)}, u32[]{:S(2)}) collective-permute-start(bf16[16,32,128]{2,1,0:T(8,128)(2,1)} %get-tuple-element.58), channel_id=1, source_target_pairs={{0,64},{32,96},{64,0},{96,32},{1,65},{33,97},{65,1},{97,33},{2,66}... | collective-permute-start | bytes 393224 | tf_op jit(solution)/shard_map/ppermute | solution.py:397
  104.3 7.1 %collective-permute-start.19 = (bf16[16,32,128]{2,1,0:T(8,128)(2,1)}, bf16[16,32,128]{2,1,0:T(8,128)(2,1)S(1)}, u32[]{:S(2)}, u32[]{:S(2)}) collective-permute-start(bf16[16,32,128]{2,1,0:T(8,128)(2,1)} %get-tuple-element.59), channel_id=1, source_target_pairs={{0,32},{32,64},{64,96},{96,0},{1,33},{33,65},{65,97},{97,1},{2,34}... | collective-permute-start | bytes 393224 | tf_op jit(solution)/shard_map/ppermute | solution.py:397
  104.4 7.0 %collective-permute-start.20 = (bf16[16,32,128]{2,1,0:T(8,128)(2,1)}, bf16[16,32,128]{2,1,0:T(8,128)(2,1)S(1)}, u32[]{:S(2)}, u32[]{:S(2)}) collective-permute-start(bf16[16,32,128]{2,1,0:T(8,128)(2,1)} %get-tuple-element.60), channel_id=1, source_target_pairs={{0,96},{32,0},{64,32},{96,64},{1,97},{33,1},{65,33},{97,65},{2,98}... | collective-permute-start | bytes 393224 | tf_op jit(solution)/shard_map/ppermute | solution.py:397
  112.4 10.9 %collective-permute-start.21 = (bf16[16,32,128]{2,1,0:T(8,128)(2,1)S(1)}, bf16[16,32,128]{2,1,0:T(8,128)(2,1)S(1)}, u32[]{:S(2)}, u32[]{:S(2)}) collective-permute-start(bf16[16,32,128]{2,1,0:T(8,128)(2,1)S(1)} %add_convert_fusion.2), channel_id=1, source_target_pairs={{0,8},{4,12},{8,0},{12,4},{1,9},{5,13},{9,1},{13,5},{2,10},{6,14},... | collective-permute-start | bytes 393224 | tf_op jit(solution)/shard_map/ppermute | solution.py:397
  115.5 13.1 %collective-permute-start.22 = (bf16[16,32,128]{2,1,0:T(8,128)(2,1)S(1)}, bf16[16,32,128]{2,1,0:T(8,128)(2,1)S(1)}, u32[]{:S(2)}, u32[]{:S(2)}) collective-permute-start(bf16[16,32,128]{2,1,0:T(8,128)(2,1)S(1)} %add_convert_fusion.2), channel_id=1, source_target_pairs={{0,4},{4,8},{8,12},{12,0},{1,5},{5,9},{9,13},{13,1},{2,6},{6,10},{... | collective-permute-start | bytes 393224 | tf_op jit(solution)/shard_map/ppermute | solution.py:397
  115.8 12.8 %collective-permute-start.23 = (bf16[16,32,128]{2,1,0:T(8,128)(2,1)S(1)}, bf16[16,32,128]{2,1,0:T(8,128)(2,1)S(1)}, u32[]{:S(2)}, u32[]{:S(2)}) collective-permute-start(bf16[16,32,128]{2,1,0:T(8,128)(2,1)S(1)} %add_convert_fusion.2), channel_id=1, source_target_pairs={{0,12},{4,0},{8,4},{12,8},{1,13},{5,1},{9,5},{13,9},{2,14},{6,2},{... | collective-permute-start | bytes 393224 | tf_op jit(solution)/shard_map/ppermute | solution.py:397
  128.7 10.3 %collective-permute-start.24 = (bf16[16,32,128]{2,1,0:T(8,128)(2,1)S(1)}, bf16[16,32,128]{2,1,0:T(8,128)(2,1)S(1)}, u32[]{:S(2)}, u32[]{:S(2)}) collective-permute-start(bf16[16,32,128]{2,1,0:T(8,128)(2,1)S(1)} %add_convert_fusion.1), channel_id=1, source_target_pairs={{0,1},{1,2},{2,3},{3,0},{4,5},{5,6},{6,7},{7,4},{8,9},{9,10},{10,1... | collective-permute-start | bytes 393224 | tf_op jit(solution)/shard_map/ppermute | solution.py:397
  130.0 9.0 %collective-permute-start.25 = (bf16[16,32,128]{2,1,0:T(8,128)(2,1)S(1)}, bf16[16,32,128]{2,1,0:T(8,128)(2,1)S(1)}, u32[]{:S(2)}, u32[]{:S(2)}) collective-permute-start(bf16[16,32,128]{2,1,0:T(8,128)(2,1)S(1)} %add_convert_fusion.1), channel_id=1, source_target_pairs={{0,2},{1,3},{2,0},{3,1},{4,6},{5,7},{6,4},{7,5},{8,10},{9,11},{10,... | collective-permute-start | bytes 393224 | tf_op jit(solution)/shard_map/ppermute | solution.py:397
  132.4 6.6 %collective-permute-start.26 = (bf16[16,32,128]{2,1,0:T(8,128)(2,1)S(1)}, bf16[16,32,128]{2,1,0:T(8,128)(2,1)S(1)}, u32[]{:S(2)}, u32[]{:S(2)}) collective-permute-start(bf16[16,32,128]{2,1,0:T(8,128)(2,1)S(1)} %add_convert_fusion.1), channel_id=1, source_target_pairs={{0,3},{1,0},{2,1},{3,2},{4,7},{5,4},{6,5},{7,6},{8,11},{9,8},{10,9... | collective-permute-start | bytes 393224 | tf_op jit(solution)/shard_map/ppermute | solution.py:397
  133.3 1.5 copy-start.1
  139.1 5.1 %collective-permute-start.27 = (bf16[16,32,128]{2,1,0:T(8,128)(2,1)S(1)}, bf16[16,32,128]{2,1,0:T(8,128)(2,1)S(1)}, u32[]{:S(2)}, u32[]{:S(2)}) collective-permute-start(bf16[16,32,128]{2,1,0:T(8,128)(2,1)S(1)} %add_convert_fusion), channel_id=1, source_target_pairs={{0,32},{32,64},{64,96},{96,0},{1,33},{33,65},{65,97},{97,1},{2,34}... | collective-permute-start | bytes 393224 | tf_op jit(solution)/shard_map/ppermute | solution.py:397
  140.2 6.7 %collective-permute-start.28 = (bf16[16,32,128]{2,1,0:T(8,128)(2,1)S(1)}, bf16[16,32,128]{2,1,0:T(8,128)(2,1)S(1)}, u32[]{:S(2)}, u32[]{:S(2)}) collective-permute-start(bf16[16,32,128]{2,1,0:T(8,128)(2,1)S(1)} %add_convert_fusion), channel_id=1, source_target_pairs={{0,64},{32,96},{64,0},{96,32},{1,65},{33,97},{65,1},{97,33},{2,66}... | collective-permute-start | bytes 393224 | tf_op jit(solution)/shard_map/ppermute | solution.py:397
  142.3 4.7 %collective-permute-start.29 = (bf16[16,32,128]{2,1,0:T(8,128)(2,1)S(1)}, bf16[16,32,128]{2,1,0:T(8,128)(2,1)S(1)}, u32[]{:S(2)}, u32[]{:S(2)}) collective-permute-start(bf16[16,32,128]{2,1,0:T(8,128)(2,1)S(1)} %add_convert_fusion), channel_id=1, source_target_pairs={{0,96},{32,0},{64,32},{96,64},{1,97},{33,1},{65,33},{97,65},{2,98}... | collective-permute-start | bytes 393224 | tf_op jit(solution)/shard_map/ppermute | solution.py:397
  147.1 4.3 %copy-start.2 = (bf16[4,512,128]{2,1,0:T(8,128)(2,1)}, bf16[4,512,128]{2,1,0:T(8,128)(2,1)S(1)}, u32[]{:S(2)}) copy-start(bf16[4,512,128]{2,1,0:T(8,128)(2,1)S(1)} %pad_maximum_fusion.own_ref) | copy-start | bytes 1572868
  147.1 4.2 %collective-permute-start.30 = (bf16[4,512,128]{2,1,0:T(8,128)(2,1)S(1)}, bf16[4,512,128]{2,1,0:T(8,128)(2,1)S(1)}, u32[]{:S(2)}, u32[]{:S(2)}) collective-permute-start(bf16[4,512,128]{2,1,0:T(8,128)(2,1)S(1)} %pad_maximum_fusion.own_ref), channel_id=1, source_target_pairs={{0,16},{16,0},{1,17},{17,1},{2,18},{18,2},{3,19},{19,3},{4,20},{20... | collective-permute-start | bytes 1572872 | tf_op jit(solution)/shard_map/ppermute | solution.py:401
  151.4 0.8 copy-start.4
Sparse Core Ops, SparseCore 0:
  25.6 7.6 sort.11.cloned.1.call-done
  (1 shorter events, 0.0 us)
Sparse Core Ops, SparseCore 1:
  27.7 30.5 all-gather.2

commit v5 on v4

--- a/solution.py
+++ b/solution.py
@@ -223,7 +223,7 @@
             lanes = pl.ds(start + at * PER, PER)
             both = jnp.concatenate([total_rel[0:HALF, lanes], total_rel[SECOND : SECOND + HALF, lanes]], 0)
             ref[at, 0:D, :] = both.astype(BF)
-            ref[at, D:512, :] = jnp.zeros((512 - D, PER), BF)
+            ref[at, D:TALL, :] = jnp.zeros((TALL - D, PER), BF)
         stores.append(move(ref, hbm))
     for c in range(0, EDGES, wide):
         marks = onehot(lhs_of(keys_ref[0:1, c : c + wide]), LOCAL)
@@ -257,8 +257,8 @@
         out_specs=[anywhere] * 3 + [pl.BlockSpec(memory_space=pltpu.VMEM)],
         out_shape=[
             jax.ShapeDtypeStruct((OWNERS, BACK, PER), BF),
-            jax.ShapeDtypeStruct((4, 512, PER), BF),
-            jax.ShapeDtypeStruct((4, 512, PER), BF),
+            jax.ShapeDtypeStruct((4, TALL, PER), BF),
+            jax.ShapeDtypeStruct((4, TALL, PER), BF),
             jax.ShapeDtypeStruct((D, LOCAL), F32),
         ],
         scratch_shapes=[
@@ -276,8 +276,8 @@
             pltpu.VMEM((BUFFERS, D, CHUNK), F32),
             pltpu.VMEM((BUFFERS, D, CHUNK), F32),
             pltpu.VMEM((TALL, RELP), F32),
-            pltpu.VMEM((4, 512, PER), BF),
-            pltpu.VMEM((4, 512, PER), BF),
+            pltpu.VMEM((4, TALL, PER), BF),
+            pltpu.VMEM((4, TALL, PER), BF),
             pltpu.SemaphoreType.DMA((COPIES,)),
         ],
         compiler_params=pltpu.CompilerParams(vmem_limit_bytes=58 * MIB),
@@ -301,7 +301,7 @@
     n = parts[0].shape[0]
     return pl.pallas_call(
         functools.partial(spread_kernel, axis),
-        out_shape=[jax.ShapeDtypeStruct((n // 4, 32, PER), BF)] * 4,
+        out_shape=[jax.ShapeDtypeStruct((n // 4, TALL, PER), BF)] * 4,
         name="spread",
     )(*parts)
 
@@ -464,14 +464,14 @@
     returned = lax.all_to_all(back, ROW, 0, 0, tiled=True)
     new_lhs, new_lhs_accum = left_update(lhs_t, lhs_accum, lhs_sum)
     new_rhs, new_rhs_accum = right_update(partner, ext_all, returned)
-    pieces = spread("x", [own.reshape(64, 32, PER), other_core(other).reshape(64, 32, PER)])
+    pieces = spread("x", [own, other_core(other)])
     total = add_four([pieces[0]] + [shift(pieces[d], "x", d) for d in (1, 2, 3)])
     total = add_four([total] + [shift(total, "z", d) for d in (1, 2, 3)])
     pieces = [total] + [shift(total, "y", d) for d in (1, 2, 3)]
     pieces, new_lhs, new_rhs = lax.optimization_barrier((pieces, new_lhs, new_rhs))
     total = add_four(pieces)
     pieces = [total] + [shift(total, "x", d) for d in (1, 2, 3)]
-    own = jnp.stack(pieces).reshape(4, 512, PER)
+    own = jnp.stack(pieces).reshape(4, TALL, PER)
     new_rel, new_rel_accum = relation_update(rel_t, rel_accum[None], own, other_core(own))
     return (
         new_lhs.T[None],

time: 164 us -> 162 us (0.988)
  waiting for transfers between devices: 32.4 us -> 29.5 us
    ppermute x27, waiting for transfers between devices: 28.1 us -> 25.8 us  [shift(): return lax.ppermute(value, axis, [(i, i + distance & 3) for i in range(4)])]
    unnamed x27 -> x29, local copies, waits for them, and re-layouts: 4.1 us -> 4.06 us
where the time goes in v5:
time: 162 us; the launch traced here: 161 us
  starting transfers between devices  63.4 us (39%)
  Pallas kernels  39 us (24%)
  waiting for transfers between devices  29.5 us (18%)
  between operations  17.7 us (11%)
  other arithmetic  6.9 us (4%)
  local copies, waits for them, and re-layouts  4.8 us (3%)
    ppermute x27, starting transfers between devices, shift(): return lax.ppermute(value, axis, [(i, i + distance & 3) for i in range(4)])  43.5 us
    ppermute x27, waiting for transfers between devices, shift(): return lax.ppermute(value, axis, [(i, i + distance & 3) for i in range(4)])  25.8 us
    pallas_call x1, Pallas kernels, edges(): pl.pallas_call(edge_kernel, in_specs=[pl.BlockSpec(memory_space=pltpu.SME...  18.9 us
    ppermute x4, starting transfers between devices, other_core(): return lax.ppermute(value, 'core', CORES)  11.4 us
    pallas_call x1, Pallas kernels, make_query(): pl.pallas_call(query_kernel, grid=(STEPS,), in_specs=[pl.BlockSpec((2, CH...  8.58 us
    all_to_all x1, starting transfers between devices, body(): returned = lax.all_to_all(back, ROW, 0, 0, tiled=True)  8.46 us
    pallas_call x1, Pallas kernels, right_update(): pl.pallas_call(right_kernel, grid_spec=pltpu.PrefetchScalarGridSpec(num_s...  4.18 us
    unnamed x29, local copies, waits for them, and re-layouts  4.06 us
  transfers between devices with their start and end apart: 33, of which 17 were waited for; matrix products, arithmetic and copies ran while one was open for 4% of the time, Pallas kernels for 22%

profile of v5, /device:TPU:1, one launch (start us, length us, event | category | flops | bytes accessed | tf_op | source)
XLA Modules:
  0.0 161.3 jit_solution(4320055143730764211)
XLA Ops:
  8.1 1.1 bitcast_convert_fusion
  9.1 2.1 %collective-permute-start = (bf16[400,256]{1,0:T(8,128)(2,1)S(1)}, bf16[400,256]{1,0:T(8,128)(2,1)S(1)}, u32[]{:S(2)}, u32[]{:S(2)}) collective-permute-start(bf16[400,256]{1,0:T(8,128)(2,1)S(1)} %bitcast_convert_fusion), channel_id=1, source_target_pairs={{0,32},{32,64},{64,96},{96,0},{1,33},{33,65},{65,97},{97,1},{2,34}... | collective-permute-start | bytes 614408 | tf_op jit(solution)/shard_map/ppermute | solution.py:397
  11.2 2.5 %collective-permute-start.1 = (bf16[400,256]{1,0:T(8,128)(2,1)S(1)}, bf16[400,256]{1,0:T(8,128)(2,1)S(1)}, u32[]{:S(2)}, u32[]{:S(2)}) collective-permute-start(bf16[400,256]{1,0:T(8,128)(2,1)S(1)} %bitcast_convert_fusion), channel_id=1, source_target_pairs={{0,64},{32,96},{64,0},{96,32},{1,65},{33,97},{65,1},{97,33},{2,66}... | collective-permute-start | bytes 614408 | tf_op jit(solution)/shard_map/ppermute | solution.py:397
  13.7 1.2 collective-permute-start.2
  14.8 1.5 collective-permute-start.3
  17.7 0.7 shift-left_or_fusion
  18.4 0.8 fusion
  19.2 0.5 and_or_fusion.place_ref
  19.7 0.7 broadcast_in_dim.18
  20.4 1.8 %pad_maximum_fusion = f32[408,256]{1,0:T(8,128)} fusion(f32[8,256]{1,0:T(8,128)S(1)} %broadcast_in_dim.18, f32[400,256]{1,0:T(8,128)} %bitcast.52), kind=kLoop, calls=%fused_computation.1 | loop fusion | flops 104448 | bytes 835584 | tf_op jit(solution)/shard_map/concatenate | solution.py:456
  22.9 1.3 collective-permute-start.4
  24.3 0.6 pad_add_fusion
  24.9 0.5 collective-permute-done.4
  25.5 0.5 all-gather.3.cloned.1.call-update
  26.1 3.8 %collective-permute-start.10 = (bf16[400,128]{1,0:T(8,128)(2,1)S(1)}, bf16[400,128]{1,0:T(8,128)(2,1)S(1)}, u32[]{:S(2)}, u32[]{:S(2)}) collective-permute-start(bf16[400,128]{1,0:T(8,128)(2,1)S(1)} %get-tuple-element.48), channel_id=1, source_target_pairs={{0,12},{4,0},{8,4},{12,8},{1,13},{5,1},{9,5},{13,9},{2,14},{6,2},{... | collective-permute-start | bytes 307208 | tf_op jit(solution)/shard_map/ppermute | solution.py:397
  29.9 2.9 %collective-permute-start.5 = (bf16[400,128]{1,0:T(8,128)(2,1)S(1)}, bf16[400,128]{1,0:T(8,128)(2,1)S(1)}, u32[]{:S(2)}, u32[]{:S(2)}) collective-permute-start(bf16[400,128]{1,0:T(8,128)(2,1)S(1)} %get-tuple-element.44), channel_id=1, source_target_pairs={{0,2},{1,3},{2,0},{3,1},{4,6},{5,7},{6,4},{7,5},{8,10},{9,11},{10,... | collective-permute-start | bytes 307208 | tf_op jit(solution)/shard_map/ppermute | solution.py:397
  32.8 0.4 collective-permute-start.6
  33.2 2.3 %collective-permute-start.7 = (bf16[400,128]{1,0:T(8,128)(2,1)S(1)}, bf16[400,128]{1,0:T(8,128)(2,1)S(1)}, u32[]{:S(2)}, u32[]{:S(2)}) collective-permute-start(bf16[400,128]{1,0:T(8,128)(2,1)S(1)} %get-tuple-element.44), channel_id=1, source_target_pairs={{0,3},{1,0},{2,1},{3,2},{4,7},{5,4},{6,5},{7,6},{8,11},{9,8},{10,9... | collective-permute-start | bytes 307208 | tf_op jit(solution)/shard_map/ppermute | solution.py:397
  35.5 0.7 collective-permute-start.9
  36.2 1.3 collective-permute-done.6
  37.5 0.3 collective-permute-done.7
  37.8 2.8 %collective-permute-done.8 = bf16[400,128]{1,0:T(8,128)(2,1)S(1)} collective-permute-done((bf16[400,128]{1,0:T(8,128)(2,1)S(1)}, bf16[400,128]{1,0:T(8,128)(2,1)S(1)}, u32[]{:S(2)}, u32[]{:S(2)}) %collective-permute-start.8) | collective-permute-done | bytes 102432 | tf_op jit(solution)/shard_map/ppermute | solution.py:397
  40.6 1.2 collective-permute-done.9
  42.0 2.6 %collective-permute-start.15 = (bf16[4,400,128]{2,1,0:T(8,128)(2,1)S(1)}, bf16[4,400,128]{2,1,0:T(8,128)(2,1)S(1)}, u32[]{:S(2)}, u32[]{:S(2)}) collective-permute-start(bf16[4,400,128]{2,1,0:T(8,128)(2,1)S(1)} %pad_maximum_fusion.2.b0), channel_id=1, source_target_pairs={{0,2},{1,3},{2,0},{3,1},{4,6},{5,7},{6,4},{7,5},{8,10},{9,11},{10,... | collective-permute-start | bytes 1228808 | tf_op jit(solution)/shard_map/ppermute | solution.py:397
  44.5 0.8 collective-permute-start.16
  45.5 1.1 collective-permute-start.12
  46.6 5.3 %collective-permute-done.14.b1 = bf16[4,400,128]{2,1,0:T(8,128)(2,1)S(1)} collective-permute-done((bf16[4,400,128]{2,1,0:T(8,128)(2,1)S(1)}, bf16[4,400,128]{2,1,0:T(8,128)(2,1)S(1)}, u32[]{:S(2)}, u32[]{:S(2)}) %collective-permute-start.14) | collective-permute-done | bytes 409632 | tf_op jit(solution)/shard_map/ppermute | solution.py:397
  51.9 1.8 %collective-permute-start.13 = (bf16[4,400,128]{2,1,0:T(8,128)(2,1)S(1)}, bf16[4,400,128]{2,1,0:T(8,128)(2,1)S(1)}, u32[]{:S(2)}, u32[]{:S(2)}) collective-permute-start(bf16[4,400,128]{2,1,0:T(8,128)(2,1)S(1)} %pad_maximum_fusion.1.a0), channel_id=1, source_target_pairs={{0,12},{4,0},{8,4},{12,8},{1,13},{5,1},{9,5},{13,9},{2,14},{6,2},{... | collective-permute-start | bytes 1228808 | tf_op jit(solution)/shard_map/ppermute | solution.py:397
  53.7 8.6 %make_query.1 = (bf16[416,2048]{1,0:T(8,128)(2,1)}, bf16[416,2048]{1,0:T(8,128)(2,1)}, bf16[400,2048]{1,0:T(8,128)(2,1)}) custom-call(s32[2,2048]{1,0:T(2,128)} %sort.9.cloned.1.call-done.keys_ref, f32[400,256]{1,0:T(8,128)} %bitcast.58, f32[400,1000]{1,0:T(8,128)} %bitcast.53), custom_call_target="tpu_custom_call" | custom-call | flops 5000000000 | bytes 10000000 | tf_op jit(solution)/shard_map/make_query/pallas_call | solution.py:85
  62.3 0.6 collective-permute-done.16.b3
  62.9 0.2 collective-permute-done.13.a3
  63.1 0.6 copy-done.10
  64.1 18.9 %edges.1 = (bf16[16,624,128]{2,1,0:T(8,128)(2,1)}, bf16[4,416,128]{2,1,0:T(8,128)(2,1)}, bf16[4,416,128]{2,1,0:T(8,128)(2,1)}, f32[400,256]{1,0:T(8,128)}) custom-call(s32[16]{0:T(128)} %and_or_fusion.place_ref, s32[2,2048]{1,0:T(2,128)} %sort.9.cloned.1.call-done.keys_ref, bf16[4,400,128]{2,1,0:T(8,128)(2,1)} %copy-done.6, bf16[4,400,128]{2,1,0:T(8,128)(2,1)} %copy-done.11, ...), custom_call_target="tpu_custom_call" | custom-call | flops 8000000000 | bytes 20000000 | tf_op jit(solution)/shard_map/edges/pallas_call | solution.py:254
  83.0 8.5 %all-to-all-start = ((bf16[16,624,128]{2,1,0:T(8,128)(2,1)}), bf16[16,624,128]{2,1,0:T(8,128)(2,1)S(1)}, u32[]{:S(2)}, u32[]{:S(2)}) async-start(bf16[16,624,128]{2,1,0:T(8,128)(2,1)} %get-tuple-element.64), calls=%async_computation | async-start | bytes 5111808 | tf_op jit(solution)/shard_map/all_to_all | solution.py:464
  91.4 6.1 %collective-permute-start.17 = (bf16[4,416,128]{2,1,0:T(8,128)(2,1)S(1)}, bf16[4,416,128]{2,1,0:T(8,128)(2,1)S(1)}, u32[]{:S(2)}, u32[]{:S(2)}) collective-permute-start(bf16[4,416,128]{2,1,0:T(8,128)(2,1)S(1)} %copy-done.7), channel_id=1, source_target_pairs={{0,16},{16,0},{1,17},{17,1},{2,18},{18,2},{3,19},{19,3},{4,20},{20... | collective-permute-start | bytes 1277960 | tf_op jit(solution)/shard_map/ppermute | solution.py:401
  97.5 1.4 collective-permute-done.17.refs_1_
  98.9 0.8 copy-done.4
  99.7 1.9 %spread.1 = (bf16[1,416,128]{2,1,0:T(8,128)(2,1)}, bf16[1,416,128]{2,1,0:T(8,128)(2,1)}, bf16[1,416,128]{2,1,0:T(8,128)(2,1)}, bf16[1,416,128]{2,1,0:T(8,128)(2,1)}) custom-call(bf16[4,416,128]{2,1,0:T(8,128)(2,1)} %get-tuple-element.55.refs_0_, bf16[4,416,128]{2,1,0:T(8,128)(2,1)} %copy-done.4), custom_call_target="tpu_custom_call" | custom-call | tf_op jit(solution)/shard_map/spread/pallas_call | solution.py:302
  101.6 2.4 %collective-permute-start.18 = (bf16[1,416,128]{2,1,0:T(8,128)(2,1)}, bf16[1,416,128]{2,1,0:T(8,128)(2,1)S(1)}, u32[]{:S(2)}, u32[]{:S(2)}) collective-permute-start(bf16[1,416,128]{2,1,0:T(8,128)(2,1)} %get-tuple-element.58), channel_id=1, source_target_pairs={{0,64},{32,96},{64,0},{96,32},{1,65},{33,97},{65,1},{97,33},{2,66}... | collective-permute-start | bytes 319496 | tf_op jit(solution)/shard_map/ppermute | solution.py:397
  104.1 2.5 %collective-permute-start.20 = (bf16[1,416,128]{2,1,0:T(8,128)(2,1)}, bf16[1,416,128]{2,1,0:T(8,128)(2,1)S(1)}, u32[]{:S(2)}, u32[]{:S(2)}) collective-permute-start(bf16[1,416,128]{2,1,0:T(8,128)(2,1)} %get-tuple-element.60), channel_id=1, source_target_pairs={{0,96},{32,0},{64,32},{96,64},{1,97},{33,1},{65,33},{97,65},{2,98}... | collective-permute-start | bytes 319496 | tf_op jit(solution)/shard_map/ppermute | solution.py:397
  106.6 0.8 collective-permute-done.18
  107.5 2.6 %collective-permute-done.19 = bf16[1,416,128]{2,1,0:T(8,128)(2,1)S(1)} collective-permute-done((bf16[1,416,128]{2,1,0:T(8,128)(2,1)}, bf16[1,416,128]{2,1,0:T(8,128)(2,1)S(1)}, u32[]{:S(2)}, u32[]{:S(2)}) %collective-permute-start.19) | collective-permute-done | bytes 106528 | tf_op jit(solution)/shard_map/ppermute | solution.py:397
  110.1 1.0 add_convert_fusion.2
  111.1 3.2 %collective-permute-start.21 = (bf16[1,416,128]{2,1,0:T(8,128)(2,1)S(1)}, bf16[1,416,128]{2,1,0:T(8,128)(2,1)S(1)}, u32[]{:S(2)}, u32[]{:S(2)}) collective-permute-start(bf16[1,416,128]{2,1,0:T(8,128)(2,1)S(1)} %add_convert_fusion.2), channel_id=1, source_target_pairs={{0,8},{4,12},{8,0},{12,4},{1,9},{5,13},{9,1},{13,5},{2,10},{6,14},... | collective-permute-start | bytes 319496 | tf_op jit(solution)/shard_map/ppermute | solution.py:397
  114.2 0.3 collective-permute-start.22
  114.5 2.4 %collective-permute-start.23 = (bf16[1,416,128]{2,1,0:T(8,128)(2,1)S(1)}, bf16[1,416,128]{2,1,0:T(8,128)(2,1)S(1)}, u32[]{:S(2)}, u32[]{:S(2)}) collective-permute-start(bf16[1,416,128]{2,1,0:T(8,128)(2,1)S(1)} %add_convert_fusion.2), channel_id=1, source_target_pairs={{0,12},{4,0},{8,4},{12,8},{1,13},{5,1},{9,5},{13,9},{2,14},{6,2},{... | collective-permute-start | bytes 319496 | tf_op jit(solution)/shard_map/ppermute | solution.py:397
  116.9 2.0 %left_update.1 = (f32[400,256]{1,0:T(8,128)}, f32[1,256]{1,0:T(1,128)}) custom-call(f32[400,256]{1,0:T(8,128)} %bitcast.59, f32[1,256]{1,0:T(1,128)} %accum_ref.1, f32[400,256]{1,0:T(8,128)} %get-tuple-element.61.grad_ref), custom_call_target="tpu_custom_call" | custom-call | tf_op jit(solution)/shard_map/left_update/pallas_call | solution.py:366
  118.9 4.0 %collective-permute-done.21 = bf16[1,416,128]{2,1,0:T(8,128)(2,1)S(1)} collective-permute-done((bf16[1,416,128]{2,1,0:T(8,128)(2,1)S(1)}, bf16[1,416,128]{2,1,0:T(8,128)(2,1)S(1)}, u32[]{:S(2)}, u32[]{:S(2)}) %collective-permute-start.21) | collective-permute-done | bytes 106528 | tf_op jit(solution)/shard_map/ppermute | solution.py:397
  122.9 3.3 %collective-permute-done.22 = bf16[1,416,128]{2,1,0:T(8,128)(2,1)S(1)} collective-permute-done((bf16[1,416,128]{2,1,0:T(8,128)(2,1)S(1)}, bf16[1,416,128]{2,1,0:T(8,128)(2,1)S(1)}, u32[]{:S(2)}, u32[]{:S(2)}) %collective-permute-start.22) | collective-permute-done | bytes 106528 | tf_op jit(solution)/shard_map/ppermute | solution.py:397
  126.3 2.9 %collective-permute-start.24 = (bf16[1,416,128]{2,1,0:T(8,128)(2,1)S(1)}, bf16[1,416,128]{2,1,0:T(8,128)(2,1)S(1)}, u32[]{:S(2)}, u32[]{:S(2)}) collective-permute-start(bf16[1,416,128]{2,1,0:T(8,128)(2,1)S(1)} %add_convert_fusion.1), channel_id=1, source_target_pairs={{0,1},{1,2},{2,3},{3,0},{4,5},{5,6},{6,7},{7,4},{8,9},{9,10},{10,1... | collective-permute-start | bytes 319496 | tf_op jit(solution)/shard_map/ppermute | solution.py:397
  129.1 1.9 %collective-permute-start.25 = (bf16[1,416,128]{2,1,0:T(8,128)(2,1)S(1)}, bf16[1,416,128]{2,1,0:T(8,128)(2,1)S(1)}, u32[]{:S(2)}, u32[]{:S(2)}) collective-permute-start(bf16[1,416,128]{2,1,0:T(8,128)(2,1)S(1)} %add_convert_fusion.1), channel_id=1, source_target_pairs={{0,2},{1,3},{2,0},{3,1},{4,6},{5,7},{6,4},{7,5},{8,10},{9,11},{10,... | collective-permute-start | bytes 319496 | tf_op jit(solution)/shard_map/ppermute | solution.py:397
  131.1 1.4 collective-permute-start.26
  132.4 1.5 copy-done.1
  133.9 4.2 %right_update.1 = (f32[400,256]{1,0:T(8,128)}, f32[1,256]{1,0:T(1,128)}) custom-call(s32[1]{0:T(128)S(6)} %copy.21.partner_ref, f32[8,408,256]{2,1,0:T(8,128)} %bitcast.73, bf16[16,624,128]{2,1,0:T(8,128)(2,1)} %copy-done.1), custom_call_target="tpu_custom_call" | custom-call | flops 2000000000 | bytes 5000000 | tf_op jit(solution)/shard_map/right_update/pallas_call | solution.py:336
  138.2 1.1 collective-permute-start.27
  139.3 2.1 %collective-permute-start.28 = (bf16[1,416,128]{2,1,0:T(8,128)(2,1)S(1)}, bf16[1,416,128]{2,1,0:T(8,128)(2,1)S(1)}, u32[]{:S(2)}, u32[]{:S(2)}) collective-permute-start(bf16[1,416,128]{2,1,0:T(8,128)(2,1)S(1)} %add_convert_fusion), channel_id=1, source_target_pairs={{0,64},{32,96},{64,0},{96,32},{1,65},{33,97},{65,1},{97,33},{2,66}... | collective-permute-start | bytes 319496 | tf_op jit(solution)/shard_map/ppermute | solution.py:397
  141.4 1.1 collective-permute-start.29
  142.5 0.5 collective-permute-done.27
  143.0 2.0 %collective-permute-done.28 = bf16[1,416,128]{2,1,0:T(8,128)(2,1)S(1)} collective-permute-done((bf16[1,416,128]{2,1,0:T(8,128)(2,1)S(1)}, bf16[1,416,128]{2,1,0:T(8,128)(2,1)S(1)}, u32[]{:S(2)}, u32[]{:S(2)}) %collective-permute-start.28) | collective-permute-done | bytes 106528 | tf_op jit(solution)/shard_map/ppermute | solution.py:397
  145.0 0.7 collective-permute-done.29
  145.8 2.5 %collective-permute-start.30 = (bf16[4,416,128]{2,1,0:T(8,128)(2,1)S(1)}, bf16[4,416,128]{2,1,0:T(8,128)(2,1)S(1)}, u32[]{:S(2)}, u32[]{:S(2)}) collective-permute-start(bf16[4,416,128]{2,1,0:T(8,128)(2,1)S(1)} %maximum_bitcast_fusion.own_ref), channel_id=1, source_target_pairs={{0,16},{16,0},{1,17},{17,1},{2,18},{18,2},{3,19},{19,3},{4,20},{20... | collective-permute-start | bytes 1277960 | tf_op jit(solution)/shard_map/ppermute | solution.py:401
  148.3 1.4 collective-permute-done.30.other_ref
  149.7 0.8 copy-done.3
  150.5 3.4 %relation_update.1 = (f32[400,1000]{1,0:T(8,128)}, f32[1,1000]{1,0:T(1,128)}) custom-call(f32[400,1000]{1,0:T(8,128)} %bitcast.54, f32[1,1000]{1,0:T(1,128)} %bitcast.71, bf16[4,416,128]{2,1,0:T(8,128)(2,1)} %copy-done.2, bf16[4,416,128]{2,1,0:T(8,128)(2,1)} %copy-done.3), custom_call_target="tpu_custom_call" | custom-call | tf_op jit(solution)/shard_map/relation_update/pallas_call | solution.py:384
  (57 shorter events, 1.4 us)
Async XLA Ops:
  8.0 14.9 %copy-start = (f32[1,256,400]{1,2,0:T(8,128)S(1)}, f32[1,256,400]{1,2,0:T(8,128)}, u32[]{:S(2)}) copy-start(f32[1,256,400]{1,2,0:T(8,128)} %param.14) | copy-start | bytes 1228804
  8.0 45.6 %sort.9.cloned.1.call-start = ((), (), s32[]{:S(2)}) async-start(), calls=%async_computation.2 | async-start | bytes 49184 | tf_op jit(solution)/shard_map/sort | solution.py:460
  9.1 13.7 %collective-permute-start = (bf16[400,256]{1,0:T(8,128)(2,1)S(1)}, bf16[400,256]{1,0:T(8,128)(2,1)S(1)}, u32[]{:S(2)}, u32[]{:S(2)}) collective-permute-start(bf16[400,256]{1,0:T(8,128)(2,1)S(1)} %bitcast_convert_fusion), channel_id=1, source_target_pairs={{0,32},{32,64},{64,96},{96,0},{1,33},{33,65},{65,97},{97,1},{2,34}... | collective-permute-start | bytes 614408 | tf_op jit(solution)/shard_map/ppermute | solution.py:397
  11.2 11.6 %collective-permute-start.1 = (bf16[400,256]{1,0:T(8,128)(2,1)S(1)}, bf16[400,256]{1,0:T(8,128)(2,1)S(1)}, u32[]{:S(2)}, u32[]{:S(2)}) collective-permute-start(bf16[400,256]{1,0:T(8,128)(2,1)S(1)} %bitcast_convert_fusion), channel_id=1, source_target_pairs={{0,64},{32,96},{64,0},{96,32},{1,65},{33,97},{65,1},{97,33},{2,66}... | collective-permute-start | bytes 614408 | tf_op jit(solution)/shard_map/ppermute | solution.py:397
  13.7 9.2 %collective-permute-start.2 = (bf16[400,256]{1,0:T(8,128)(2,1)S(1)}, bf16[400,256]{1,0:T(8,128)(2,1)S(1)}, u32[]{:S(2)}, u32[]{:S(2)}) collective-permute-start(bf16[400,256]{1,0:T(8,128)(2,1)S(1)} %bitcast_convert_fusion), channel_id=1, source_target_pairs={{0,96},{32,0},{64,32},{96,64},{1,97},{33,1},{65,33},{97,65},{2,98}... | collective-permute-start | bytes 614408 | tf_op jit(solution)/shard_map/ppermute | solution.py:397
  14.8 7.4 %collective-permute-start.3 = (s32[1]{0:T(128)}, s32[1]{0:T(128)}, u32[]{:S(2)}, u32[]{:S(2)}) collective-permute-start(s32[1]{0:T(128)} %param.18), channel_id=1, source_target_pairs={{0,16},{16,0},{1,17},{17,1},{2,18},{18,2},{3,19},{19,3},{4,20},{20... | collective-permute-start | bytes 20 | tf_op jit(solution)/shard_map/ppermute | solution.py:401
  22.9 2.4 %collective-permute-start.4 = (bf16[400,256]{1,0:T(8,128)(2,1)S(1)}, bf16[400,256]{1,0:T(8,128)(2,1)S(1)}, u32[]{:S(2)}, u32[]{:S(2)}) collective-permute-start(bf16[400,256]{1,0:T(8,128)(2,1)S(1)} %select_select_fusion), channel_id=1, source_target_pairs={{0,16},{16,0},{1,17},{17,1},{2,18},{18,2},{3,19},{19,3},{4,20},{20... | collective-permute-start | bytes 614408 | tf_op jit(solution)/shard_map/ppermute | solution.py:401
  25.4 107.0 %all-gather.3.cloned.1.call-start = ((), (), s32[]{:S(2)}) async-start(), calls=%async_computation.1 | async-start | bytes 3760128 | tf_op jit(solution)/shard_map/all_gather | solution.py:458
  26.1 9.4 %collective-permute-start.10 = (bf16[400,128]{1,0:T(8,128)(2,1)S(1)}, bf16[400,128]{1,0:T(8,128)(2,1)S(1)}, u32[]{:S(2)}, u32[]{:S(2)}) collective-permute-start(bf16[400,128]{1,0:T(8,128)(2,1)S(1)} %get-tuple-element.48), channel_id=1, source_target_pairs={{0,12},{4,0},{8,4},{12,8},{1,13},{5,1},{9,5},{13,9},{2,14},{6,2},{... | collective-permute-start | bytes 307208 | tf_op jit(solution)/shard_map/ppermute | solution.py:397
  29.9 6.3 %collective-permute-start.5 = (bf16[400,128]{1,0:T(8,128)(2,1)S(1)}, bf16[400,128]{1,0:T(8,128)(2,1)S(1)}, u32[]{:S(2)}, u32[]{:S(2)}) collective-permute-start(bf16[400,128]{1,0:T(8,128)(2,1)S(1)} %get-tuple-element.44), channel_id=1, source_target_pairs={{0,2},{1,3},{2,0},{3,1},{4,6},{5,7},{6,4},{7,5},{8,10},{9,11},{10,... | collective-permute-start | bytes 307208 | tf_op jit(solution)/shard_map/ppermute | solution.py:397
  32.8 4.7 %collective-permute-start.6 = (bf16[400,128]{1,0:T(8,128)(2,1)S(1)}, bf16[400,128]{1,0:T(8,128)(2,1)S(1)}, u32[]{:S(2)}, u32[]{:S(2)}) collective-permute-start(bf16[400,128]{1,0:T(8,128)(2,1)S(1)} %get-tuple-element.44), channel_id=1, source_target_pairs={{0,1},{1,2},{2,3},{3,0},{4,5},{5,6},{6,7},{7,4},{8,9},{9,10},{10,1... | collective-permute-start | bytes 307208 | tf_op jit(solution)/shard_map/ppermute | solution.py:397
  33.2 4.6 %collective-permute-start.7 = (bf16[400,128]{1,0:T(8,128)(2,1)S(1)}, bf16[400,128]{1,0:T(8,128)(2,1)S(1)}, u32[]{:S(2)}, u32[]{:S(2)}) collective-permute-start(bf16[400,128]{1,0:T(8,128)(2,1)S(1)} %get-tuple-element.44), channel_id=1, source_target_pairs={{0,3},{1,0},{2,1},{3,2},{4,7},{5,4},{6,5},{7,6},{8,11},{9,8},{10,9... | collective-permute-start | bytes 307208 | tf_op jit(solution)/shard_map/ppermute | solution.py:397
  35.5 5.1 %collective-permute-start.8 = (bf16[400,128]{1,0:T(8,128)(2,1)S(1)}, bf16[400,128]{1,0:T(8,128)(2,1)S(1)}, u32[]{:S(2)}, u32[]{:S(2)}) collective-permute-start(bf16[400,128]{1,0:T(8,128)(2,1)S(1)} %get-tuple-element.48), channel_id=1, source_target_pairs={{0,8},{4,12},{8,0},{12,4},{1,9},{5,13},{9,1},{13,5},{2,10},{6,14},... | collective-permute-start | bytes 307208 | tf_op jit(solution)/shard_map/ppermute | solution.py:397
  35.5 6.4 %collective-permute-start.9 = (bf16[400,128]{1,0:T(8,128)(2,1)S(1)}, bf16[400,128]{1,0:T(8,128)(2,1)S(1)}, u32[]{:S(2)}, u32[]{:S(2)}) collective-permute-start(bf16[400,128]{1,0:T(8,128)(2,1)S(1)} %get-tuple-element.48), channel_id=1, source_target_pairs={{0,4},{4,8},{8,12},{12,0},{1,5},{5,9},{9,13},{13,1},{2,6},{6,10},{... | collective-permute-start | bytes 307208 | tf_op jit(solution)/shard_map/ppermute | solution.py:397
  41.9 20.4 %copy-start.5 = (bf16[4,400,128]{2,1,0:T(8,128)(2,1)}, bf16[4,400,128]{2,1,0:T(8,128)(2,1)S(1)}, u32[]{:S(2)}) copy-start(bf16[4,400,128]{2,1,0:T(8,128)(2,1)S(1)} %pad_maximum_fusion.2.b0) | copy-start | bytes 1228804
  41.9 10.0 %collective-permute-start.14 = (bf16[4,400,128]{2,1,0:T(8,128)(2,1)S(1)}, bf16[4,400,128]{2,1,0:T(8,128)(2,1)S(1)}, u32[]{:S(2)}, u32[]{:S(2)}) collective-permute-start(bf16[4,400,128]{2,1,0:T(8,128)(2,1)S(1)} %pad_maximum_fusion.2.b0), channel_id=1, source_target_pairs={{0,1},{1,2},{2,3},{3,0},{4,5},{5,6},{6,7},{7,4},{8,9},{9,10},{10,1... | collective-permute-start | bytes 1228808 | tf_op jit(solution)/shard_map/ppermute | solution.py:397
  42.0 20.3 %collective-permute-start.15 = (bf16[4,400,128]{2,1,0:T(8,128)(2,1)S(1)}, bf16[4,400,128]{2,1,0:T(8,128)(2,1)S(1)}, u32[]{:S(2)}, u32[]{:S(2)}) collective-permute-start(bf16[4,400,128]{2,1,0:T(8,128)(2,1)S(1)} %pad_maximum_fusion.2.b0), channel_id=1, source_target_pairs={{0,2},{1,3},{2,0},{3,1},{4,6},{5,7},{6,4},{7,5},{8,10},{9,11},{10,... | collective-permute-start | bytes 1228808 | tf_op jit(solution)/shard_map/ppermute | solution.py:397
  44.5 18.4 %collective-permute-start.16 = (bf16[4,400,128]{2,1,0:T(8,128)(2,1)S(1)}, bf16[4,400,128]{2,1,0:T(8,128)(2,1)S(1)}, u32[]{:S(2)}, u32[]{:S(2)}) collective-permute-start(bf16[4,400,128]{2,1,0:T(8,128)(2,1)S(1)} %pad_maximum_fusion.2.b0), channel_id=1, source_target_pairs={{0,3},{1,0},{2,1},{3,2},{4,7},{5,4},{6,5},{7,6},{8,11},{9,8},{10,9... | collective-permute-start | bytes 1228808 | tf_op jit(solution)/shard_map/ppermute | solution.py:397
  45.4 16.9 %copy-start.6 = (bf16[4,400,128]{2,1,0:T(8,128)(2,1)}, bf16[4,400,128]{2,1,0:T(8,128)(2,1)S(1)}, u32[]{:S(2)}) copy-start(bf16[4,400,128]{2,1,0:T(8,128)(2,1)S(1)} %pad_maximum_fusion.1.a0) | copy-start | bytes 1228804
  45.4 17.5 %collective-permute-start.11 = (bf16[4,400,128]{2,1,0:T(8,128)(2,1)S(1)}, bf16[4,400,128]{2,1,0:T(8,128)(2,1)S(1)}, u32[]{:S(2)}, u32[]{:S(2)}) collective-permute-start(bf16[4,400,128]{2,1,0:T(8,128)(2,1)S(1)} %pad_maximum_fusion.1.a0), channel_id=1, source_target_pairs={{0,4},{4,8},{8,12},{12,0},{1,5},{5,9},{9,13},{13,1},{2,6},{6,10},{... | collective-permute-start | bytes 1228808 | tf_op jit(solution)/shard_map/ppermute | solution.py:397
  45.5 17.5 %collective-permute-start.12 = (bf16[4,400,128]{2,1,0:T(8,128)(2,1)S(1)}, bf16[4,400,128]{2,1,0:T(8,128)(2,1)S(1)}, u32[]{:S(2)}, u32[]{:S(2)}) collective-permute-start(bf16[4,400,128]{2,1,0:T(8,128)(2,1)S(1)} %pad_maximum_fusion.1.a0), channel_id=1, source_target_pairs={{0,8},{4,12},{8,0},{12,4},{1,9},{5,13},{9,1},{13,5},{2,10},{6,14},... | collective-permute-start | bytes 1228808 | tf_op jit(solution)/shard_map/ppermute | solution.py:397
  51.9 10.4 %copy-start.8 = (bf16[4,400,128]{2,1,0:T(8,128)(2,1)}, bf16[4,400,128]{2,1,0:T(8,128)(2,1)S(1)}, u32[]{:S(2)}) copy-start(bf16[4,400,128]{2,1,0:T(8,128)(2,1)S(1)} %collective-permute-done.14.b1) | copy-start | bytes 1228804
  51.9 11.2 %collective-permute-start.13 = (bf16[4,400,128]{2,1,0:T(8,128)(2,1)S(1)}, bf16[4,400,128]{2,1,0:T(8,128)(2,1)S(1)}, u32[]{:S(2)}, u32[]{:S(2)}) collective-permute-start(bf16[4,400,128]{2,1,0:T(8,128)(2,1)S(1)} %pad_maximum_fusion.1.a0), channel_id=1, source_target_pairs={{0,12},{4,0},{8,4},{12,8},{1,13},{5,1},{9,5},{13,9},{2,14},{6,2},{... | collective-permute-start | bytes 1228808 | tf_op jit(solution)/shard_map/ppermute | solution.py:397
  62.3 0.8 copy-start.9
  62.9 0.8 copy-start.10
  62.9 0.9 copy-start.11
  62.9 1.0 copy-start.12
  63.1 1.0 copy-start.13
  83.0 8.5 %copy-start.7 = (bf16[4,416,128]{2,1,0:T(8,128)(2,1)S(1)}, bf16[4,416,128]{2,1,0:T(8,128)(2,1)}, u32[]{:S(2)}) copy-start(bf16[4,416,128]{2,1,0:T(8,128)(2,1)} %get-tuple-element.56) | copy-start | bytes 1277956
  83.0 49.5 %all-to-all-start = ((bf16[16,624,128]{2,1,0:T(8,128)(2,1)}), bf16[16,624,128]{2,1,0:T(8,128)(2,1)S(1)}, u32[]{:S(2)}, u32[]{:S(2)}) async-start(bf16[16,624,128]{2,1,0:T(8,128)(2,1)} %get-tuple-element.64), calls=%async_computation | async-start | bytes 5111808 | tf_op jit(solution)/shard_map/all_to_all | solution.py:464
  91.4 7.5 %collective-permute-start.17 = (bf16[4,416,128]{2,1,0:T(8,128)(2,1)S(1)}, bf16[4,416,128]{2,1,0:T(8,128)(2,1)S(1)}, u32[]{:S(2)}, u32[]{:S(2)}) collective-permute-start(bf16[4,416,128]{2,1,0:T(8,128)(2,1)S(1)} %copy-done.7), channel_id=1, source_target_pairs={{0,16},{16,0},{1,17},{17,1},{2,18},{18,2},{3,19},{19,3},{4,20},{20... | collective-permute-start | bytes 1277960 | tf_op jit(solution)/shard_map/ppermute | solution.py:401
  98.9 0.8 copy-start.4
  101.6 5.9 %collective-permute-start.18 = (bf16[1,416,128]{2,1,0:T(8,128)(2,1)}, bf16[1,416,128]{2,1,0:T(8,128)(2,1)S(1)}, u32[]{:S(2)}, u32[]{:S(2)}) collective-permute-start(bf16[1,416,128]{2,1,0:T(8,128)(2,1)} %get-tuple-element.58), channel_id=1, source_target_pairs={{0,64},{32,96},{64,0},{96,32},{1,65},{33,97},{65,1},{97,33},{2,66}... | collective-permute-start | bytes 319496 | tf_op jit(solution)/shard_map/ppermute | solution.py:397
  104.0 6.1 %collective-permute-start.19 = (bf16[1,416,128]{2,1,0:T(8,128)(2,1)}, bf16[1,416,128]{2,1,0:T(8,128)(2,1)S(1)}, u32[]{:S(2)}, u32[]{:S(2)}) collective-permute-start(bf16[1,416,128]{2,1,0:T(8,128)(2,1)} %get-tuple-element.59), channel_id=1, source_target_pairs={{0,32},{32,64},{64,96},{96,0},{1,33},{33,65},{65,97},{97,1},{2,34}... | collective-permute-start | bytes 319496 | tf_op jit(solution)/shard_map/ppermute | solution.py:397
  104.1 6.0 %collective-permute-start.20 = (bf16[1,416,128]{2,1,0:T(8,128)(2,1)}, bf16[1,416,128]{2,1,0:T(8,128)(2,1)S(1)}, u32[]{:S(2)}, u32[]{:S(2)}) collective-permute-start(bf16[1,416,128]{2,1,0:T(8,128)(2,1)} %get-tuple-element.60), channel_id=1, source_target_pairs={{0,96},{32,0},{64,32},{96,64},{1,97},{33,1},{65,33},{97,65},{2,98}... | collective-permute-start | bytes 319496 | tf_op jit(solution)/shard_map/ppermute | solution.py:397
  111.1 11.9 %collective-permute-start.21 = (bf16[1,416,128]{2,1,0:T(8,128)(2,1)S(1)}, bf16[1,416,128]{2,1,0:T(8,128)(2,1)S(1)}, u32[]{:S(2)}, u32[]{:S(2)}) collective-permute-start(bf16[1,416,128]{2,1,0:T(8,128)(2,1)S(1)} %add_convert_fusion.2), channel_id=1, source_target_pairs={{0,8},{4,12},{8,0},{12,4},{1,9},{5,13},{9,1},{13,5},{2,10},{6,14},... | collective-permute-start | bytes 319496 | tf_op jit(solution)/shard_map/ppermute | solution.py:397
  114.2 12.0 %collective-permute-start.22 = (bf16[1,416,128]{2,1,0:T(8,128)(2,1)S(1)}, bf16[1,416,128]{2,1,0:T(8,128)(2,1)S(1)}, u32[]{:S(2)}, u32[]{:S(2)}) collective-permute-start(bf16[1,416,128]{2,1,0:T(8,128)(2,1)S(1)} %add_convert_fusion.2), channel_id=1, source_target_pairs={{0,4},{4,8},{8,12},{12,0},{1,5},{5,9},{9,13},{13,1},{2,6},{6,10},{... | collective-permute-start | bytes 319496 | tf_op jit(solution)/shard_map/ppermute | solution.py:397
  114.5 11.7 %collective-permute-start.23 = (bf16[1,416,128]{2,1,0:T(8,128)(2,1)S(1)}, bf16[1,416,128]{2,1,0:T(8,128)(2,1)S(1)}, u32[]{:S(2)}, u32[]{:S(2)}) collective-permute-start(bf16[1,416,128]{2,1,0:T(8,128)(2,1)S(1)} %add_convert_fusion.2), channel_id=1, source_target_pairs={{0,12},{4,0},{8,4},{12,8},{1,13},{5,1},{9,5},{13,9},{2,14},{6,2},{... | collective-permute-start | bytes 319496 | tf_op jit(solution)/shard_map/ppermute | solution.py:397
  126.3 11.8 %collective-permute-start.24 = (bf16[1,416,128]{2,1,0:T(8,128)(2,1)S(1)}, bf16[1,416,128]{2,1,0:T(8,128)(2,1)S(1)}, u32[]{:S(2)}, u32[]{:S(2)}) collective-permute-start(bf16[1,416,128]{2,1,0:T(8,128)(2,1)S(1)} %add_convert_fusion.1), channel_id=1, source_target_pairs={{0,1},{1,2},{2,3},{3,0},{4,5},{5,6},{6,7},{7,4},{8,9},{9,10},{10,1... | collective-permute-start | bytes 319496 | tf_op jit(solution)/shard_map/ppermute | solution.py:397
  129.1 9.0 %collective-permute-start.25 = (bf16[1,416,128]{2,1,0:T(8,128)(2,1)S(1)}, bf16[1,416,128]{2,1,0:T(8,128)(2,1)S(1)}, u32[]{:S(2)}, u32[]{:S(2)}) collective-permute-start(bf16[1,416,128]{2,1,0:T(8,128)(2,1)S(1)} %add_convert_fusion.1), channel_id=1, source_target_pairs={{0,2},{1,3},{2,0},{3,1},{4,6},{5,7},{6,4},{7,5},{8,10},{9,11},{10,... | collective-permute-start | bytes 319496 | tf_op jit(solution)/shard_map/ppermute | solution.py:397
  131.1 7.1 %collective-permute-start.26 = (bf16[1,416,128]{2,1,0:T(8,128)(2,1)S(1)}, bf16[1,416,128]{2,1,0:T(8,128)(2,1)S(1)}, u32[]{:S(2)}, u32[]{:S(2)}) collective-permute-start(bf16[1,416,128]{2,1,0:T(8,128)(2,1)S(1)} %add_convert_fusion.1), channel_id=1, source_target_pairs={{0,3},{1,0},{2,1},{3,2},{4,7},{5,4},{6,5},{7,6},{8,11},{9,8},{10,9... | collective-permute-start | bytes 319496 | tf_op jit(solution)/shard_map/ppermute | solution.py:397
  132.4 1.5 copy-start.1
  138.2 4.8 %collective-permute-start.27 = (bf16[1,416,128]{2,1,0:T(8,128)(2,1)S(1)}, bf16[1,416,128]{2,1,0:T(8,128)(2,1)S(1)}, u32[]{:S(2)}, u32[]{:S(2)}) collective-permute-start(bf16[1,416,128]{2,1,0:T(8,128)(2,1)S(1)} %add_convert_fusion), channel_id=1, source_target_pairs={{0,32},{32,64},{64,96},{96,0},{1,33},{33,65},{65,97},{97,1},{2,34}... | collective-permute-start | bytes 319496 | tf_op jit(solution)/shard_map/ppermute | solution.py:397
  139.3 5.7 %collective-permute-start.28 = (bf16[1,416,128]{2,1,0:T(8,128)(2,1)S(1)}, bf16[1,416,128]{2,1,0:T(8,128)(2,1)S(1)}, u32[]{:S(2)}, u32[]{:S(2)}) collective-permute-start(bf16[1,416,128]{2,1,0:T(8,128)(2,1)S(1)} %add_convert_fusion), channel_id=1, source_target_pairs={{0,64},{32,96},{64,0},{96,32},{1,65},{33,97},{65,1},{97,33},{2,66}... | collective-permute-start | bytes 319496 | tf_op jit(solution)/shard_map/ppermute | solution.py:397
  141.4 4.2 %collective-permute-start.29 = (bf16[1,416,128]{2,1,0:T(8,128)(2,1)S(1)}, bf16[1,416,128]{2,1,0:T(8,128)(2,1)S(1)}, u32[]{:S(2)}, u32[]{:S(2)}) collective-permute-start(bf16[1,416,128]{2,1,0:T(8,128)(2,1)S(1)} %add_convert_fusion), channel_id=1, source_target_pairs={{0,96},{32,0},{64,32},{96,64},{1,97},{33,1},{65,33},{97,65},{2,98}... | collective-permute-start | bytes 319496 | tf_op jit(solution)/shard_map/ppermute | solution.py:397
  145.7 3.9 %copy-start.2 = (bf16[4,416,128]{2,1,0:T(8,128)(2,1)}, bf16[4,416,128]{2,1,0:T(8,128)(2,1)S(1)}, u32[]{:S(2)}) copy-start(bf16[4,416,128]{2,1,0:T(8,128)(2,1)S(1)} %maximum_bitcast_fusion.own_ref) | copy-start | bytes 1277956
  145.8 3.9 %collective-permute-start.30 = (bf16[4,416,128]{2,1,0:T(8,128)(2,1)S(1)}, bf16[4,416,128]{2,1,0:T(8,128)(2,1)S(1)}, u32[]{:S(2)}, u32[]{:S(2)}) collective-permute-start(bf16[4,416,128]{2,1,0:T(8,128)(2,1)S(1)} %maximum_bitcast_fusion.own_ref), channel_id=1, source_target_pairs={{0,16},{16,0},{1,17},{17,1},{2,18},{18,2},{3,19},{19,3},{4,20},{20... | collective-permute-start | bytes 1277960 | tf_op jit(solution)/shard_map/ppermute | solution.py:401
  149.7 0.8 copy-start.3
Sparse Core Ops, SparseCore 0:
  25.6 7.6 sort.11.cloned.1.call-done
  (1 shorter events, 0.0 us)
Sparse Core Ops, SparseCore 1:
  27.7 30.5 all-gather.2

commit v6 on v5

--- a/solution.py
+++ b/solution.py
@@ -352,7 +352,7 @@
             ],
         ),
         out_shape=[jax.ShapeDtypeStruct((D, LOCAL), F32), jax.ShapeDtypeStruct((1, LOCAL), F32)],
-        compiler_params=pltpu.CompilerParams(vmem_limit_bytes=58 * MIB),
+        compiler_params=pltpu.CompilerParams(vmem_limit_bytes=20 * MIB),
         cost_estimate=pl.CostEstimate(flops=2_000_000_000, bytes_accessed=5_000_000, transcendentals=0),
         name="right_update",
     )(partner, ext_all, back)

time: 162 us -> 161 us (level)
  Pallas kernels: 39 us -> 37.1 us
    pallas_call x1, Pallas kernels: 4.18 us -> 2.35 us  [right_update(): pl.pallas_call(right_kernel, grid_spec=pltpu.PrefetchScalarGridSpec(num_s...]
  transfers between devices with their start and end apart: 33 -> 33, of which waited for: 17 -> 17; matrix products, arithmetic and copies ran while one was open for 4% -> 4% of each run, Pallas kernels for 22% -> 21%
where the time goes in v6:
time: 161 us; the launch traced here: 160 us
  starting transfers between devices  63.4 us (39%)
  Pallas kernels  37.1 us (23%)
  waiting for transfers between devices  29.5 us (18%)
  between operations  17.7 us (11%)
  other arithmetic  6.9 us (4%)
  local copies, waits for them, and re-layouts  5.23 us (3%)
    ppermute x27, starting transfers between devices, shift(): return lax.ppermute(value, axis, [(i, i + distance & 3) for i in range(4)])  43.5 us
    ppermute x27, waiting for transfers between devices, shift(): return lax.ppermute(value, axis, [(i, i + distance & 3) for i in range(4)])  25.8 us
    pallas_call x1, Pallas kernels, edges(): pl.pallas_call(edge_kernel, in_specs=[pl.BlockSpec(memory_space=pltpu.SME...  18.9 us
    ppermute x4, starting transfers between devices, other_core(): return lax.ppermute(value, 'core', CORES)  11.4 us
    pallas_call x1, Pallas kernels, make_query(): pl.pallas_call(query_kernel, grid=(STEPS,), in_specs=[pl.BlockSpec((2, CH...  8.58 us
    all_to_all x1, starting transfers between devices, body(): returned = lax.all_to_all(back, ROW, 0, 0, tiled=True)  8.46 us
    unnamed x29, local copies, waits for them, and re-layouts  4.49 us
    pallas_call x1, Pallas kernels, relation_update(): pl.pallas_call(relation_kernel, out_shape=[jax.ShapeDtypeStruct((D, REL),...  3.39 us
  transfers between devices with their start and end apart: 33, of which 17 were waited for; matrix products, arithmetic and copies ran while one was open for 4% of the time, Pallas kernels for 21%

profile of v6, /device:TPU:1, one launch (start us, length us, event | category | flops | bytes accessed | tf_op | source)
XLA Modules:
  0.0 159.9 jit_solution(5768065928395927339)
XLA Ops:
  8.1 1.1 bitcast_convert_fusion
  9.1 2.1 %collective-permute-start = (bf16[400,256]{1,0:T(8,128)(2,1)S(1)}, bf16[400,256]{1,0:T(8,128)(2,1)S(1)}, u32[]{:S(2)}, u32[]{:S(2)}) collective-permute-start(bf16[400,256]{1,0:T(8,128)(2,1)S(1)} %bitcast_convert_fusion), channel_id=1, source_target_pairs={{0,32},{32,64},{64,96},{96,0},{1,33},{33,65},{65,97},{97,1},{2,34}... | collective-permute-start | bytes 614408 | tf_op jit(solution)/shard_map/ppermute | solution.py:397
  11.2 2.5 %collective-permute-start.1 = (bf16[400,256]{1,0:T(8,128)(2,1)S(1)}, bf16[400,256]{1,0:T(8,128)(2,1)S(1)}, u32[]{:S(2)}, u32[]{:S(2)}) collective-permute-start(bf16[400,256]{1,0:T(8,128)(2,1)S(1)} %bitcast_convert_fusion), channel_id=1, source_target_pairs={{0,64},{32,96},{64,0},{96,32},{1,65},{33,97},{65,1},{97,33},{2,66}... | collective-permute-start | bytes 614408 | tf_op jit(solution)/shard_map/ppermute | solution.py:397
  13.7 1.2 collective-permute-start.2
  14.8 1.5 collective-permute-start.3
  17.7 0.7 shift-left_or_fusion
  18.4 0.8 fusion
  19.2 0.5 and_or_fusion.place_ref
  19.7 0.7 broadcast_in_dim.18
  20.4 1.8 %pad_maximum_fusion = f32[408,256]{1,0:T(8,128)} fusion(f32[8,256]{1,0:T(8,128)S(1)} %broadcast_in_dim.18, f32[400,256]{1,0:T(8,128)} %bitcast.53), kind=kLoop, calls=%fused_computation.1 | loop fusion | flops 104448 | bytes 835584 | tf_op jit(solution)/shard_map/concatenate | solution.py:456
  22.9 1.3 collective-permute-start.4
  24.3 0.6 pad_add_fusion
  24.9 0.5 collective-permute-done.4
  25.5 0.5 all-gather.3.cloned.1.call-update
  26.1 3.8 %collective-permute-start.10 = (bf16[400,128]{1,0:T(8,128)(2,1)S(1)}, bf16[400,128]{1,0:T(8,128)(2,1)S(1)}, u32[]{:S(2)}, u32[]{:S(2)}) collective-permute-start(bf16[400,128]{1,0:T(8,128)(2,1)S(1)} %get-tuple-element.48), channel_id=1, source_target_pairs={{0,12},{4,0},{8,4},{12,8},{1,13},{5,1},{9,5},{13,9},{2,14},{6,2},{... | collective-permute-start | bytes 307208 | tf_op jit(solution)/shard_map/ppermute | solution.py:397
  29.9 2.9 %collective-permute-start.5 = (bf16[400,128]{1,0:T(8,128)(2,1)S(1)}, bf16[400,128]{1,0:T(8,128)(2,1)S(1)}, u32[]{:S(2)}, u32[]{:S(2)}) collective-permute-start(bf16[400,128]{1,0:T(8,128)(2,1)S(1)} %get-tuple-element.44), channel_id=1, source_target_pairs={{0,2},{1,3},{2,0},{3,1},{4,6},{5,7},{6,4},{7,5},{8,10},{9,11},{10,... | collective-permute-start | bytes 307208 | tf_op jit(solution)/shard_map/ppermute | solution.py:397
  32.8 0.4 collective-permute-start.6
  33.2 2.3 %collective-permute-start.7 = (bf16[400,128]{1,0:T(8,128)(2,1)S(1)}, bf16[400,128]{1,0:T(8,128)(2,1)S(1)}, u32[]{:S(2)}, u32[]{:S(2)}) collective-permute-start(bf16[400,128]{1,0:T(8,128)(2,1)S(1)} %get-tuple-element.44), channel_id=1, source_target_pairs={{0,3},{1,0},{2,1},{3,2},{4,7},{5,4},{6,5},{7,6},{8,11},{9,8},{10,9... | collective-permute-start | bytes 307208 | tf_op jit(solution)/shard_map/ppermute | solution.py:397
  35.5 0.7 collective-permute-start.9
  36.2 1.3 collective-permute-done.6
  37.5 0.3 collective-permute-done.7
  37.8 2.8 %collective-permute-done.8 = bf16[400,128]{1,0:T(8,128)(2,1)S(1)} collective-permute-done((bf16[400,128]{1,0:T(8,128)(2,1)S(1)}, bf16[400,128]{1,0:T(8,128)(2,1)S(1)}, u32[]{:S(2)}, u32[]{:S(2)}) %collective-permute-start.8) | collective-permute-done | bytes 102432 | tf_op jit(solution)/shard_map/ppermute | solution.py:397
  40.6 1.2 collective-permute-done.9
  42.0 2.6 %collective-permute-start.15 = (bf16[4,400,128]{2,1,0:T(8,128)(2,1)S(1)}, bf16[4,400,128]{2,1,0:T(8,128)(2,1)S(1)}, u32[]{:S(2)}, u32[]{:S(2)}) collective-permute-start(bf16[4,400,128]{2,1,0:T(8,128)(2,1)S(1)} %pad_maximum_fusion.2.b0), channel_id=1, source_target_pairs={{0,2},{1,3},{2,0},{3,1},{4,6},{5,7},{6,4},{7,5},{8,10},{9,11},{10,... | collective-permute-start | bytes 1228808 | tf_op jit(solution)/shard_map/ppermute | solution.py:397
  44.5 0.8 collective-permute-start.16
  45.5 1.1 collective-permute-start.12
  46.6 5.3 %collective-permute-done.14.b1 = bf16[4,400,128]{2,1,0:T(8,128)(2,1)S(1)} collective-permute-done((bf16[4,400,128]{2,1,0:T(8,128)(2,1)S(1)}, bf16[4,400,128]{2,1,0:T(8,128)(2,1)S(1)}, u32[]{:S(2)}, u32[]{:S(2)}) %collective-permute-start.14) | collective-permute-done | bytes 409632 | tf_op jit(solution)/shard_map/ppermute | solution.py:397
  51.9 1.8 %collective-permute-start.13 = (bf16[4,400,128]{2,1,0:T(8,128)(2,1)S(1)}, bf16[4,400,128]{2,1,0:T(8,128)(2,1)S(1)}, u32[]{:S(2)}, u32[]{:S(2)}) collective-permute-start(bf16[4,400,128]{2,1,0:T(8,128)(2,1)S(1)} %pad_maximum_fusion.1.a0), channel_id=1, source_target_pairs={{0,12},{4,0},{8,4},{12,8},{1,13},{5,1},{9,5},{13,9},{2,14},{6,2},{... | collective-permute-start | bytes 1228808 | tf_op jit(solution)/shard_map/ppermute | solution.py:397
  53.7 8.6 %make_query.1 = (bf16[416,2048]{1,0:T(8,128)(2,1)}, bf16[416,2048]{1,0:T(8,128)(2,1)}, bf16[400,2048]{1,0:T(8,128)(2,1)}) custom-call(s32[2,2048]{1,0:T(2,128)} %sort.9.cloned.1.call-done.keys_ref, f32[400,256]{1,0:T(8,128)} %bitcast.59, f32[400,1000]{1,0:T(8,128)} %bitcast.54), custom_call_target="tpu_custom_call" | custom-call | flops 5000000000 | bytes 10000000 | tf_op jit(solution)/shard_map/make_query/pallas_call | solution.py:85
  62.3 0.6 collective-permute-done.16.b3
  62.9 0.2 collective-permute-done.13.a3
  63.1 0.6 copy-done.10
  64.1 18.9 %edges.1 = (bf16[16,624,128]{2,1,0:T(8,128)(2,1)}, bf16[4,416,128]{2,1,0:T(8,128)(2,1)}, bf16[4,416,128]{2,1,0:T(8,128)(2,1)}, f32[400,256]{1,0:T(8,128)}) custom-call(s32[16]{0:T(128)} %and_or_fusion.place_ref, s32[2,2048]{1,0:T(2,128)} %sort.9.cloned.1.call-done.keys_ref, bf16[4,400,128]{2,1,0:T(8,128)(2,1)} %copy-done.6, bf16[4,400,128]{2,1,0:T(8,128)(2,1)} %copy-done.11, ...), custom_call_target="tpu_custom_call" | custom-call | flops 8000000000 | bytes 20000000 | tf_op jit(solution)/shard_map/edges/pallas_call | solution.py:254
  83.0 8.5 %all-to-all-start = ((bf16[16,624,128]{2,1,0:T(8,128)(2,1)}), bf16[16,624,128]{2,1,0:T(8,128)(2,1)S(1)}, u32[]{:S(2)}, u32[]{:S(2)}) async-start(bf16[16,624,128]{2,1,0:T(8,128)(2,1)} %get-tuple-element.64), calls=%async_computation | async-start | bytes 5111808 | tf_op jit(solution)/shard_map/all_to_all | solution.py:464
  91.4 6.1 %collective-permute-start.17 = (bf16[4,416,128]{2,1,0:T(8,128)(2,1)S(1)}, bf16[4,416,128]{2,1,0:T(8,128)(2,1)S(1)}, u32[]{:S(2)}, u32[]{:S(2)}) collective-permute-start(bf16[4,416,128]{2,1,0:T(8,128)(2,1)S(1)} %copy-done.7), channel_id=1, source_target_pairs={{0,16},{16,0},{1,17},{17,1},{2,18},{18,2},{3,19},{19,3},{4,20},{20... | collective-permute-start | bytes 1277960 | tf_op jit(solution)/shard_map/ppermute | solution.py:401
  97.5 1.4 collective-permute-done.17.refs_1_
  98.9 0.8 copy-done.4
  99.7 1.9 %spread.1 = (bf16[1,416,128]{2,1,0:T(8,128)(2,1)}, bf16[1,416,128]{2,1,0:T(8,128)(2,1)}, bf16[1,416,128]{2,1,0:T(8,128)(2,1)}, bf16[1,416,128]{2,1,0:T(8,128)(2,1)}) custom-call(bf16[4,416,128]{2,1,0:T(8,128)(2,1)} %get-tuple-element.55.refs_0_, bf16[4,416,128]{2,1,0:T(8,128)(2,1)} %copy-done.4), custom_call_target="tpu_custom_call" | custom-call | tf_op jit(solution)/shard_map/spread/pallas_call | solution.py:302
  101.6 2.4 %collective-permute-start.18 = (bf16[1,416,128]{2,1,0:T(8,128)(2,1)}, bf16[1,416,128]{2,1,0:T(8,128)(2,1)S(1)}, u32[]{:S(2)}, u32[]{:S(2)}) collective-permute-start(bf16[1,416,128]{2,1,0:T(8,128)(2,1)} %get-tuple-element.58), channel_id=1, source_target_pairs={{0,64},{32,96},{64,0},{96,32},{1,65},{33,97},{65,1},{97,33},{2,66}... | collective-permute-start | bytes 319496 | tf_op jit(solution)/shard_map/ppermute | solution.py:397
  104.1 2.5 %collective-permute-start.20 = (bf16[1,416,128]{2,1,0:T(8,128)(2,1)}, bf16[1,416,128]{2,1,0:T(8,128)(2,1)S(1)}, u32[]{:S(2)}, u32[]{:S(2)}) collective-permute-start(bf16[1,416,128]{2,1,0:T(8,128)(2,1)} %get-tuple-element.60), channel_id=1, source_target_pairs={{0,96},{32,0},{64,32},{96,64},{1,97},{33,1},{65,33},{97,65},{2,98}... | collective-permute-start | bytes 319496 | tf_op jit(solution)/shard_map/ppermute | solution.py:397
  106.6 0.8 collective-permute-done.18
  107.5 2.6 %collective-permute-done.19 = bf16[1,416,128]{2,1,0:T(8,128)(2,1)S(1)} collective-permute-done((bf16[1,416,128]{2,1,0:T(8,128)(2,1)}, bf16[1,416,128]{2,1,0:T(8,128)(2,1)S(1)}, u32[]{:S(2)}, u32[]{:S(2)}) %collective-permute-start.19) | collective-permute-done | bytes 106528 | tf_op jit(solution)/shard_map/ppermute | solution.py:397
  110.1 1.0 add_convert_fusion.2
  111.1 3.2 %collective-permute-start.21 = (bf16[1,416,128]{2,1,0:T(8,128)(2,1)S(1)}, bf16[1,416,128]{2,1,0:T(8,128)(2,1)S(1)}, u32[]{:S(2)}, u32[]{:S(2)}) collective-permute-start(bf16[1,416,128]{2,1,0:T(8,128)(2,1)S(1)} %add_convert_fusion.2), channel_id=1, source_target_pairs={{0,8},{4,12},{8,0},{12,4},{1,9},{5,13},{9,1},{13,5},{2,10},{6,14},... | collective-permute-start | bytes 319496 | tf_op jit(solution)/shard_map/ppermute | solution.py:397
  114.2 0.3 collective-permute-start.22
  114.5 2.4 %collective-permute-start.23 = (bf16[1,416,128]{2,1,0:T(8,128)(2,1)S(1)}, bf16[1,416,128]{2,1,0:T(8,128)(2,1)S(1)}, u32[]{:S(2)}, u32[]{:S(2)}) collective-permute-start(bf16[1,416,128]{2,1,0:T(8,128)(2,1)S(1)} %add_convert_fusion.2), channel_id=1, source_target_pairs={{0,12},{4,0},{8,4},{12,8},{1,13},{5,1},{9,5},{13,9},{2,14},{6,2},{... | collective-permute-start | bytes 319496 | tf_op jit(solution)/shard_map/ppermute | solution.py:397
  116.9 2.0 %left_update.1 = (f32[400,256]{1,0:T(8,128)}, f32[1,256]{1,0:T(1,128)}) custom-call(f32[400,256]{1,0:T(8,128)} %bitcast.60, f32[1,256]{1,0:T(1,128)} %accum_ref.1, f32[400,256]{1,0:T(8,128)} %get-tuple-element.61.grad_ref), custom_call_target="tpu_custom_call" | custom-call | tf_op jit(solution)/shard_map/left_update/pallas_call | solution.py:366
  118.9 4.0 %collective-permute-done.21 = bf16[1,416,128]{2,1,0:T(8,128)(2,1)S(1)} collective-permute-done((bf16[1,416,128]{2,1,0:T(8,128)(2,1)S(1)}, bf16[1,416,128]{2,1,0:T(8,128)(2,1)S(1)}, u32[]{:S(2)}, u32[]{:S(2)}) %collective-permute-start.21) | collective-permute-done | bytes 106528 | tf_op jit(solution)/shard_map/ppermute | solution.py:397
  122.9 3.3 %collective-permute-done.22 = bf16[1,416,128]{2,1,0:T(8,128)(2,1)S(1)} collective-permute-done((bf16[1,416,128]{2,1,0:T(8,128)(2,1)S(1)}, bf16[1,416,128]{2,1,0:T(8,128)(2,1)S(1)}, u32[]{:S(2)}, u32[]{:S(2)}) %collective-permute-start.22) | collective-permute-done | bytes 106528 | tf_op jit(solution)/shard_map/ppermute | solution.py:397
  126.3 2.9 %collective-permute-start.24 = (bf16[1,416,128]{2,1,0:T(8,128)(2,1)S(1)}, bf16[1,416,128]{2,1,0:T(8,128)(2,1)S(1)}, u32[]{:S(2)}, u32[]{:S(2)}) collective-permute-start(bf16[1,416,128]{2,1,0:T(8,128)(2,1)S(1)} %add_convert_fusion.1), channel_id=1, source_target_pairs={{0,1},{1,2},{2,3},{3,0},{4,5},{5,6},{6,7},{7,4},{8,9},{9,10},{10,1... | collective-permute-start | bytes 319496 | tf_op jit(solution)/shard_map/ppermute | solution.py:397
  129.1 1.9 %collective-permute-start.25 = (bf16[1,416,128]{2,1,0:T(8,128)(2,1)S(1)}, bf16[1,416,128]{2,1,0:T(8,128)(2,1)S(1)}, u32[]{:S(2)}, u32[]{:S(2)}) collective-permute-start(bf16[1,416,128]{2,1,0:T(8,128)(2,1)S(1)} %add_convert_fusion.1), channel_id=1, source_target_pairs={{0,2},{1,3},{2,0},{3,1},{4,6},{5,7},{6,4},{7,5},{8,10},{9,11},{10,... | collective-permute-start | bytes 319496 | tf_op jit(solution)/shard_map/ppermute | solution.py:397
  131.1 1.4 collective-permute-start.26
  132.4 1.9 %copy-done = f32[3264,256]{1,0:T(8,128)S(1)} copy-done((f32[3264,256]{1,0:T(8,128)S(1)}, f32[3264,256]{1,0:T(8,128)}, u32[]{:S(2)}) %copy-start) | copy-done | bytes 3342360
  134.4 2.4 %right_update.1 = (f32[400,256]{1,0:T(8,128)}, f32[1,256]{1,0:T(1,128)}) custom-call(s32[1]{0:T(128)S(6)} %copy.21.partner_ref, f32[8,408,256]{2,1,0:T(8,128)S(1)} %bitcast.52, bf16[16,624,128]{2,1,0:T(8,128)(2,1)S(1)} %all-to-all-done.back_ref), custom_call_target="tpu_custom_call" | custom-call | flops 2000000000 | bytes 5000000 | tf_op jit(solution)/shard_map/right_update/pallas_call | solution.py:336
  136.8 1.1 collective-permute-start.27
  137.9 2.1 %collective-permute-start.28 = (bf16[1,416,128]{2,1,0:T(8,128)(2,1)S(1)}, bf16[1,416,128]{2,1,0:T(8,128)(2,1)S(1)}, u32[]{:S(2)}, u32[]{:S(2)}) collective-permute-start(bf16[1,416,128]{2,1,0:T(8,128)(2,1)S(1)} %add_convert_fusion), channel_id=1, source_target_pairs={{0,64},{32,96},{64,0},{96,32},{1,65},{33,97},{65,1},{97,33},{2,66}... | collective-permute-start | bytes 319496 | tf_op jit(solution)/shard_map/ppermute | solution.py:397
  140.0 1.1 collective-permute-start.29
  141.1 0.5 collective-permute-done.27
  141.6 1.9 %collective-permute-done.28 = bf16[1,416,128]{2,1,0:T(8,128)(2,1)S(1)} collective-permute-done((bf16[1,416,128]{2,1,0:T(8,128)(2,1)S(1)}, bf16[1,416,128]{2,1,0:T(8,128)(2,1)S(1)}, u32[]{:S(2)}, u32[]{:S(2)}) %collective-permute-start.28) | collective-permute-done | bytes 106528 | tf_op jit(solution)/shard_map/ppermute | solution.py:397
  143.6 0.7 collective-permute-done.29
  144.3 2.5 %collective-permute-start.30 = (bf16[4,416,128]{2,1,0:T(8,128)(2,1)S(1)}, bf16[4,416,128]{2,1,0:T(8,128)(2,1)S(1)}, u32[]{:S(2)}, u32[]{:S(2)}) collective-permute-start(bf16[4,416,128]{2,1,0:T(8,128)(2,1)S(1)} %maximum_bitcast_fusion.own_ref), channel_id=1, source_target_pairs={{0,16},{16,0},{1,17},{17,1},{2,18},{18,2},{3,19},{19,3},{4,20},{20... | collective-permute-start | bytes 1277960 | tf_op jit(solution)/shard_map/ppermute | solution.py:401
  146.9 1.4 collective-permute-done.30.other_ref
  148.3 0.8 copy-done.3
  149.1 3.4 %relation_update.1 = (f32[400,1000]{1,0:T(8,128)}, f32[1,1000]{1,0:T(1,128)}) custom-call(f32[400,1000]{1,0:T(8,128)} %bitcast.55, f32[1,1000]{1,0:T(1,128)} %bitcast.72, bf16[4,416,128]{2,1,0:T(8,128)(2,1)} %copy-done.2, bf16[4,416,128]{2,1,0:T(8,128)(2,1)} %copy-done.3), custom_call_target="tpu_custom_call" | custom-call | tf_op jit(solution)/shard_map/relation_update/pallas_call | solution.py:384
  (57 shorter events, 1.4 us)
Async XLA Ops:
  8.0 14.9 %copy-start.1 = (f32[1,256,400]{1,2,0:T(8,128)S(1)}, f32[1,256,400]{1,2,0:T(8,128)}, u32[]{:S(2)}) copy-start(f32[1,256,400]{1,2,0:T(8,128)} %param.14) | copy-start | bytes 1228804
  8.0 45.6 %sort.9.cloned.1.call-start = ((), (), s32[]{:S(2)}) async-start(), calls=%async_computation.2 | async-start | bytes 49184 | tf_op jit(solution)/shard_map/sort | solution.py:460
  9.1 13.7 %collective-permute-start = (bf16[400,256]{1,0:T(8,128)(2,1)S(1)}, bf16[400,256]{1,0:T(8,128)(2,1)S(1)}, u32[]{:S(2)}, u32[]{:S(2)}) collective-permute-start(bf16[400,256]{1,0:T(8,128)(2,1)S(1)} %bitcast_convert_fusion), channel_id=1, source_target_pairs={{0,32},{32,64},{64,96},{96,0},{1,33},{33,65},{65,97},{97,1},{2,34}... | collective-permute-start | bytes 614408 | tf_op jit(solution)/shard_map/ppermute | solution.py:397
  11.2 11.6 %collective-permute-start.1 = (bf16[400,256]{1,0:T(8,128)(2,1)S(1)}, bf16[400,256]{1,0:T(8,128)(2,1)S(1)}, u32[]{:S(2)}, u32[]{:S(2)}) collective-permute-start(bf16[400,256]{1,0:T(8,128)(2,1)S(1)} %bitcast_convert_fusion), channel_id=1, source_target_pairs={{0,64},{32,96},{64,0},{96,32},{1,65},{33,97},{65,1},{97,33},{2,66}... | collective-permute-start | bytes 614408 | tf_op jit(solution)/shard_map/ppermute | solution.py:397
  13.7 9.2 %collective-permute-start.2 = (bf16[400,256]{1,0:T(8,128)(2,1)S(1)}, bf16[400,256]{1,0:T(8,128)(2,1)S(1)}, u32[]{:S(2)}, u32[]{:S(2)}) collective-permute-start(bf16[400,256]{1,0:T(8,128)(2,1)S(1)} %bitcast_convert_fusion), channel_id=1, source_target_pairs={{0,96},{32,0},{64,32},{96,64},{1,97},{33,1},{65,33},{97,65},{2,98}... | collective-permute-start | bytes 614408 | tf_op jit(solution)/shard_map/ppermute | solution.py:397
  14.8 7.4 %collective-permute-start.3 = (s32[1]{0:T(128)}, s32[1]{0:T(128)}, u32[]{:S(2)}, u32[]{:S(2)}) collective-permute-start(s32[1]{0:T(128)} %param.18), channel_id=1, source_target_pairs={{0,16},{16,0},{1,17},{17,1},{2,18},{18,2},{3,19},{19,3},{4,20},{20... | collective-permute-start | bytes 20 | tf_op jit(solution)/shard_map/ppermute | solution.py:401
  22.9 2.4 %collective-permute-start.4 = (bf16[400,256]{1,0:T(8,128)(2,1)S(1)}, bf16[400,256]{1,0:T(8,128)(2,1)S(1)}, u32[]{:S(2)}, u32[]{:S(2)}) collective-permute-start(bf16[400,256]{1,0:T(8,128)(2,1)S(1)} %select_select_fusion), channel_id=1, source_target_pairs={{0,16},{16,0},{1,17},{17,1},{2,18},{18,2},{3,19},{19,3},{4,20},{20... | collective-permute-start | bytes 614408 | tf_op jit(solution)/shard_map/ppermute | solution.py:401
  25.4 107.0 %all-gather.3.cloned.1.call-start = ((), (), s32[]{:S(2)}) async-start(), calls=%async_computation.1 | async-start | bytes 3760128 | tf_op jit(solution)/shard_map/all_gather | solution.py:458
  26.1 9.4 %collective-permute-start.10 = (bf16[400,128]{1,0:T(8,128)(2,1)S(1)}, bf16[400,128]{1,0:T(8,128)(2,1)S(1)}, u32[]{:S(2)}, u32[]{:S(2)}) collective-permute-start(bf16[400,128]{1,0:T(8,128)(2,1)S(1)} %get-tuple-element.48), channel_id=1, source_target_pairs={{0,12},{4,0},{8,4},{12,8},{1,13},{5,1},{9,5},{13,9},{2,14},{6,2},{... | collective-permute-start | bytes 307208 | tf_op jit(solution)/shard_map/ppermute | solution.py:397
  29.9 6.3 %collective-permute-start.5 = (bf16[400,128]{1,0:T(8,128)(2,1)S(1)}, bf16[400,128]{1,0:T(8,128)(2,1)S(1)}, u32[]{:S(2)}, u32[]{:S(2)}) collective-permute-start(bf16[400,128]{1,0:T(8,128)(2,1)S(1)} %get-tuple-element.44), channel_id=1, source_target_pairs={{0,2},{1,3},{2,0},{3,1},{4,6},{5,7},{6,4},{7,5},{8,10},{9,11},{10,... | collective-permute-start | bytes 307208 | tf_op jit(solution)/shard_map/ppermute | solution.py:397
  32.8 4.7 %collective-permute-start.6 = (bf16[400,128]{1,0:T(8,128)(2,1)S(1)}, bf16[400,128]{1,0:T(8,128)(2,1)S(1)}, u32[]{:S(2)}, u32[]{:S(2)}) collective-permute-start(bf16[400,128]{1,0:T(8,128)(2,1)S(1)} %get-tuple-element.44), channel_id=1, source_target_pairs={{0,1},{1,2},{2,3},{3,0},{4,5},{5,6},{6,7},{7,4},{8,9},{9,10},{10,1... | collective-permute-start | bytes 307208 | tf_op jit(solution)/shard_map/ppermute | solution.py:397
  33.2 4.6 %collective-permute-start.7 = (bf16[400,128]{1,0:T(8,128)(2,1)S(1)}, bf16[400,128]{1,0:T(8,128)(2,1)S(1)}, u32[]{:S(2)}, u32[]{:S(2)}) collective-permute-start(bf16[400,128]{1,0:T(8,128)(2,1)S(1)} %get-tuple-element.44), channel_id=1, source_target_pairs={{0,3},{1,0},{2,1},{3,2},{4,7},{5,4},{6,5},{7,6},{8,11},{9,8},{10,9... | collective-permute-start | bytes 307208 | tf_op jit(solution)/shard_map/ppermute | solution.py:397
  35.5 5.1 %collective-permute-start.8 = (bf16[400,128]{1,0:T(8,128)(2,1)S(1)}, bf16[400,128]{1,0:T(8,128)(2,1)S(1)}, u32[]{:S(2)}, u32[]{:S(2)}) collective-permute-start(bf16[400,128]{1,0:T(8,128)(2,1)S(1)} %get-tuple-element.48), channel_id=1, source_target_pairs={{0,8},{4,12},{8,0},{12,4},{1,9},{5,13},{9,1},{13,5},{2,10},{6,14},... | collective-permute-start | bytes 307208 | tf_op jit(solution)/shard_map/ppermute | solution.py:397
  35.5 6.4 %collective-permute-start.9 = (bf16[400,128]{1,0:T(8,128)(2,1)S(1)}, bf16[400,128]{1,0:T(8,128)(2,1)S(1)}, u32[]{:S(2)}, u32[]{:S(2)}) collective-permute-start(bf16[400,128]{1,0:T(8,128)(2,1)S(1)} %get-tuple-element.48), channel_id=1, source_target_pairs={{0,4},{4,8},{8,12},{12,0},{1,5},{5,9},{9,13},{13,1},{2,6},{6,10},{... | collective-permute-start | bytes 307208 | tf_op jit(solution)/shard_map/ppermute | solution.py:397
  41.9 20.4 %copy-start.5 = (bf16[4,400,128]{2,1,0:T(8,128)(2,1)}, bf16[4,400,128]{2,1,0:T(8,128)(2,1)S(1)}, u32[]{:S(2)}) copy-start(bf16[4,400,128]{2,1,0:T(8,128)(2,1)S(1)} %pad_maximum_fusion.2.b0) | copy-start | bytes 1228804
  41.9 10.0 %collective-permute-start.14 = (bf16[4,400,128]{2,1,0:T(8,128)(2,1)S(1)}, bf16[4,400,128]{2,1,0:T(8,128)(2,1)S(1)}, u32[]{:S(2)}, u32[]{:S(2)}) collective-permute-start(bf16[4,400,128]{2,1,0:T(8,128)(2,1)S(1)} %pad_maximum_fusion.2.b0), channel_id=1, source_target_pairs={{0,1},{1,2},{2,3},{3,0},{4,5},{5,6},{6,7},{7,4},{8,9},{9,10},{10,1... | collective-permute-start | bytes 1228808 | tf_op jit(solution)/shard_map/ppermute | solution.py:397
  42.0 20.3 %collective-permute-start.15 = (bf16[4,400,128]{2,1,0:T(8,128)(2,1)S(1)}, bf16[4,400,128]{2,1,0:T(8,128)(2,1)S(1)}, u32[]{:S(2)}, u32[]{:S(2)}) collective-permute-start(bf16[4,400,128]{2,1,0:T(8,128)(2,1)S(1)} %pad_maximum_fusion.2.b0), channel_id=1, source_target_pairs={{0,2},{1,3},{2,0},{3,1},{4,6},{5,7},{6,4},{7,5},{8,10},{9,11},{10,... | collective-permute-start | bytes 1228808 | tf_op jit(solution)/shard_map/ppermute | solution.py:397
  44.5 18.4 %collective-permute-start.16 = (bf16[4,400,128]{2,1,0:T(8,128)(2,1)S(1)}, bf16[4,400,128]{2,1,0:T(8,128)(2,1)S(1)}, u32[]{:S(2)}, u32[]{:S(2)}) collective-permute-start(bf16[4,400,128]{2,1,0:T(8,128)(2,1)S(1)} %pad_maximum_fusion.2.b0), channel_id=1, source_target_pairs={{0,3},{1,0},{2,1},{3,2},{4,7},{5,4},{6,5},{7,6},{8,11},{9,8},{10,9... | collective-permute-start | bytes 1228808 | tf_op jit(solution)/shard_map/ppermute | solution.py:397
  45.4 16.9 %copy-start.6 = (bf16[4,400,128]{2,1,0:T(8,128)(2,1)}, bf16[4,400,128]{2,1,0:T(8,128)(2,1)S(1)}, u32[]{:S(2)}) copy-start(bf16[4,400,128]{2,1,0:T(8,128)(2,1)S(1)} %pad_maximum_fusion.1.a0) | copy-start | bytes 1228804
  45.4 17.5 %collective-permute-start.11 = (bf16[4,400,128]{2,1,0:T(8,128)(2,1)S(1)}, bf16[4,400,128]{2,1,0:T(8,128)(2,1)S(1)}, u32[]{:S(2)}, u32[]{:S(2)}) collective-permute-start(bf16[4,400,128]{2,1,0:T(8,128)(2,1)S(1)} %pad_maximum_fusion.1.a0), channel_id=1, source_target_pairs={{0,4},{4,8},{8,12},{12,0},{1,5},{5,9},{9,13},{13,1},{2,6},{6,10},{... | collective-permute-start | bytes 1228808 | tf_op jit(solution)/shard_map/ppermute | solution.py:397
  45.5 17.5 %collective-permute-start.12 = (bf16[4,400,128]{2,1,0:T(8,128)(2,1)S(1)}, bf16[4,400,128]{2,1,0:T(8,128)(2,1)S(1)}, u32[]{:S(2)}, u32[]{:S(2)}) collective-permute-start(bf16[4,400,128]{2,1,0:T(8,128)(2,1)S(1)} %pad_maximum_fusion.1.a0), channel_id=1, source_target_pairs={{0,8},{4,12},{8,0},{12,4},{1,9},{5,13},{9,1},{13,5},{2,10},{6,14},... | collective-permute-start | bytes 1228808 | tf_op jit(solution)/shard_map/ppermute | solution.py:397
  51.9 10.4 %copy-start.8 = (bf16[4,400,128]{2,1,0:T(8,128)(2,1)}, bf16[4,400,128]{2,1,0:T(8,128)(2,1)S(1)}, u32[]{:S(2)}) copy-start(bf16[4,400,128]{2,1,0:T(8,128)(2,1)S(1)} %collective-permute-done.14.b1) | copy-start | bytes 1228804
  51.9 11.2 %collective-permute-start.13 = (bf16[4,400,128]{2,1,0:T(8,128)(2,1)S(1)}, bf16[4,400,128]{2,1,0:T(8,128)(2,1)S(1)}, u32[]{:S(2)}, u32[]{:S(2)}) collective-permute-start(bf16[4,400,128]{2,1,0:T(8,128)(2,1)S(1)} %pad_maximum_fusion.1.a0), channel_id=1, source_target_pairs={{0,12},{4,0},{8,4},{12,8},{1,13},{5,1},{9,5},{13,9},{2,14},{6,2},{... | collective-permute-start | bytes 1228808 | tf_op jit(solution)/shard_map/ppermute | solution.py:397
  62.3 0.8 copy-start.9
  62.9 0.8 copy-start.10
  62.9 0.9 copy-start.11
  62.9 1.0 copy-start.12
  63.1 1.0 copy-start.13
  83.0 8.5 %copy-start.7 = (bf16[4,416,128]{2,1,0:T(8,128)(2,1)S(1)}, bf16[4,416,128]{2,1,0:T(8,128)(2,1)}, u32[]{:S(2)}) copy-start(bf16[4,416,128]{2,1,0:T(8,128)(2,1)} %get-tuple-element.56) | copy-start | bytes 1277956
  83.0 49.5 %all-to-all-start = ((bf16[16,624,128]{2,1,0:T(8,128)(2,1)}), bf16[16,624,128]{2,1,0:T(8,128)(2,1)S(1)}, u32[]{:S(2)}, u32[]{:S(2)}) async-start(bf16[16,624,128]{2,1,0:T(8,128)(2,1)} %get-tuple-element.64), calls=%async_computation | async-start | bytes 5111808 | tf_op jit(solution)/shard_map/all_to_all | solution.py:464
  91.4 7.5 %collective-permute-start.17 = (bf16[4,416,128]{2,1,0:T(8,128)(2,1)S(1)}, bf16[4,416,128]{2,1,0:T(8,128)(2,1)S(1)}, u32[]{:S(2)}, u32[]{:S(2)}) collective-permute-start(bf16[4,416,128]{2,1,0:T(8,128)(2,1)S(1)} %copy-done.7), channel_id=1, source_target_pairs={{0,16},{16,0},{1,17},{17,1},{2,18},{18,2},{3,19},{19,3},{4,20},{20... | collective-permute-start | bytes 1277960 | tf_op jit(solution)/shard_map/ppermute | solution.py:401
  98.9 0.8 copy-start.4
  101.6 5.9 %collective-permute-start.18 = (bf16[1,416,128]{2,1,0:T(8,128)(2,1)}, bf16[1,416,128]{2,1,0:T(8,128)(2,1)S(1)}, u32[]{:S(2)}, u32[]{:S(2)}) collective-permute-start(bf16[1,416,128]{2,1,0:T(8,128)(2,1)} %get-tuple-element.58), channel_id=1, source_target_pairs={{0,64},{32,96},{64,0},{96,32},{1,65},{33,97},{65,1},{97,33},{2,66}... | collective-permute-start | bytes 319496 | tf_op jit(solution)/shard_map/ppermute | solution.py:397
  104.0 6.1 %collective-permute-start.19 = (bf16[1,416,128]{2,1,0:T(8,128)(2,1)}, bf16[1,416,128]{2,1,0:T(8,128)(2,1)S(1)}, u32[]{:S(2)}, u32[]{:S(2)}) collective-permute-start(bf16[1,416,128]{2,1,0:T(8,128)(2,1)} %get-tuple-element.59), channel_id=1, source_target_pairs={{0,32},{32,64},{64,96},{96,0},{1,33},{33,65},{65,97},{97,1},{2,34}... | collective-permute-start | bytes 319496 | tf_op jit(solution)/shard_map/ppermute | solution.py:397
  104.1 6.0 %collective-permute-start.20 = (bf16[1,416,128]{2,1,0:T(8,128)(2,1)}, bf16[1,416,128]{2,1,0:T(8,128)(2,1)S(1)}, u32[]{:S(2)}, u32[]{:S(2)}) collective-permute-start(bf16[1,416,128]{2,1,0:T(8,128)(2,1)} %get-tuple-element.60), channel_id=1, source_target_pairs={{0,96},{32,0},{64,32},{96,64},{1,97},{33,1},{65,33},{97,65},{2,98}... | collective-permute-start | bytes 319496 | tf_op jit(solution)/shard_map/ppermute | solution.py:397
  111.1 11.9 %collective-permute-start.21 = (bf16[1,416,128]{2,1,0:T(8,128)(2,1)S(1)}, bf16[1,416,128]{2,1,0:T(8,128)(2,1)S(1)}, u32[]{:S(2)}, u32[]{:S(2)}) collective-permute-start(bf16[1,416,128]{2,1,0:T(8,128)(2,1)S(1)} %add_convert_fusion.2), channel_id=1, source_target_pairs={{0,8},{4,12},{8,0},{12,4},{1,9},{5,13},{9,1},{13,5},{2,10},{6,14},... | collective-permute-start | bytes 319496 | tf_op jit(solution)/shard_map/ppermute | solution.py:397
  114.2 12.0 %collective-permute-start.22 = (bf16[1,416,128]{2,1,0:T(8,128)(2,1)S(1)}, bf16[1,416,128]{2,1,0:T(8,128)(2,1)S(1)}, u32[]{:S(2)}, u32[]{:S(2)}) collective-permute-start(bf16[1,416,128]{2,1,0:T(8,128)(2,1)S(1)} %add_convert_fusion.2), channel_id=1, source_target_pairs={{0,4},{4,8},{8,12},{12,0},{1,5},{5,9},{9,13},{13,1},{2,6},{6,10},{... | collective-permute-start | bytes 319496 | tf_op jit(solution)/shard_map/ppermute | solution.py:397
  114.5 11.7 %collective-permute-start.23 = (bf16[1,416,128]{2,1,0:T(8,128)(2,1)S(1)}, bf16[1,416,128]{2,1,0:T(8,128)(2,1)S(1)}, u32[]{:S(2)}, u32[]{:S(2)}) collective-permute-start(bf16[1,416,128]{2,1,0:T(8,128)(2,1)S(1)} %add_convert_fusion.2), channel_id=1, source_target_pairs={{0,12},{4,0},{8,4},{12,8},{1,13},{5,1},{9,5},{13,9},{2,14},{6,2},{... | collective-permute-start | bytes 319496 | tf_op jit(solution)/shard_map/ppermute | solution.py:397
  126.3 10.4 %collective-permute-start.24 = (bf16[1,416,128]{2,1,0:T(8,128)(2,1)S(1)}, bf16[1,416,128]{2,1,0:T(8,128)(2,1)S(1)}, u32[]{:S(2)}, u32[]{:S(2)}) collective-permute-start(bf16[1,416,128]{2,1,0:T(8,128)(2,1)S(1)} %add_convert_fusion.1), channel_id=1, source_target_pairs={{0,1},{1,2},{2,3},{3,0},{4,5},{5,6},{6,7},{7,4},{8,9},{9,10},{10,1... | collective-permute-start | bytes 319496 | tf_op jit(solution)/shard_map/ppermute | solution.py:397
  129.1 7.6 %collective-permute-start.25 = (bf16[1,416,128]{2,1,0:T(8,128)(2,1)S(1)}, bf16[1,416,128]{2,1,0:T(8,128)(2,1)S(1)}, u32[]{:S(2)}, u32[]{:S(2)}) collective-permute-start(bf16[1,416,128]{2,1,0:T(8,128)(2,1)S(1)} %add_convert_fusion.1), channel_id=1, source_target_pairs={{0,2},{1,3},{2,0},{3,1},{4,6},{5,7},{6,4},{7,5},{8,10},{9,11},{10,... | collective-permute-start | bytes 319496 | tf_op jit(solution)/shard_map/ppermute | solution.py:397
  131.1 5.7 %collective-permute-start.26 = (bf16[1,416,128]{2,1,0:T(8,128)(2,1)S(1)}, bf16[1,416,128]{2,1,0:T(8,128)(2,1)S(1)}, u32[]{:S(2)}, u32[]{:S(2)}) collective-permute-start(bf16[1,416,128]{2,1,0:T(8,128)(2,1)S(1)} %add_convert_fusion.1), channel_id=1, source_target_pairs={{0,3},{1,0},{2,1},{3,2},{4,7},{5,4},{6,5},{7,6},{8,11},{9,8},{10,9... | collective-permute-start | bytes 319496 | tf_op jit(solution)/shard_map/ppermute | solution.py:397
  132.4 1.9 %copy-start = (f32[3264,256]{1,0:T(8,128)S(1)}, f32[3264,256]{1,0:T(8,128)}, u32[]{:S(2)}) copy-start(f32[3264,256]{1,0:T(8,128)} %all-gather.3.cloned.1.call-done) | copy-start | bytes 10027012
  136.8 4.8 %collective-permute-start.27 = (bf16[1,416,128]{2,1,0:T(8,128)(2,1)S(1)}, bf16[1,416,128]{2,1,0:T(8,128)(2,1)S(1)}, u32[]{:S(2)}, u32[]{:S(2)}) collective-permute-start(bf16[1,416,128]{2,1,0:T(8,128)(2,1)S(1)} %add_convert_fusion), channel_id=1, source_target_pairs={{0,32},{32,64},{64,96},{96,0},{1,33},{33,65},{65,97},{97,1},{2,34}... | collective-permute-start | bytes 319496 | tf_op jit(solution)/shard_map/ppermute | solution.py:397
  137.9 5.7 %collective-permute-start.28 = (bf16[1,416,128]{2,1,0:T(8,128)(2,1)S(1)}, bf16[1,416,128]{2,1,0:T(8,128)(2,1)S(1)}, u32[]{:S(2)}, u32[]{:S(2)}) collective-permute-start(bf16[1,416,128]{2,1,0:T(8,128)(2,1)S(1)} %add_convert_fusion), channel_id=1, source_target_pairs={{0,64},{32,96},{64,0},{96,32},{1,65},{33,97},{65,1},{97,33},{2,66}... | collective-permute-start | bytes 319496 | tf_op jit(solution)/shard_map/ppermute | solution.py:397
  140.0 4.2 %collective-permute-start.29 = (bf16[1,416,128]{2,1,0:T(8,128)(2,1)S(1)}, bf16[1,416,128]{2,1,0:T(8,128)(2,1)S(1)}, u32[]{:S(2)}, u32[]{:S(2)}) collective-permute-start(bf16[1,416,128]{2,1,0:T(8,128)(2,1)S(1)} %add_convert_fusion), channel_id=1, source_target_pairs={{0,96},{32,0},{64,32},{96,64},{1,97},{33,1},{65,33},{97,65},{2,98}... | collective-permute-start | bytes 319496 | tf_op jit(solution)/shard_map/ppermute | solution.py:397
  144.3 3.9 %copy-start.2 = (bf16[4,416,128]{2,1,0:T(8,128)(2,1)}, bf16[4,416,128]{2,1,0:T(8,128)(2,1)S(1)}, u32[]{:S(2)}) copy-start(bf16[4,416,128]{2,1,0:T(8,128)(2,1)S(1)} %maximum_bitcast_fusion.own_ref) | copy-start | bytes 1277956
  144.3 3.9 %collective-permute-start.30 = (bf16[4,416,128]{2,1,0:T(8,128)(2,1)S(1)}, bf16[4,416,128]{2,1,0:T(8,128)(2,1)S(1)}, u32[]{:S(2)}, u32[]{:S(2)}) collective-permute-start(bf16[4,416,128]{2,1,0:T(8,128)(2,1)S(1)} %maximum_bitcast_fusion.own_ref), channel_id=1, source_target_pairs={{0,16},{16,0},{1,17},{17,1},{2,18},{18,2},{3,19},{19,3},{4,20},{20... | collective-permute-start | bytes 1277960 | tf_op jit(solution)/shard_map/ppermute | solution.py:401
  148.3 0.8 copy-start.3
Sparse Core Ops, SparseCore 0:
  25.6 7.6 sort.11.cloned.1.call-done
  (1 shorter events, 0.0 us)
Sparse Core Ops, SparseCore 1:
  27.7 30.5 all-gather.2
